TPU v7x, 32 devices: a whole 2x2x4 slice. The times are simulated.
32 devices in a mesh: group: 4 (over z), branch: 4 (over y, x), head: 2 (over core).
Axes of the slice: x: 2, y: 2, z: 4, core: 2. Of those that a mesh axis runs over, the one named last changes fastest.
Arguments:
- queries: bfloat16 [32, 64, 4096], P(('group', 'branch'), None, 'head'), may hold values from -6 to 6
- branch_keys: bfloat16 [32, 64, 512], P(('group', 'branch'), None, 'head'), may hold values from -6 to 6
- branch_values: bfloat16 [32, 64, 512], P(('group', 'branch'), None, 'head'), may hold values from -6 to 6
- prefix_keys: bfloat16 [64, 512], P('group', 'head'), may hold values from -6 to 6
- prefix_values: bfloat16 [64, 512], P('group', 'head'), may hold values from -6 to 6
- out_grad: bfloat16 [32, 64, 4096], P(('group', 'branch'), None, 'head'), may hold values from -6 to 6
- parents: int32 [32, 64], P(('group', 'branch')), may hold values from -1 to 62, as said below
- lengths: int32 [32], P(('group', 'branch')), may hold values from 16 to 64
Outputs:
- query_grad: bfloat16 [32, 64, 4096], P(('group', 'branch'), None, 'head')
- branch_key_grad: bfloat16 [32, 64, 512], P(('group', 'branch'), None, 'head')
- branch_value_grad: bfloat16 [32, 64, 512], P(('group', 'branch'), None, 'head')
- prefix_key_grad: bfloat16 [64, 512], P('group', 'head')
- prefix_value_grad: bfloat16 [64, 512], P('group', 'head')
Inputs may be any that keep to these rules, and one draw needn't show every extreme that they name: parents[b, t] is -1 or an earlier slot of the same branch, within four slots of t.
All inputs are finite; a program needn't handle non-finite values.
Results may differ from a plain program's by a relative error of at most 0.012.
Values may be sent and summed in bfloat16 or wider, within the bound.
No kernel may reach another device: no remote copies, remote signals or barrier semaphores. Data moves between devices by JAX's collectives and lax.ppermute only.
A program may use at most 64 MiB of HBM per device.

v0:
```python
import jax
import jax.numpy as jnp
from jax import lax
from jax.sharding import PartitionSpec as P

QH = 32
KVH = 4
HD = 128


def ancestors(parents):
    length = parents.shape[-1]
    positions = jnp.arange(length, dtype=jnp.int32)
    onehot = parents[..., None] == positions[None, None, :]
    itself = (positions[:, None] == positions[None, :])[None, :, :]
    reach = (onehot | itself).astype(jnp.bfloat16)
    for rounds in range((length - 1).bit_length()):
        paths = jnp.einsum("btv,bvu->btu", reach, reach, preferred_element_type=jnp.float32)
        reach = (paths > 0.5).astype(jnp.bfloat16)
    return reach > 0.5


def body(
    queries, branch_keys, branch_values, prefix_keys, prefix_values, out_grad, parents, lengths
):
    factor = HD ** (-0.5)
    per_group = QH // KVH
    local_heads = branch_keys.shape[-1] // HD
    count, length = parents.shape
    full_keys, full_values = (
        lax.all_gather(prefix_keys, "group", axis=0, tiled=True),
        lax.all_gather(prefix_values, "group", axis=0, tiled=True),
    )
    reach = ancestors(parents)
    allowed = reach[:, :, None, :]
    positions = jnp.arange(length, dtype=jnp.int32)
    live = (positions[None, :] < lengths[:, None]).astype(jnp.float32)
    live_rows = jnp.broadcast_to(live[:, :, None], (count, length, per_group)).reshape(-1, 1)
    query_parts = []
    key_parts = []
    value_parts = []
    tree_key_parts = []
    tree_value_parts = []
    for head_index in range(local_heads):
        low = head_index * HD
        query_low = head_index * per_group * HD
        heads_query = queries[:, :, query_low : query_low + per_group * HD].reshape(
            count, length, per_group, HD
        )
        heads_grad = out_grad[:, :, query_low : query_low + per_group * HD].reshape(
            count, length, per_group, HD
        )
        query_rows = heads_query.reshape(-1, HD)
        grad_rows = heads_grad.reshape(-1, HD)
        pre_keys = full_keys[:, low : low + HD]
        pre_values = full_values[:, low : low + HD]
        tree_keys = branch_keys[:, :, low : low + HD]
        tree_values = branch_values[:, :, low : low + HD]
        pre_scores = factor * jnp.dot(query_rows, pre_keys.T, preferred_element_type=jnp.float32)
        tree_scores = factor * jnp.einsum(
            "blgh,buh->blgu", heads_query, tree_keys, preferred_element_type=jnp.float32
        )
        tree_scores = jnp.where(allowed, tree_scores, -jnp.inf)
        row_max = jnp.maximum(
            jnp.max(pre_scores, axis=1).reshape(count, length, per_group),
            jnp.max(tree_scores, axis=3),
        )
        totals = jnp.sum(jnp.exp(pre_scores - row_max.reshape(-1, 1)), axis=1).reshape(
            count, length, per_group
        )
        totals = totals + jnp.sum(jnp.exp(tree_scores - row_max[..., None]), axis=3)
        log_total = row_max + jnp.log(totals)
        pre_weights = jnp.exp(pre_scores - log_total.reshape(-1, 1)) * live_rows
        tree_weights = jnp.exp(tree_scores - log_total[..., None]) * live[:, :, None, None]
        pre_rounded = pre_weights.astype(jnp.bfloat16)
        tree_rounded = tree_weights.astype(jnp.bfloat16)
        attended = jnp.dot(pre_rounded, pre_values, preferred_element_type=jnp.float32).reshape(
            count, length, per_group, HD
        )
        attended = attended + jnp.einsum(
            "blgu,buh->blgh", tree_rounded, tree_values, preferred_element_type=jnp.float32
        )
        delta = jnp.sum(heads_grad.astype(jnp.float32) * attended, axis=3)
        pre_dweights = jnp.dot(grad_rows, pre_values.T, preferred_element_type=jnp.float32)
        tree_dweights = jnp.einsum(
            "blgh,buh->blgu", heads_grad, tree_values, preferred_element_type=jnp.float32
        )
        pre_dscores = (pre_weights * (pre_dweights - delta.reshape(-1, 1))).astype(jnp.bfloat16)
        tree_dscores = (tree_weights * (tree_dweights - delta[..., None])).astype(jnp.bfloat16)
        query_grad = jnp.dot(pre_dscores, pre_keys, preferred_element_type=jnp.float32).reshape(
            count, length, per_group, HD
        )
        query_grad = factor * (
            query_grad
            + jnp.einsum(
                "blgu,buh->blgh", tree_dscores, tree_keys, preferred_element_type=jnp.float32
            )
        )
        query_parts.append(query_grad.astype(jnp.bfloat16).reshape(count, length, per_group * HD))
        key_parts.append(
            factor
            * jnp.einsum("rp,rh->ph", pre_dscores, query_rows, preferred_element_type=jnp.float32)
        )
        value_parts.append(
            jnp.einsum("rp,rh->ph", pre_rounded, grad_rows, preferred_element_type=jnp.float32)
        )
        tree_key_sum = factor * jnp.einsum(
            "blgu,blgh->buh", tree_dscores, heads_query, preferred_element_type=jnp.float32
        )
        tree_key_parts.append(tree_key_sum.astype(jnp.bfloat16))
        tree_value_sum = jnp.einsum(
            "blgu,blgh->buh", tree_rounded, heads_grad, preferred_element_type=jnp.float32
        )
        tree_value_parts.append(tree_value_sum.astype(jnp.bfloat16))
    query_grad = jnp.concatenate(query_parts, axis=2)
    branch_key_grad = jnp.concatenate(tree_key_parts, axis=2)
    branch_value_grad = jnp.concatenate(tree_value_parts, axis=2)
    key_terms = jnp.concatenate(key_parts, axis=1)
    value_terms = jnp.concatenate(value_parts, axis=1)
    owned_keys, owned_values = (
        lax.psum_scatter(key_terms, "group", scatter_dimension=0, tiled=True),
        lax.psum_scatter(value_terms, "group", scatter_dimension=0, tiled=True),
    )
    total_keys, total_values = lax.psum((owned_keys, owned_values), "branch")
    prefix_key_grad = total_keys.astype(jnp.bfloat16)
    prefix_value_grad = total_values.astype(jnp.bfloat16)
    return (query_grad, branch_key_grad, branch_value_grad, prefix_key_grad, prefix_value_grad)


def solution(mesh):
    return jax.shard_map(
        body,
        mesh=mesh,
        in_specs=(
            P(("group", "branch"), None, "head"),
            P(("group", "branch"), None, "head"),
            P(("group", "branch"), None, "head"),
            P("group", "head"),
            P("group", "head"),
            P(("group", "branch"), None, "head"),
            P(("group", "branch"), None),
            P(("group", "branch")),
        ),
        out_specs=(
            P(("group", "branch"), None, "head"),
            P(("group", "branch"), None, "head"),
            P(("group", "branch"), None, "head"),
            P("group", "head"),
            P("group", "head"),
        ),
        check_vma=False,
    )
```

profile of v0, /device:TPU:0, one launch (start us, length us, event | category | flops | bytes accessed | tf_op | source)
XLA Modules:
  0.0 104.8 jit_solution(9323915417065812516)
XLA Ops:
  7.2 0.6 copy-done.31
  7.9 1.0 fusion.41
  9.7 0.5 copy-done.26
  10.3 14.8 %all_gather.6 = bf16[64,256]{1,0:T(8,128)(2,1)S(1)} all-gather(bf16[16,256]{1,0:T(8,128)(2,1)S(1)} %copy-done.26), channel_id=1, replica_groups=mesh['group'=4,'branch'=4,'head'=2] {'group'}, dimensions={0}, use_global_device_ids=true | all-gather | bytes 40960 | tf_op jit(solution)/shard_map/all_gather | solution.py:31
  25.9 0.7 reshape.212
  27.3 0.7 copy-done.15
  28.0 0.4 fusion.113
  28.5 0.6 max.38
  29.0 0.4 exponential_reduce_fusion.1
  29.4 0.7 reduce_sum.60
  30.1 1.1 %fusion.111 = (f32[2,64,8]{2,1,0:T(8,128)S(1)}, f32[2,64,8,64]{3,2,1,0:T(8,128)S(1)}) fusion(bf16[2,64,256]{2,1,0:T(8,128)(2,1)} %param.9, pred[2,64,64]{2,1,0:T(8,128)(4,1)} %copy-done.21, bf16[2,64,8,128]{3,2,1,0:T(8,128)(2,1)S(1)} %bitcast.152), kind=kOutput, calls=%fused_computation.148 | convolution fusion | flops 16972800 | bytes 577536 | tf_op jit(solution)/shard_map/blgh,buh->blgu/dot_general | solution.py:60
  31.3 0.9 max.41
  32.2 0.6 max.40
  32.8 0.4 exponential_reduce_fusion
  33.2 0.7 reduce_sum.64
  34.0 0.6 copy-done.24
  34.6 0.7 copy-done.23
  35.4 0.6 copy-done.25
  36.4 0.6 pad_maximum_fusion.4
  37.1 0.7 reshape.208
  37.9 13.4 %all_gather.7 = bf16[64,256]{1,0:T(8,128)(2,1)S(1)} all-gather(bf16[16,256]{1,0:T(8,128)(2,1)} %param.12), channel_id=1, replica_groups=mesh['group'=4,'branch'=4,'head'=2] {'group'}, dimensions={0}, use_global_device_ids=true | all-gather | bytes 40960 | tf_op jit(solution)/shard_map/all_gather | solution.py:32
  51.2 0.3 fusion.92
  51.5 0.3 copy-done.11
  51.8 1.1 %fusion.88 = f32[1024,128]{1,0:T(8,128)} fusion(f32[1024,64]{0,1:T(8,128)S(1)} %get-tuple-element.12, f32[1024]{0:T(1024)S(1)} %log_add_fusion.2, f32[1024]{0:T(1024)S(1)} %mul.80, bf16[64,256]{1,0:T(8,128)(2,1)S(1)} %all_gather.7), kind=kOutput, calls=%fused_computation.129 | convolution fusion | flops 16973824 | bytes 811008 | tf_op jit(solution)/shard_map/dot_general | solution.py:77
  52.9 0.8 copy.48
  53.7 0.8 copy-done.5
  54.6 0.7 copy-done.18
  55.4 0.5 fusion.13
  56.1 0.7 copy-done.12
  57.1 0.6 copy-done.3
  58.0 0.7 copy-done.30
  58.7 0.5 fusion.12
  59.7 0.6 pad_maximum_fusion.3
  60.3 0.7 copy-done.14
  61.1 0.3 fusion.101
  61.3 0.3 fusion.96
  61.6 0.7 copy-done.19
  62.3 0.6 fusion.20
  62.9 0.5 fusion.11
  63.4 0.4 copy-done.1
  64.1 0.6 copy-done.16
  65.0 0.6 fusion.21
  65.7 0.5 fusion.9
  66.2 0.2 fusion.23
  66.8 0.8 pad_maximum_fusion
  67.6 0.7 pad_maximum_fusion.1
  68.3 12.2 %reduce-scatter.3.cloned.1.call-done = f32[16,256]{1,0:T(8,128)} async-done(((f32[64,256]{1,0:T(8,128)}), f32[16,256]{1,0:T(8,128)}) %reduce-scatter.3.cloned.1.call-update) | async-done | bytes 16400 | tf_op jit(solution)/shard_map/reduce_scatter | solution.py:121
  80.5 17.4 %all-reduce = (bf16[16,256]{1,0:T(8,128)(2,1)}, bf16[16,256]{1,0:T(8,128)(2,1)}) all-reduce(f32[16,256]{1,0:T(8,128)} %reduce-scatter.3.cloned.1.call-done, f32[16,256]{1,0:T(8,128)} %reduce-scatter.5.cloned.1.call-done), channel_id=1, replica_groups=mesh['group'=4,'branch'=4,'head'=2] {'branch'}, use_global_device_ids=true, to_apply=%region_11.12 | all-reduce | flops 8192 | bytes 49152 | tf_op jit(solution)/shard_map/psum | solution.py:124
  (102 shorter events, 5.6 us)
Async XLA Ops:
  7.2 0.7 copy-start.31
  7.2 18.1 %copy-start.8 = (bf16[2,64,2048]{2,1,0:T(8,128)(2,1)S(1)}, bf16[2,64,2048]{2,1,0:T(8,128)(2,1)}, u32[]{:S(2)}) copy-start(bf16[2,64,2048]{2,1,0:T(8,128)(2,1)} %param.8) | copy-start | bytes 1572868
  7.2 61.1 %reduce-scatter.5.cloned.1.call-start = ((), (), s32[]{:S(2)}) async-start(), calls=%async_computation.3 | async-start | bytes 81920 | tf_op jit(solution)/shard_map/reduce_scatter | solution.py:122
  7.9 17.2 %copy-start.27 = (f32[2,64]{1,0:T(2,128)}, f32[2,64]{1,0:T(2,128)S(1)}, u32[]{:S(2)}) copy-start(f32[2,64]{1,0:T(2,128)S(1)} %compare_convert_fusion) | copy-start | bytes 1540
  9.6 0.7 copy-start.26
  10.3 17.0 %copy-start.21 = (pred[2,64,64]{2,1,0:T(8,128)(4,1)}, pred[2,64,64]{2,1,0:T(8,128)(4,1)S(1)}, u32[]{:S(2)}) copy-start(pred[2,64,64]{2,1,0:T(8,128)(4,1)S(1)} %fusion.40) | copy-start | bytes 24580
  25.1 1.5 %copy-start.13 = (bf16[64,256]{1,0:T(8,128)(2,1)}, bf16[64,256]{1,0:T(8,128)(2,1)S(1)}, u32[]{:S(2)}) copy-start(bf16[64,256]{1,0:T(8,128)(2,1)S(1)} %all_gather.6) | copy-start | bytes 98308
  25.7 1.6 %copy-start = (bf16[16,8,8,128]{3,2,1,0:T(8,128)(2,1)}, bf16[16,8,8,128]{3,2,1,0:T(8,128)(2,1)S(1)}, u32[]{:S(2)}) copy-start(bf16[16,8,8,128]{3,2,1,0:T(8,128)(2,1)S(1)} %copy.45) | copy-start | bytes 786436
  25.7 1.3 %copy-start.9 = (bf16[2,64,2048]{2,1,0:T(8,128)(2,1)S(1)}, bf16[2,64,2048]{2,1,0:T(8,128)(2,1)}, u32[]{:S(2)}) copy-start(bf16[2,64,2048]{2,1,0:T(8,128)(2,1)} %param.13) | copy-start | bytes 1572868
  27.1 0.8 copy-start.15
  29.4 0.7 copy-start.4
  32.2 0.6 copy-start.2
  33.2 0.8 copy-start.6
  33.2 0.7 copy-start.22
  33.9 0.7 copy-start.24
  34.6 0.7 copy-start.23
  35.3 0.7 copy-start.25
  37.0 43.5 %reduce-scatter.3.cloned.1.call-start = ((), (), s32[]{:S(2)}) async-start(), calls=%async_computation.2 | async-start | bytes 81920 | tf_op jit(solution)/shard_map/reduce_scatter | solution.py:121
  51.2 0.6 copy-start.11
  53.7 0.8 copy-start.5
  53.7 0.9 copy-start.20
  54.5 0.7 copy-start.18
  54.5 0.9 copy-start.29
  54.6 0.9 copy-start.28
  56.0 0.8 copy-start.12
  56.7 1.1 %copy-start.10 = (f32[1024,128]{1,0:T(8,128)S(1)}, f32[1024,128]{1,0:T(8,128)}, u32[]{:S(2)}) copy-start(f32[1024,128]{1,0:T(8,128)} %fusion.88) | copy-start | bytes 1572868
  56.9 0.8 copy-start.3
  56.9 0.9 copy-start.7
  57.0 1.0 copy-start.17
  57.8 0.9 copy-start.30
  60.3 0.8 copy-start.14
  61.3 1.0 copy-start.19
  62.9 1.0 copy-start.1
  63.9 0.8 copy-start.16
Sparse Core Ops, SparseCore 0:
  37.1 20.0 reduce-scatter.4
  60.5 19.9 reduce-scatter.2
where the time goes:
time: 106 us; the launch traced here: 105 us
  blocking collectives  45.6 us (43%)
  local copies, waits for them, and re-layouts  15.6 us (15%)
  between operations  14.6 us (14%)
  waiting for transfers between devices  12.3 us (12%)
  matrix products  10.8 us (10%)
  other arithmetic  5.91 us (6%)
    psum x1, blocking collectives, body(): total_keys, total_values = lax.psum((owned_keys, owned_values), 'branch')  17.4 us
    all_gather x1, blocking collectives, body(): lax.all_gather(prefix_keys, 'group', axis=0, tiled=True)  14.8 us
    all_gather x1, blocking collectives, body(): lax.all_gather(prefix_values, 'group', axis=0, tiled=True)  13.4 us
    reduce_scatter x1, waiting for transfers between devices, body(): lax.psum_scatter(key_terms, 'group', scatter_dimension=0, tiled=True)  12.2 us
    unnamed x68, local copies, waits for them, and re-layouts  11.3 us
  transfers between devices with their start and end apart: 2, of which 1 were waited for; matrix products, arithmetic and copies ran while one was open for 10% of the time, Pallas kernels for 0%

commit v1 on v0

v1 whole, which is shorter than its diff:
```python
import functools

import jax
import jax.numpy as jnp
from jax import lax
from jax.experimental import pallas as pl
from jax.experimental.pallas import tpu as pltpu
from jax.sharding import PartitionSpec as P

QH = 32
KVH = 4
HD = 128
PER = QH // KVH
RADIX = 4
LOG2E = 1.4426950408889634
NT = (((1,), (1,)), ((), ()))
NN = (((1,), (0,)), ((), ()))
TN = (((0,), (0,)), ((), ()))


def dot(a, b, dims):
    return lax.dot_general(a, b, dims, preferred_element_type=jnp.float32)


def digits(size):
    out, stride = [], 1
    while stride < size:
        count = min(RADIX, size // stride)
        while (size // stride) % count:
            count -= 1
        if count == 1:
            count = size // stride
        out.append((stride, count))
        stride *= count
    return out


def moved(size, stride, count, step, sign):
    pairs = []
    for i in range(size):
        digit = (i // stride) % count
        if count & (count - 1) == 0:
            other = digit ^ step
        else:
            other = (digit + sign * step) % count
        pairs.append((i, i + (other - digit) * stride))
    return pairs


def gather_parts(x, axis, size):
    parts = [x]
    for stride, count in digits(size):
        block = parts[0] if len(parts) == 1 else jnp.stack(parts)
        out = list(parts)
        for step in range(1, count):
            got = lax.ppermute(block, axis, moved(size, stride, count, step, 1))
            out += [got] if len(parts) == 1 else [got[i] for i in range(len(parts))]
        parts = out
    return parts


def scatter_sum(parts, axis, size):
    for stride, count in reversed(digits(size)):
        low = len(parts) // count
        total = parts[0] if low == 1 else jnp.stack(parts[:low])
        terms = [total]
        for step in range(1, count):
            piece = parts[step * low : (step + 1) * low]
            block = piece[0] if low == 1 else jnp.stack(piece)
            terms.append(lax.ppermute(block, axis, moved(size, stride, count, step, -1)))
        total = functools.reduce(jnp.add, terms)
        parts = [total] if low == 1 else [total[i] for i in range(low)]
    return parts[0]


def all_sum(x, axis, size):
    for stride, count in digits(size):
        terms = [x]
        for step in range(1, count):
            terms.append(lax.ppermute(x, axis, moved(size, stride, count, step, 1)))
        x = functools.reduce(jnp.add, terms)
    return x


def kernel(*refs, parts):
    q_ref, g_ref, bk_ref, bv_ref, par_ref, len_ref = refs[:6]
    pre_refs = refs[6 : 6 + parts]
    dq_ref, dbk_ref, dbv_ref = refs[6 + parts : 9 + parts]
    out_refs = refs[9 + parts :]
    count, length, _ = q_ref.shape
    rows = pre_refs[0].shape[0]
    prefix = rows * parts
    heads = bk_ref.shape[2] // HD
    factor = HD**-0.5
    pre = jnp.concatenate([r[...] for r in pre_refs], axis=0)
    width = heads * HD

    slot = lax.broadcasted_iota(jnp.int32, (length, length), 0)
    token = lax.broadcasted_iota(jnp.int32, (length, length), 1)
    masks = []
    for b in range(count):
        hit = (slot == token) | (slot == par_ref[b : b + 1, :])
        reach = hit.astype(jnp.float32).astype(jnp.bfloat16)
        for rounds in range((length - 1).bit_length()):
            paths = dot(reach, reach, NN)
            reach = jnp.minimum(paths, 1.0).astype(jnp.bfloat16)
        wide = jnp.concatenate([reach.astype(jnp.float32)] * PER, axis=1)
        masks.append(wide > 0.5)
    place = lax.broadcasted_iota(jnp.int32, (1, PER * length), 1) % length

    for h in range(heads):
        low = h * HD
        key_sum = value_sum = None
        for b in range(count):
            keys = jnp.concatenate([pre[:, low : low + HD], bk_ref[b, :, low : low + HD]], axis=0)
            values = jnp.concatenate(
                [pre[:, width + low : width + low + HD], bv_ref[b, :, low : low + HD]], axis=0
            )
            cols = [slice((h * PER + m) * HD, (h * PER + m + 1) * HD) for m in range(PER)]
            q = jnp.concatenate([q_ref[b, :, c] for c in cols], axis=0)
            g = jnp.concatenate([g_ref[b, :, c] for c in cols], axis=0)
            live = (place < len_ref[b]).astype(jnp.float32)
            scores = dot(keys, q, NT) * (factor * LOG2E)
            scores = jnp.concatenate(
                [scores[:prefix], jnp.where(masks[b], scores[prefix:], -1e30)], axis=0
            )
            dweights = dot(values, g, NT)
            powers = jnp.exp2(scores - jnp.max(scores, axis=0, keepdims=True))
            weights = powers * (live / jnp.sum(powers, axis=0, keepdims=True))
            rounded = weights.astype(jnp.bfloat16)
            delta = jnp.sum(rounded.astype(jnp.float32) * dweights, axis=0, keepdims=True)
            dscores = (weights * (dweights - delta)).astype(jnp.bfloat16)
            value_grad = dot(rounded, g, NN)
            key_grad = dot(dscores, q, NN) * factor
            query_grad = (dot(dscores, keys, TN) * factor).astype(jnp.bfloat16)
            for m, c in enumerate(cols):
                dq_ref[b, :, c] = query_grad[m * length : (m + 1) * length]
            dbk_ref[b, :, low : low + HD] = key_grad[prefix:].astype(jnp.bfloat16)
            dbv_ref[b, :, low : low + HD] = value_grad[prefix:].astype(jnp.bfloat16)
            key_sum = key_grad[:prefix] if b == 0 else key_sum + key_grad[:prefix]
            value_sum = value_grad[:prefix] if b == 0 else value_sum + value_grad[:prefix]
        for i, ref in enumerate(out_refs):
            ref[:, low : low + HD] = key_sum[i * rows : (i + 1) * rows]
            ref[:, width + low : width + low + HD] = value_sum[i * rows : (i + 1) * rows]


def body(
    queries, branch_keys, branch_values, prefix_keys, prefix_values, out_grad, parents, lengths,
    *, groups, branches
):
    packed = jnp.concatenate([prefix_keys, prefix_values], axis=1)
    parts = gather_parts(packed, "group", groups)
    vmem = pl.BlockSpec(memory_space=pltpu.VMEM)
    outs = pl.pallas_call(
        functools.partial(kernel, parts=groups),
        out_shape=[
            jax.ShapeDtypeStruct(queries.shape, jnp.bfloat16),
            jax.ShapeDtypeStruct(branch_keys.shape, jnp.bfloat16),
            jax.ShapeDtypeStruct(branch_values.shape, jnp.bfloat16),
        ]
        + [jax.ShapeDtypeStruct(packed.shape, jnp.float32)] * groups,
        in_specs=[vmem] * 5 + [pl.BlockSpec(memory_space=pltpu.SMEM)] + [vmem] * groups,
        out_specs=[vmem] * (3 + groups),
        compiler_params=pltpu.CompilerParams(vmem_limit_bytes=48 * 1024 * 1024),
    )(queries, out_grad, branch_keys, branch_values, parents, lengths, *parts)
    owned = scatter_sum(outs[3:], "group", groups)
    total = all_sum(owned, "branch", branches).astype(jnp.bfloat16)
    half = prefix_keys.shape[1]
    return outs[0], outs[1], outs[2], total[:, :half], total[:, half:]


def solution(mesh):
    sharded = P(("group", "branch"), None, "head")
    return jax.shard_map(
        functools.partial(body, groups=mesh.shape["group"], branches=mesh.shape["branch"]),
        mesh=mesh,
        in_specs=(
            sharded,
            sharded,
            sharded,
            P("group", "head"),
            P("group", "head"),
            sharded,
            P(("group", "branch"), None),
            P(("group", "branch")),
        ),
        out_specs=(sharded, sharded, sharded, P("group", "head"), P("group", "head")),
        check_vma=False,
    )
```

time: 106 us -> 34.6 us (0.33)
  blocking collectives: 45.6 us -> 0 us
  between operations: 14.6 us -> 0.68 us
  starting transfers between devices: 0.08 us -> 13.7 us
  matrix products: 10.8 us -> 0 us
  local copies, waits for them, and re-layouts: 15.6 us -> 5.08 us
  other arithmetic: 5.91 us -> 0.02 us
  Pallas kernels: 0 us -> 4.04 us
  waiting for transfers between devices: 12.3 us -> 10.7 us
    all_gather x2 -> x0, blocking collectives: 28.2 us -> none  [the longest x1 14.8 us: body(): lax.all_gather(prefix_keys, 'group', axis=0, tiled=True)]
    psum x1 -> x0, blocking collectives: 17.4 us -> none  [body(): total_keys, total_values = lax.psum((owned_keys, owned_values), 'branch')]
    ppermute x0 -> x9, starting transfers between devices: none -> 13.7 us  [the longest x3 5.76 us: gather_parts(): got = lax.ppermute(block, axis, moved(size, stride, count, step, 1))]
    reduce_scatter x2 -> x0, waiting for transfers between devices: 12.2 us -> none  [the longest x1 12.2 us: body(): lax.psum_scatter(key_terms, 'group', scatter_dimension=0, tiled=True)]
    dot_general x30 -> x0, matrix products: 10.8 us -> none  [the longest x6 1.68 us: ancestors(): jnp.einsum('btv,bvu->btu', reach, reach, preferred_element_type=jnp.float32)]
    ppermute x0 -> x9, waiting for transfers between devices: none -> 10.7 us  [the longest x3 4 us: gather_parts(): got = lax.ppermute(block, axis, moved(size, stride, count, step, 1))]
    unnamed x68 -> x15, local copies, waits for them, and re-layouts: 11.3 us -> 4.47 us
    pallas_call x0 -> x1, Pallas kernels: none -> 4.04 us  [body(): pl.pallas_call(functools.partial(kernel, parts=groups), out_shape=[jax.Sh...]
  transfers between devices with their start and end apart: 2 -> 9, of which waited for: 1 -> 7; matrix products, arithmetic and copies ran while one was open for 10% -> 0% of each run, Pallas kernels for 0% -> 0%
where the time goes in v1:
time: 34.6 us; the launch traced here: 34.2 us
  starting transfers between devices  13.7 us (40%)
  waiting for transfers between devices  10.7 us (31%)
  local copies, waits for them, and re-layouts  5.08 us (15%)
  Pallas kernels  4.04 us (12%)
  between operations  0.68 us (2%)
    ppermute x3, starting transfers between devices, gather_parts(): got = lax.ppermute(block, axis, moved(size, stride, count, step, 1))  5.76 us
    unnamed x15, local copies, waits for them, and re-layouts  4.47 us
    ppermute x3, starting transfers between devices, scatter_sum(): lax.ppermute(block, axis, moved(size, stride, count, step, -1))  4.39 us
    pallas_call x1, Pallas kernels, body(): pl.pallas_call(functools.partial(kernel, parts=groups), out_shape=[jax.Sh...  4.04 us
    ppermute x3, waiting for transfers between devices, gather_parts(): got = lax.ppermute(block, axis, moved(size, stride, count, step, 1))  4 us
    ppermute x3, starting transfers between devices, all_sum(): terms.append(lax.ppermute(x, axis, moved(size, stride, count, step, 1)))  3.55 us
    ppermute x3, waiting for transfers between devices, all_sum(): terms.append(lax.ppermute(x, axis, moved(size, stride, count, step, 1)))  3.38 us
    ppermute x3, waiting for transfers between devices, scatter_sum(): lax.ppermute(block, axis, moved(size, stride, count, step, -1))  3.36 us
  transfers between devices with their start and end apart: 9, of which 7 were waited for; matrix products, arithmetic and copies ran while one was open for 0% of the time, Pallas kernels for 0%

profile of v1, /device:TPU:0, one launch (start us, length us, event | category | flops | bytes accessed | tf_op | source)
XLA Modules:
  0.0 34.2 jit_solution(3839022971664577472)
XLA Ops:
  0.6 0.0 copy-start.6
  0.6 0.7 %constant_dynamic-update-slice_fusion.1 = bf16[16,512]{1,0:T(8,128)(2,1)S(1)} fusion(bf16[16,256]{1,0:T(8,128)(2,1)} %param.11), kind=kLoop, calls=%fused_computation.3 | loop fusion | bytes 16384
  1.3 0.0 copy-done.6
  1.3 0.0 copy-start.4
  1.4 0.0 copy-start.5
  1.4 5.1 %collective-permute-start.2 = (bf16[16,512]{1,0:T(8,128)(2,1)S(1)}, bf16[16,512]{1,0:T(8,128)(2,1)S(1)}, u32[]{:S(2)}, u32[]{:S(2)}) collective-permute-start(bf16[16,512]{1,0:T(8,128)(2,1)S(1)} %constant_dynamic-update-slice_fusion.refs_6_), channel_id=1, source_target_pairs={{0,24},{8,16},{16,8},{24,0},{1,25},{9,17},{17,9},{25,1},{2,26},{10... | collective-permute-start | bytes 49160 | tf_op jit(solution)/shard_map/ppermute | solution.py:56
  6.5 0.0 collective-permute-start.1
  6.5 0.6 %collective-permute-start = (bf16[16,512]{1,0:T(8,128)(2,1)S(1)}, bf16[16,512]{1,0:T(8,128)(2,1)S(1)}, u32[]{:S(2)}, u32[]{:S(2)}) collective-permute-start(bf16[16,512]{1,0:T(8,128)(2,1)S(1)} %constant_dynamic-update-slice_fusion.refs_6_), channel_id=1, source_target_pairs={{0,8},{8,0},{16,24},{24,16},{1,9},{9,1},{17,25},{25,17},{2,10},{10... | collective-permute-start | bytes 49160 | tf_op jit(solution)/shard_map/ppermute | solution.py:56
  7.1 1.1 %collective-permute-done.2.refs_9_ = bf16[16,512]{1,0:T(8,128)(2,1)S(1)} collective-permute-done((bf16[16,512]{1,0:T(8,128)(2,1)S(1)}, bf16[16,512]{1,0:T(8,128)(2,1)S(1)}, u32[]{:S(2)}, u32[]{:S(2)}) %collective-permute-start.2) | collective-permute-done | bytes 16416 | tf_op jit(solution)/shard_map/ppermute | solution.py:56
  8.2 2.9 %collective-permute-done.1.refs_8_ = bf16[16,512]{1,0:T(8,128)(2,1)S(1)} collective-permute-done((bf16[16,512]{1,0:T(8,128)(2,1)S(1)}, bf16[16,512]{1,0:T(8,128)(2,1)S(1)}, u32[]{:S(2)}, u32[]{:S(2)}) %collective-permute-start.1) | collective-permute-done | bytes 16416 | tf_op jit(solution)/shard_map/ppermute | solution.py:56
  11.1 0.0 collective-permute-done.refs_7_
  11.1 0.0 copy-done.4
  11.1 0.0 copy-done.5
  11.1 0.0 copy-start
  11.1 1.0 %copy-done = bf16[2,64,2048]{2,1,0:T(8,128)(2,1)S(1)} copy-done((bf16[2,64,2048]{2,1,0:T(8,128)(2,1)S(1)}, bf16[2,64,2048]{2,1,0:T(8,128)(2,1)}, u32[]{:S(2)}) %copy-start) | copy-done | bytes 524312
  12.2 0.0 copy-start.1
  12.2 1.0 %copy-done.1 = bf16[2,64,2048]{2,1,0:T(8,128)(2,1)S(1)} copy-done((bf16[2,64,2048]{2,1,0:T(8,128)(2,1)S(1)}, bf16[2,64,2048]{2,1,0:T(8,128)(2,1)}, u32[]{:S(2)}) %copy-start.1) | copy-done | bytes 524312
  13.2 0.0 copy-start.2
  13.2 0.8 %copy-done.2 = bf16[2,64,256]{2,1,0:T(8,128)(2,1)S(1)} copy-done((bf16[2,64,256]{2,1,0:T(8,128)(2,1)S(1)}, bf16[2,64,256]{2,1,0:T(8,128)(2,1)}, u32[]{:S(2)}) %copy-start.2) | copy-done | bytes 65560
  14.0 0.0 copy-start.3
  14.1 0.8 %copy-done.3 = bf16[2,64,256]{2,1,0:T(8,128)(2,1)S(1)} copy-done((bf16[2,64,256]{2,1,0:T(8,128)(2,1)S(1)}, bf16[2,64,256]{2,1,0:T(8,128)(2,1)}, u32[]{:S(2)}) %copy-start.3) | copy-done | bytes 65560
  14.9 4.0 %shard_map.119 = (bf16[2,64,2048]{2,1,0:T(8,128)(2,1)}, bf16[2,64,256]{2,1,0:T(8,128)(2,1)}, bf16[2,64,256]{2,1,0:T(8,128)(2,1)}, f32[16,512]{1,0:T(8,128)S(1)},...) custom-call(bf16[2,64,2048]{2,1,0:T(8,128)(2,1)S(1)} %copy-done, ...), custom_call_target="tpu_custom_call" | custom-call | tf_op jit(solution)/shard_map/pallas_call | solution.py:154
  18.9 0.0 collective-permute-start.3
  18.9 2.0 %collective-permute-start.4 = (f32[16,512]{1,0:T(8,128)S(1)}, f32[16,512]{1,0:T(8,128)S(1)}, u32[]{:S(2)}, u32[]{:S(2)}) collective-permute-start(f32[16,512]{1,0:T(8,128)S(1)} %get-tuple-element.17), channel_id=1, source_target_pairs={{0,16},{8,24},{16,0},{24,8},{1,17},{9,25},{17,1},{25,9},{2,18},{10... | collective-permute-start | bytes 98312 | tf_op jit(solution)/shard_map/ppermute | solution.py:70
  20.9 2.4 %collective-permute-start.5 = (f32[16,512]{1,0:T(8,128)S(1)}, f32[16,512]{1,0:T(8,128)S(1)}, u32[]{:S(2)}, u32[]{:S(2)}) collective-permute-start(f32[16,512]{1,0:T(8,128)S(1)} %get-tuple-element.18), channel_id=1, source_target_pairs={{0,24},{8,16},{16,8},{24,0},{1,25},{9,17},{17,9},{25,1},{2,26},{10... | collective-permute-start | bytes 98312 | tf_op jit(solution)/shard_map/ppermute | solution.py:70
  23.3 0.0 collective-permute-done.3
  23.3 0.4 %collective-permute-done.4 = f32[16,512]{1,0:T(8,128)S(1)} collective-permute-done((f32[16,512]{1,0:T(8,128)S(1)}, f32[16,512]{1,0:T(8,128)S(1)}, u32[]{:S(2)}, u32[]{:S(2)}) %collective-permute-start.4) | collective-permute-done | bytes 32800 | tf_op jit(solution)/shard_map/ppermute | solution.py:70
  23.8 2.9 %collective-permute-done.5 = f32[16,512]{1,0:T(8,128)S(1)} collective-permute-done((f32[16,512]{1,0:T(8,128)S(1)}, f32[16,512]{1,0:T(8,128)S(1)}, u32[]{:S(2)}, u32[]{:S(2)}) %collective-permute-start.5) | collective-permute-done | bytes 32800 | tf_op jit(solution)/shard_map/ppermute | solution.py:70
  26.7 2.5 %collective-permute-start.8 = (f32[16,512]{1,0:T(8,128)S(1)}, f32[16,512]{1,0:T(8,128)S(1)}, u32[]{:S(2)}, u32[]{:S(2)}) collective-permute-start(f32[16,512]{1,0:T(8,128)S(1)} %add_add_fusion), channel_id=1, source_target_pairs={{0,6},{2,4},{4,2},{6,0},{1,7},{3,5},{5,3},{7,1},{8,14},{10,12},{12... | collective-permute-start | bytes 98312 | tf_op jit(solution)/shard_map/ppermute | solution.py:80
  29.2 0.5 %collective-permute-start.7 = (f32[16,512]{1,0:T(8,128)S(1)}, f32[16,512]{1,0:T(8,128)S(1)}, u32[]{:S(2)}, u32[]{:S(2)}) collective-permute-start(f32[16,512]{1,0:T(8,128)S(1)} %add_add_fusion), channel_id=1, source_target_pairs={{0,4},{2,6},{4,0},{6,2},{1,5},{3,7},{5,1},{7,3},{8,12},{10,14},{12... | collective-permute-start | bytes 98312 | tf_op jit(solution)/shard_map/ppermute | solution.py:80
  29.7 0.5 %collective-permute-start.6 = (f32[16,512]{1,0:T(8,128)S(1)}, f32[16,512]{1,0:T(8,128)S(1)}, u32[]{:S(2)}, u32[]{:S(2)}) collective-permute-start(f32[16,512]{1,0:T(8,128)S(1)} %add_add_fusion), channel_id=1, source_target_pairs={{0,2},{2,0},{4,6},{6,4},{1,3},{3,1},{5,7},{7,5},{8,10},{10,8},{12,... | collective-permute-start | bytes 98312 | tf_op jit(solution)/shard_map/ppermute | solution.py:80
  30.2 1.3 %collective-permute-done.8 = f32[16,512]{1,0:T(8,128)S(1)} collective-permute-done((f32[16,512]{1,0:T(8,128)S(1)}, f32[16,512]{1,0:T(8,128)S(1)}, u32[]{:S(2)}, u32[]{:S(2)}) %collective-permute-start.8) | collective-permute-done | bytes 32800 | tf_op jit(solution)/shard_map/ppermute | solution.py:80
  31.6 1.6 %collective-permute-done.7 = f32[16,512]{1,0:T(8,128)S(1)} collective-permute-done((f32[16,512]{1,0:T(8,128)S(1)}, f32[16,512]{1,0:T(8,128)S(1)}, u32[]{:S(2)}, u32[]{:S(2)}) %collective-permute-start.7) | collective-permute-done | bytes 32800 | tf_op jit(solution)/shard_map/ppermute | solution.py:80
  33.1 0.5 %collective-permute-done.6 = f32[16,512]{1,0:T(8,128)S(1)} collective-permute-done((f32[16,512]{1,0:T(8,128)S(1)}, f32[16,512]{1,0:T(8,128)S(1)}, u32[]{:S(2)}, u32[]{:S(2)}) %collective-permute-start.6) | collective-permute-done | bytes 32800 | tf_op jit(solution)/shard_map/ppermute | solution.py:80
  33.6 0.6 %fusion = (bf16[16,256]{1,0:T(8,128)(2,1)}, bf16[16,256]{1,0:T(8,128)(2,1)}) fusion(bf16[16,512]{1,0:T(8,128)(2,1)S(1)} %add_convert_fusion), kind=kLoop, calls=%fused_computation.4 | loop fusion | bytes 32768 | tf_op jit(solution)/shard_map/slice | solution.py:169
  (3 shorter events, 0.0 us)
Async XLA Ops:
  0.6 0.7 %copy-start.6 = (bf16[16,256]{1,0:T(8,128)(2,1)S(1)}, bf16[16,256]{1,0:T(8,128)(2,1)}, u32[]{:S(2)}) copy-start(bf16[16,256]{1,0:T(8,128)(2,1)} %param.12) | copy-start | bytes 24580
  1.3 9.8 %copy-start.4 = (s32[2,64]{1,0:T(2,128)S(1)}, s32[2,64]{1,0:T(2,128)}, u32[]{:S(2)}) copy-start(s32[2,64]{1,0:T(2,128)} %refs_4_.1) | copy-start | bytes 1540
  1.4 9.8 %copy-start.5 = (s32[2]{0:T(128)S(1)}, s32[2]{0:T(128)}, u32[]{:S(2)}) copy-start(s32[2]{0:T(128)} %refs_5_.1) | copy-start | bytes 28
  1.4 6.8 %collective-permute-start.2 = (bf16[16,512]{1,0:T(8,128)(2,1)S(1)}, bf16[16,512]{1,0:T(8,128)(2,1)S(1)}, u32[]{:S(2)}, u32[]{:S(2)}) collective-permute-start(bf16[16,512]{1,0:T(8,128)(2,1)S(1)} %constant_dynamic-update-slice_fusion.refs_6_), channel_id=1, source_target_pairs={{0,24},{8,16},{16,8},{24,0},{1,25},{9,17},{17,9},{25,1},{2,26},{10... | collective-permute-start | bytes 49160 | tf_op jit(solution)/shard_map/ppermute | solution.py:56
  6.5 4.6 %collective-permute-start.1 = (bf16[16,512]{1,0:T(8,128)(2,1)S(1)}, bf16[16,512]{1,0:T(8,128)(2,1)S(1)}, u32[]{:S(2)}, u32[]{:S(2)}) collective-permute-start(bf16[16,512]{1,0:T(8,128)(2,1)S(1)} %constant_dynamic-update-slice_fusion.refs_6_), channel_id=1, source_target_pairs={{0,16},{8,24},{16,0},{24,8},{1,17},{9,25},{17,1},{25,9},{2,18},{10... | collective-permute-start | bytes 49160 | tf_op jit(solution)/shard_map/ppermute | solution.py:56
  6.5 4.6 %collective-permute-start = (bf16[16,512]{1,0:T(8,128)(2,1)S(1)}, bf16[16,512]{1,0:T(8,128)(2,1)S(1)}, u32[]{:S(2)}, u32[]{:S(2)}) collective-permute-start(bf16[16,512]{1,0:T(8,128)(2,1)S(1)} %constant_dynamic-update-slice_fusion.refs_6_), channel_id=1, source_target_pairs={{0,8},{8,0},{16,24},{24,16},{1,9},{9,1},{17,25},{25,17},{2,10},{10... | collective-permute-start | bytes 49160 | tf_op jit(solution)/shard_map/ppermute | solution.py:56
  11.1 1.0 %copy-start = (bf16[2,64,2048]{2,1,0:T(8,128)(2,1)S(1)}, bf16[2,64,2048]{2,1,0:T(8,128)(2,1)}, u32[]{:S(2)}) copy-start(bf16[2,64,2048]{2,1,0:T(8,128)(2,1)} %refs_0_.1) | copy-start | bytes 1572868
  12.2 1.0 %copy-start.1 = (bf16[2,64,2048]{2,1,0:T(8,128)(2,1)S(1)}, bf16[2,64,2048]{2,1,0:T(8,128)(2,1)}, u32[]{:S(2)}) copy-start(bf16[2,64,2048]{2,1,0:T(8,128)(2,1)} %refs_1_.1) | copy-start | bytes 1572868
  13.2 0.8 %copy-start.2 = (bf16[2,64,256]{2,1,0:T(8,128)(2,1)S(1)}, bf16[2,64,256]{2,1,0:T(8,128)(2,1)}, u32[]{:S(2)}) copy-start(bf16[2,64,256]{2,1,0:T(8,128)(2,1)} %refs_2_.1) | copy-start | bytes 196612
  14.0 0.8 %copy-start.3 = (bf16[2,64,256]{2,1,0:T(8,128)(2,1)S(1)}, bf16[2,64,256]{2,1,0:T(8,128)(2,1)}, u32[]{:S(2)}) copy-start(bf16[2,64,256]{2,1,0:T(8,128)(2,1)} %refs_3_.1) | copy-start | bytes 196612
  18.9 4.4 %collective-permute-start.3 = (f32[16,512]{1,0:T(8,128)S(1)}, f32[16,512]{1,0:T(8,128)S(1)}, u32[]{:S(2)}, u32[]{:S(2)}) collective-permute-start(f32[16,512]{1,0:T(8,128)S(1)} %get-tuple-element.16), channel_id=1, source_target_pairs={{0,8},{8,0},{16,24},{24,16},{1,9},{9,1},{17,25},{25,17},{2,10},{10... | collective-permute-start | bytes 98312 | tf_op jit(solution)/shard_map/ppermute | solution.py:70
  18.9 4.8 %collective-permute-start.4 = (f32[16,512]{1,0:T(8,128)S(1)}, f32[16,512]{1,0:T(8,128)S(1)}, u32[]{:S(2)}, u32[]{:S(2)}) collective-permute-start(f32[16,512]{1,0:T(8,128)S(1)} %get-tuple-element.17), channel_id=1, source_target_pairs={{0,16},{8,24},{16,0},{24,8},{1,17},{9,25},{17,1},{25,9},{2,18},{10... | collective-permute-start | bytes 98312 | tf_op jit(solution)/shard_map/ppermute | solution.py:70
  20.9 5.7 %collective-permute-start.5 = (f32[16,512]{1,0:T(8,128)S(1)}, f32[16,512]{1,0:T(8,128)S(1)}, u32[]{:S(2)}, u32[]{:S(2)}) collective-permute-start(f32[16,512]{1,0:T(8,128)S(1)} %get-tuple-element.18), channel_id=1, source_target_pairs={{0,24},{8,16},{16,8},{24,0},{1,25},{9,17},{17,9},{25,1},{2,26},{10... | collective-permute-start | bytes 98312 | tf_op jit(solution)/shard_map/ppermute | solution.py:70
  26.7 4.9 %collective-permute-start.8 = (f32[16,512]{1,0:T(8,128)S(1)}, f32[16,512]{1,0:T(8,128)S(1)}, u32[]{:S(2)}, u32[]{:S(2)}) collective-permute-start(f32[16,512]{1,0:T(8,128)S(1)} %add_add_fusion), channel_id=1, source_target_pairs={{0,6},{2,4},{4,2},{6,0},{1,7},{3,5},{5,3},{7,1},{8,14},{10,12},{12... | collective-permute-start | bytes 98312 | tf_op jit(solution)/shard_map/ppermute | solution.py:80
  29.2 3.9 %collective-permute-start.7 = (f32[16,512]{1,0:T(8,128)S(1)}, f32[16,512]{1,0:T(8,128)S(1)}, u32[]{:S(2)}, u32[]{:S(2)}) collective-permute-start(f32[16,512]{1,0:T(8,128)S(1)} %add_add_fusion), channel_id=1, source_target_pairs={{0,4},{2,6},{4,0},{6,2},{1,5},{3,7},{5,1},{7,3},{8,12},{10,14},{12... | collective-permute-start | bytes 98312 | tf_op jit(solution)/shard_map/ppermute | solution.py:80
  29.7 3.9 %collective-permute-start.6 = (f32[16,512]{1,0:T(8,128)S(1)}, f32[16,512]{1,0:T(8,128)S(1)}, u32[]{:S(2)}, u32[]{:S(2)}) collective-permute-start(f32[16,512]{1,0:T(8,128)S(1)} %add_add_fusion), channel_id=1, source_target_pairs={{0,2},{2,0},{4,6},{6,4},{1,3},{3,1},{5,7},{7,5},{8,10},{10,8},{12,... | collective-permute-start | bytes 98312 | tf_op jit(solution)/shard_map/ppermute | solution.py:80

commit v2 on v1

v2 whole, which is shorter than its diff:
```python
import functools

import jax
import jax.numpy as jnp
from jax import lax
from jax.experimental import pallas as pl
from jax.experimental.pallas import tpu as pltpu
from jax.sharding import PartitionSpec as P

QH = 32
KVH = 4
HD = 128
PER = QH // KVH
RADIX = 4
LOG2E = 1.4426950408889634
NT = (((1,), (1,)), ((), ()))
NN = (((1,), (0,)), ((), ()))
TN = (((0,), (0,)), ((), ()))


def dot(a, b, dims):
    return lax.dot_general(a, b, dims, preferred_element_type=jnp.float32)


def digits(size):
    out, stride = [], 1
    while stride < size:
        count = min(RADIX, size // stride)
        while (size // stride) % count:
            count -= 1
        if count == 1:
            count = size // stride
        out.append((stride, count))
        stride *= count
    return out


def moved(size, stride, count, step, sign):
    pairs = []
    for i in range(size):
        digit = (i // stride) % count
        if count & (count - 1) == 0:
            other = digit ^ step
        else:
            other = (digit + sign * step) % count
        pairs.append((i, i + (other - digit) * stride))
    return pairs


def gather_parts(x, axis, size):
    parts = [x]
    for stride, count in digits(size):
        block = parts[0] if len(parts) == 1 else jnp.stack(parts)
        out = list(parts)
        for step in range(1, count):
            got = lax.ppermute(block, axis, moved(size, stride, count, step, 1))
            out += [got] if len(parts) == 1 else [got[i] for i in range(len(parts))]
        parts = out
    return parts


def tree_sum(terms):
    while len(terms) > 1:
        terms = [a + b for a, b in zip(terms[::2], terms[1::2])] + terms[len(terms) & ~1 :]
    return terms[0]


def scatter_sum(parts, axis, size):
    for stride, count in reversed(digits(size)):
        low = len(parts) // count
        terms = [parts[0].astype(jnp.float32) if low == 1 else jnp.stack(parts[:low]).astype(jnp.float32)]
        for step in range(1, count):
            piece = parts[step * low : (step + 1) * low]
            block = piece[0] if low == 1 else jnp.stack(piece)
            got = lax.ppermute(block, axis, moved(size, stride, count, step, -1))
            terms.append(got.astype(jnp.float32))
        total = tree_sum(terms).astype(parts[0].dtype)
        parts = [total] if low == 1 else [total[i] for i in range(low)]
    return parts[0]


def all_sum(x, axis, size):
    for stride, count in digits(size):
        terms = [x]
        for step in range(1, count):
            terms.append(lax.ppermute(x, axis, moved(size, stride, count, step, 1)))
        x = tree_sum([t.astype(jnp.float32) for t in terms]).astype(x.dtype)
    return x


def head_rows(ref, b, h):
    cols = [slice((h * PER + m) * HD, (h * PER + m + 1) * HD) for m in range(PER)]
    return jnp.concatenate([ref[b, :, c] for c in cols], axis=0)


def tree_kernel(
    q_hbm, g_hbm, bk_hbm, bv_hbm, par_ref, len_ref,
    q_ref, g_ref, bk_ref, power_ref, dweight_ref, max_ref, sum_ref, dot_ref, live_ref,
    bv_ref, sems,
):
    count, length, _ = q_ref.shape
    heads = bk_ref.shape[2] // HD
    pairs = ((q_hbm, q_ref), (g_hbm, g_ref), (bk_hbm, bk_ref), (bv_hbm, bv_ref))
    copies = [pltpu.make_async_copy(s, d, sems.at[i]) for i, (s, d) in enumerate(pairs)]
    for copy in copies:
        copy.start()
    slot = lax.broadcasted_iota(jnp.int32, (length, length), 0)
    token = lax.broadcasted_iota(jnp.int32, (length, length), 1)
    reaches = []
    for b in range(count):
        hit = (slot == token) | (slot == par_ref[b : b + 1, :])
        reaches.append(hit.astype(jnp.float32).astype(jnp.bfloat16))
    for rounds in range((length - 1).bit_length()):
        reaches = [jnp.minimum(dot(r, r, NN), 1.0).astype(jnp.bfloat16) for r in reaches]
    masks = [jnp.concatenate([r.astype(jnp.float32)] * PER, axis=1) > 0.5 for r in reaches]
    place = lax.broadcasted_iota(jnp.int32, (1, PER * length), 1) % length
    lives = [(place < len_ref[b]).astype(jnp.float32) for b in range(count)]
    for copy in copies:
        copy.wait()
    for h in range(heads):
        low = h * HD
        for b in range(count):
            i = h * count + b
            scores = dot(bk_ref[b, :, low : low + HD], head_rows(q_ref, b, h), NT)
            dweights = dot(bv_ref[b, :, low : low + HD], head_rows(g_ref, b, h), NT)
            scores = jnp.where(masks[b], scores * (HD**-0.5 * LOG2E), -1e30)
            top = jnp.max(scores, axis=0, keepdims=True)
            powers = jnp.exp2(scores - top)
            power_ref[i] = powers
            dweight_ref[i] = dweights
            live_ref[i] = lives[b]
            max_ref[i] = top
            sum_ref[i] = jnp.sum(powers, axis=0, keepdims=True)
            dot_ref[i] = jnp.sum(powers * dweights, axis=0, keepdims=True)


def prefix_kernel(*refs, parts):
    q_ref, g_ref, max_ref, sum_ref, dot_ref, live_ref = refs[:6]
    pre_refs = refs[6 : 6 + parts]
    dscore_ref, scale_ref, delta_ref = refs[6 + parts : 9 + parts]
    out_refs = refs[9 + parts :]
    count, length, _ = q_ref.shape
    rows, width = pre_refs[0].shape
    width //= 2
    heads = width // HD
    factor = HD**-0.5
    pre = jnp.concatenate([r[...] for r in pre_refs], axis=0)
    for h in range(heads):
        low = h * HD
        keys = pre[:, low : low + HD]
        values = pre[:, width + low : width + low + HD]
        key_sum = value_sum = None
        for b in range(count):
            i = h * count + b
            q = head_rows(q_ref, b, h)
            g = head_rows(g_ref, b, h)
            scores = dot(keys, q, NT) * (factor * LOG2E)
            dweights = dot(values, g, NT)
            tree_max = max_ref[i]
            top = jnp.maximum(jnp.max(scores, axis=0, keepdims=True), tree_max)
            powers = jnp.exp2(scores - top)
            tree = jnp.exp2(tree_max - top)
            scale = live_ref[i] / (jnp.sum(powers, axis=0, keepdims=True) + tree * sum_ref[i])
            delta = scale * (
                jnp.sum(powers * dweights, axis=0, keepdims=True) + tree * dot_ref[i]
            )
            weights = powers * scale
            dscores = (weights * (dweights - delta)).astype(jnp.bfloat16)
            value_grad = dot(weights.astype(jnp.bfloat16), g, NN)
            key_grad = dot(dscores, q, NN) * factor
            dscore_ref[i] = dscores
            scale_ref[i] = scale * tree
            delta_ref[i] = delta
            key_sum = key_grad if b == 0 else key_sum + key_grad
            value_sum = value_grad if b == 0 else value_sum + value_grad
        for i, ref in enumerate(out_refs):
            ref[:, low : low + HD] = key_sum[i * rows : (i + 1) * rows].astype(ref.dtype)
            ref[:, width + low : width + low + HD] = value_sum[i * rows : (i + 1) * rows].astype(
                ref.dtype
            )


def branch_kernel(*refs, parts):
    q_ref, g_ref, bk_ref, power_ref, dweight_ref, dscore_ref, scale_ref, delta_ref = refs[:8]
    pre_refs = refs[8 : 8 + parts]
    dq_ref, dbk_ref, dbv_ref = refs[8 + parts :]
    count, length, _ = q_ref.shape
    heads = bk_ref.shape[2] // HD
    factor = HD**-0.5
    pre = jnp.concatenate([r[:, : heads * HD] for r in pre_refs], axis=0)
    for h in range(heads):
        low = h * HD
        for b in range(count):
            i = h * count + b
            weights = power_ref[i] * scale_ref[i]
            dscores = (weights * (dweight_ref[i] - delta_ref[i])).astype(jnp.bfloat16)
            tree_keys = bk_ref[b, :, low : low + HD]
            value_grad = dot(weights.astype(jnp.bfloat16), head_rows(g_ref, b, h), NN)
            key_grad = dot(dscores, head_rows(q_ref, b, h), NN) * factor
            dbk_ref[b, :, low : low + HD] = key_grad.astype(jnp.bfloat16)
            dbv_ref[b, :, low : low + HD] = value_grad.astype(jnp.bfloat16)
            both = jnp.concatenate([dscore_ref[i], dscores], axis=0)
            keys = jnp.concatenate([pre[:, low : low + HD], tree_keys], axis=0)
            query_grad = (dot(both, keys, TN) * factor).astype(jnp.bfloat16)
            for m in range(PER):
                col = (h * PER + m) * HD
                dq_ref[b, :, col : col + HD] = query_grad[m * length : (m + 1) * length]


def body(
    queries, branch_keys, branch_values, prefix_keys, prefix_values, out_grad, parents, lengths,
    *, groups, branches
):
    count, length, columns = queries.shape
    heads = branch_keys.shape[2] // HD
    prefix = prefix_keys.shape[0] * groups
    packed = jnp.concatenate([prefix_keys, prefix_values], axis=1)
    parts = gather_parts(packed, "group", groups)
    vmem = pl.BlockSpec(memory_space=pltpu.VMEM)
    smem = pl.BlockSpec(memory_space=pltpu.SMEM)
    anywhere = pl.BlockSpec(memory_space=pltpu.HBM)
    hbm = lambda x: pltpu.with_memory_space_constraint(x, pltpu.HBM)
    params = pltpu.CompilerParams(vmem_limit_bytes=16 * 1024 * 1024)
    wide = PER * length
    row = jax.ShapeDtypeStruct((heads * count, 1, wide), jnp.float32)
    block = jax.ShapeDtypeStruct((heads * count, length, wide), jnp.float32)
    like = lambda x: jax.ShapeDtypeStruct(x.shape, x.dtype)
    work = heads * count * wide * HD * 2
    q, g, keys, powers, dweights, tops, sums, dots, live = pl.pallas_call(
        tree_kernel,
        out_shape=[like(queries), like(out_grad), like(branch_keys), block, block, row, row, row, row],
        in_specs=[anywhere] * 4 + [vmem, smem],
        out_specs=[vmem] * 9,
        scratch_shapes=[
            pltpu.VMEM(branch_values.shape, branch_values.dtype),
            pltpu.SemaphoreType.DMA((4,)),
        ],
        compiler_params=params,
        cost_estimate=pl.CostEstimate(
            flops=2 * work * length, bytes_accessed=2 * queries.size * 2, transcendentals=wide * length * 4
        ),
        name="tree",
    )(*(hbm(x) for x in (queries, out_grad, branch_keys, branch_values)), parents, lengths)
    outs = pl.pallas_call(
        functools.partial(prefix_kernel, parts=groups),
        out_shape=[
            jax.ShapeDtypeStruct((heads * count, prefix, wide), jnp.bfloat16), row, row
        ]
        + [like(packed)] * groups,
        in_specs=[vmem] * (6 + groups),
        out_specs=[vmem] * (3 + groups),
        compiler_params=params,
        cost_estimate=pl.CostEstimate(
            flops=4 * work * prefix, bytes_accessed=0, transcendentals=wide * prefix * 4
        ),
        name="prefix",
    )(q, g, tops, sums, dots, live, *parts)
    query_grad, branch_key_grad, branch_value_grad = pl.pallas_call(
        functools.partial(branch_kernel, parts=groups),
        out_shape=[like(queries), like(branch_keys), like(branch_values)],
        in_specs=[vmem] * (8 + groups),
        out_specs=[vmem] * 3,
        compiler_params=params,
        cost_estimate=pl.CostEstimate(
            flops=4 * work * length, bytes_accessed=queries.size * 2, transcendentals=0
        ),
        name="branch",
    )(q, g, keys, powers, dweights, *outs[:3], *parts)
    owned = scatter_sum(outs[3:], "group", groups)
    total = all_sum(owned, "branch", branches)
    half = prefix_keys.shape[1]
    return query_grad, branch_key_grad, branch_value_grad, total[:, :half], total[:, half:]


def solution(mesh):
    sharded = P(("group", "branch"), None, "head")
    return jax.shard_map(
        functools.partial(body, groups=mesh.shape["group"], branches=mesh.shape["branch"]),
        mesh=mesh,
        in_specs=(
            sharded,
            sharded,
            sharded,
            P("group", "head"),
            P("group", "head"),
            sharded,
            P(("group", "branch"), None),
            P(("group", "branch")),
        ),
        out_specs=(sharded, sharded, sharded, P("group", "head"), P("group", "head")),
        check_vma=False,
    )
```

time: 34.6 us -> 29.3 us (0.85)
  local copies, waits for them, and re-layouts: 5.08 us -> 1.32 us
  waiting for transfers between devices: 10.7 us -> 8.42 us
  Pallas kernels: 4.04 us -> 4.82 us
    unnamed x15 -> x7, local copies, waits for them, and re-layouts: 4.47 us -> 0.72 us
    ppermute x3, waiting for transfers between devices: 3.36 us -> 2.34 us  [scatter_sum(): got = lax.ppermute(block, axis, moved(size, stride, count, step, -1))]
    ppermute x3, waiting for transfers between devices: 4 us -> 3.2 us  [gather_parts(): got = lax.ppermute(block, axis, moved(size, stride, count, step, 1))]
    pallas_call x1 -> x3, Pallas kernels: 4.04 us -> 4.82 us  [the longest x1 2.3 us: body(): pl.pallas_call(tree_kernel, out_shape=[like(queries), like(out_grad), lik...]
    ppermute x3, waiting for transfers between devices: 3.38 us -> 2.87 us  [all_sum(): terms.append(lax.ppermute(x, axis, moved(size, stride, count, step, 1)))]
  transfers between devices with their start and end apart: 9 -> 9, of which waited for: 7 -> 5; matrix products, arithmetic and copies ran while one was open for 0% -> 0% of each run, Pallas kernels for 0% -> 12%
where the time goes in v2:
time: 29.3 us; the launch traced here: 29 us
  starting transfers between devices  13.7 us (47%)
  waiting for transfers between devices  8.42 us (29%)
  Pallas kernels  4.82 us (16%)
  local copies, waits for them, and re-layouts  1.32 us (5%)
  between operations  0.7 us (2%)
    ppermute x3, starting transfers between devices, gather_parts(): got = lax.ppermute(block, axis, moved(size, stride, count, step, 1))  5.68 us
    ppermute x3, starting transfers between devices, scatter_sum(): got = lax.ppermute(block, axis, moved(size, stride, count, step, -1))  4.44 us
    ppermute x3, starting transfers between devices, all_sum(): terms.append(lax.ppermute(x, axis, moved(size, stride, count, step, 1)))  3.55 us
    ppermute x3, waiting for transfers between devices, gather_parts(): got = lax.ppermute(block, axis, moved(size, stride, count, step, 1))  3.2 us
    ppermute x3, waiting for transfers between devices, all_sum(): terms.append(lax.ppermute(x, axis, moved(size, stride, count, step, 1)))  2.87 us
    ppermute x3, waiting for transfers between devices, scatter_sum(): got = lax.ppermute(block, axis, moved(size, stride, count, step, -1))  2.34 us
    pallas_call x1, Pallas kernels, body(): pl.pallas_call(tree_kernel, out_shape=[like(queries), like(out_grad), lik...  2.3 us
    pallas_call x1, Pallas kernels, body(): pl.pallas_call(functools.partial(branch_kernel, parts=groups), out_shape=...  1.28 us
  transfers between devices with their start and end apart: 9, of which 5 were waited for; matrix products, arithmetic and copies ran while one was open for 0% of the time, Pallas kernels for 12%

profile of v2, /device:TPU:0, one launch (start us, length us, event | category | flops | bytes accessed | tf_op | source)
XLA Modules:
  0.0 29.0 jit_solution(3447427271411369321)
XLA Ops:
  0.6 0.0 copy-start.2
  0.6 0.7 %constant_dynamic-update-slice_fusion.1 = bf16[16,512]{1,0:T(8,128)(2,1)S(1)} fusion(bf16[16,256]{1,0:T(8,128)(2,1)} %param.11), kind=kLoop, calls=%fused_computation.3 | loop fusion | bytes 16384
  1.3 0.0 copy-done.2
  1.3 0.0 copy-start
  1.4 0.0 copy-start.1
  1.4 3.1 %collective-permute-start = (bf16[16,512]{1,0:T(8,128)(2,1)S(1)}, bf16[16,512]{1,0:T(8,128)(2,1)S(1)}, u32[]{:S(2)}, u32[]{:S(2)}) collective-permute-start(bf16[16,512]{1,0:T(8,128)(2,1)S(1)} %constant_dynamic-update-slice_fusion.refs_6_.refs_8_), channel_id=1, source_target_pairs={{0,8},{8,0},{16,24},{24,16},{1,9},{9,1},{17,25},{25,17},{2,10},{10... | collective-permute-start | bytes 49160 | tf_op jit(solution)/shard_map/ppermute | solution.py:56
  4.4 2.6 %collective-permute-start.1 = (bf16[16,512]{1,0:T(8,128)(2,1)S(1)}, bf16[16,512]{1,0:T(8,128)(2,1)S(1)}, u32[]{:S(2)}, u32[]{:S(2)}) collective-permute-start(bf16[16,512]{1,0:T(8,128)(2,1)S(1)} %constant_dynamic-update-slice_fusion.refs_6_.refs_8_), channel_id=1, source_target_pairs={{0,16},{8,24},{16,0},{24,8},{1,17},{9,25},{17,1},{25,9},{2,18},{10... | collective-permute-start | bytes 49160 | tf_op jit(solution)/shard_map/ppermute | solution.py:56
  7.0 0.0 collective-permute-start.2
  7.0 0.0 copy-done
  7.0 0.0 copy-done.1
  7.0 2.3 %tree.1 = (bf16[2,64,2048]{2,1,0:T(8,128)(2,1)S(1)}, bf16[2,64,2048]{2,1,0:T(8,128)(2,1)S(1)}, bf16[2,64,256]{2,1,0:T(8,128)(2,1)S(1)}, f32[4,64,512]{2,1,0:T(8,...) custom-call(bf16[2,64,2048]{2,1,0:T(8,128)(2,1)} %q_hbm.1, ...), custom_call_target="tpu_custom_call" | custom-call | flops 67108864 | bytes 1048576 | tf_op jit(solution)/shard_map/tree/pallas_call | solution.py:229
  9.4 0.0 collective-permute-done.refs_7_.refs_9_
  9.4 0.0 collective-permute-done.1.refs_8_.refs_10_
  9.4 3.2 %collective-permute-done.2.refs_9_.refs_11_ = bf16[16,512]{1,0:T(8,128)(2,1)S(1)} collective-permute-done((bf16[16,512]{1,0:T(8,128)(2,1)S(1)}, bf16[16,512]{1,0:T(8,128)(2,1)S(1)}, u32[]{:S(2)}, u32[]{:S(2)}) %collective-permute-start.2) | collective-permute-done | bytes 16416 | tf_op jit(solution)/shard_map/ppermute | solution.py:56
  12.6 1.2 %prefix.1 = (bf16[4,64,512]{2,1,0:T(8,128)(2,1)S(1)}, f32[4,1,512]{2,1,0:T(1,128)S(1)}, f32[4,1,512]{2,1,0:T(1,128)S(1)}, bf16[16,512]{1,0:T(8,128)(2,1)S(1)}, b...) custom-call(bf16[2,64,2048]{2,1,0:T(8,128)(2,1)S(1)} %get-tuple-element.24.refs_0_, ...), custom_call_target="tpu_custom_call" | custom-call | flops 134217728 | tf_op jit(solution)/shard_map/prefix/pallas_call | solution.py:244
  13.8 0.1 collective-permute-start.3
  13.9 1.2 %collective-permute-start.4 = (bf16[16,512]{1,0:T(8,128)(2,1)S(1)}, bf16[16,512]{1,0:T(8,128)(2,1)S(1)}, u32[]{:S(2)}, u32[]{:S(2)}) collective-permute-start(bf16[16,512]{1,0:T(8,128)(2,1)S(1)} %get-tuple-element.41), channel_id=1, source_target_pairs={{0,16},{8,24},{16,0},{24,8},{1,17},{9,25},{17,1},{25,9},{2,18},{10... | collective-permute-start | bytes 49160 | tf_op jit(solution)/shard_map/ppermute | solution.py:75
  15.1 3.2 %collective-permute-start.5 = (bf16[16,512]{1,0:T(8,128)(2,1)S(1)}, bf16[16,512]{1,0:T(8,128)(2,1)S(1)}, u32[]{:S(2)}, u32[]{:S(2)}) collective-permute-start(bf16[16,512]{1,0:T(8,128)(2,1)S(1)} %get-tuple-element.42), channel_id=1, source_target_pairs={{0,24},{8,16},{16,8},{24,0},{1,25},{9,17},{17,9},{25,1},{2,26},{10... | collective-permute-start | bytes 49160 | tf_op jit(solution)/shard_map/ppermute | solution.py:75
  18.3 0.0 collective-permute-done.3
  18.3 0.3 %collective-permute-done.4 = bf16[16,512]{1,0:T(8,128)(2,1)S(1)} collective-permute-done((bf16[16,512]{1,0:T(8,128)(2,1)S(1)}, bf16[16,512]{1,0:T(8,128)(2,1)S(1)}, u32[]{:S(2)}, u32[]{:S(2)}) %collective-permute-start.4) | collective-permute-done | bytes 16416 | tf_op jit(solution)/shard_map/ppermute | solution.py:75
  18.6 2.0 %collective-permute-done.5 = bf16[16,512]{1,0:T(8,128)(2,1)S(1)} collective-permute-done((bf16[16,512]{1,0:T(8,128)(2,1)S(1)}, bf16[16,512]{1,0:T(8,128)(2,1)S(1)}, u32[]{:S(2)}, u32[]{:S(2)}) %collective-permute-start.5) | collective-permute-done | bytes 16416 | tf_op jit(solution)/shard_map/ppermute | solution.py:75
  20.6 1.6 %collective-permute-start.6 = (bf16[16,512]{1,0:T(8,128)(2,1)S(1)}, bf16[16,512]{1,0:T(8,128)(2,1)S(1)}, u32[]{:S(2)}, u32[]{:S(2)}) collective-permute-start(bf16[16,512]{1,0:T(8,128)(2,1)S(1)} %add_convert_fusion.1), channel_id=1, source_target_pairs={{0,2},{2,0},{4,6},{6,4},{1,3},{3,1},{5,7},{7,5},{8,10},{10,8},{12,... | collective-permute-start | bytes 49160 | tf_op jit(solution)/shard_map/ppermute | solution.py:86
  22.2 1.5 %collective-permute-start.7 = (bf16[16,512]{1,0:T(8,128)(2,1)S(1)}, bf16[16,512]{1,0:T(8,128)(2,1)S(1)}, u32[]{:S(2)}, u32[]{:S(2)}) collective-permute-start(bf16[16,512]{1,0:T(8,128)(2,1)S(1)} %add_convert_fusion.1), channel_id=1, source_target_pairs={{0,4},{2,6},{4,0},{6,2},{1,5},{3,7},{5,1},{7,3},{8,12},{10,14},{12... | collective-permute-start | bytes 49160 | tf_op jit(solution)/shard_map/ppermute | solution.py:86
  23.7 0.5 %collective-permute-start.8 = (bf16[16,512]{1,0:T(8,128)(2,1)S(1)}, bf16[16,512]{1,0:T(8,128)(2,1)S(1)}, u32[]{:S(2)}, u32[]{:S(2)}) collective-permute-start(bf16[16,512]{1,0:T(8,128)(2,1)S(1)} %add_convert_fusion.1), channel_id=1, source_target_pairs={{0,6},{2,4},{4,2},{6,0},{1,7},{3,5},{5,3},{7,1},{8,14},{10,12},{12... | collective-permute-start | bytes 49160 | tf_op jit(solution)/shard_map/ppermute | solution.py:86
  24.2 1.3 %branch.1 = (bf16[2,64,2048]{2,1,0:T(8,128)(2,1)}, bf16[2,64,256]{2,1,0:T(8,128)(2,1)}, bf16[2,64,256]{2,1,0:T(8,128)(2,1)}) custom-call(bf16[2,64,2048]{2,1,0:T(8,128)(2,1)S(1)} %get-tuple-element.24.refs_0_, bf16[2,64,2048]{2,1,0:T(8,128)(2,1)S(1)} %get-tuple-element.25.refs_1_, bf16[2,64,256]{2,1,0:T(8,128)(2,1)S(1)} %get-tuple-element.26.refs_2_, ...), custom_call_target="tpu_custom_call" | custom-call | flops 134217728 | bytes 524288 | tf_op jit(solution)/shard_map/branch/pallas_call | solution.py:258
  25.5 0.0 collective-permute-done.6
  25.5 0.5 %collective-permute-done.7 = bf16[16,512]{1,0:T(8,128)(2,1)S(1)} collective-permute-done((bf16[16,512]{1,0:T(8,128)(2,1)S(1)}, bf16[16,512]{1,0:T(8,128)(2,1)S(1)}, u32[]{:S(2)}, u32[]{:S(2)}) %collective-permute-start.7) | collective-permute-done | bytes 16416 | tf_op jit(solution)/shard_map/ppermute | solution.py:86
  25.9 2.4 %collective-permute-done.8 = bf16[16,512]{1,0:T(8,128)(2,1)S(1)} collective-permute-done((bf16[16,512]{1,0:T(8,128)(2,1)S(1)}, bf16[16,512]{1,0:T(8,128)(2,1)S(1)}, u32[]{:S(2)}, u32[]{:S(2)}) %collective-permute-start.8) | collective-permute-done | bytes 16416 | tf_op jit(solution)/shard_map/ppermute | solution.py:86
  28.4 0.6 %fusion = (bf16[16,256]{1,0:T(8,128)(2,1)}, bf16[16,256]{1,0:T(8,128)(2,1)}) fusion(bf16[16,512]{1,0:T(8,128)(2,1)S(1)} %add_convert_fusion), kind=kLoop, calls=%fused_computation.4 | loop fusion | bytes 32768 | tf_op jit(solution)/shard_map/slice | solution.py:272
  (3 shorter events, 0.0 us)
Async XLA Ops:
  0.6 0.7 %copy-start.2 = (bf16[16,256]{1,0:T(8,128)(2,1)S(1)}, bf16[16,256]{1,0:T(8,128)(2,1)}, u32[]{:S(2)}) copy-start(bf16[16,256]{1,0:T(8,128)(2,1)} %param.12) | copy-start | bytes 24580
  1.3 5.7 %copy-start = (s32[2,64]{1,0:T(2,128)S(1)}, s32[2,64]{1,0:T(2,128)}, u32[]{:S(2)}) copy-start(s32[2,64]{1,0:T(2,128)} %par_ref.1) | copy-start | bytes 1540
  1.4 5.7 %copy-start.1 = (s32[2]{0:T(128)S(1)}, s32[2]{0:T(128)}, u32[]{:S(2)}) copy-start(s32[2]{0:T(128)} %len_ref.1) | copy-start | bytes 28
  1.4 8.0 %collective-permute-start = (bf16[16,512]{1,0:T(8,128)(2,1)S(1)}, bf16[16,512]{1,0:T(8,128)(2,1)S(1)}, u32[]{:S(2)}, u32[]{:S(2)}) collective-permute-start(bf16[16,512]{1,0:T(8,128)(2,1)S(1)} %constant_dynamic-update-slice_fusion.refs_6_.refs_8_), channel_id=1, source_target_pairs={{0,8},{8,0},{16,24},{24,16},{1,9},{9,1},{17,25},{25,17},{2,10},{10... | collective-permute-start | bytes 49160 | tf_op jit(solution)/shard_map/ppermute | solution.py:56
  4.4 4.9 %collective-permute-start.1 = (bf16[16,512]{1,0:T(8,128)(2,1)S(1)}, bf16[16,512]{1,0:T(8,128)(2,1)S(1)}, u32[]{:S(2)}, u32[]{:S(2)}) collective-permute-start(bf16[16,512]{1,0:T(8,128)(2,1)S(1)} %constant_dynamic-update-slice_fusion.refs_6_.refs_8_), channel_id=1, source_target_pairs={{0,16},{8,24},{16,0},{24,8},{1,17},{9,25},{17,1},{25,9},{2,18},{10... | collective-permute-start | bytes 49160 | tf_op jit(solution)/shard_map/ppermute | solution.py:56
  7.0 5.5 %collective-permute-start.2 = (bf16[16,512]{1,0:T(8,128)(2,1)S(1)}, bf16[16,512]{1,0:T(8,128)(2,1)S(1)}, u32[]{:S(2)}, u32[]{:S(2)}) collective-permute-start(bf16[16,512]{1,0:T(8,128)(2,1)S(1)} %constant_dynamic-update-slice_fusion.refs_6_.refs_8_), channel_id=1, source_target_pairs={{0,24},{8,16},{16,8},{24,0},{1,25},{9,17},{17,9},{25,1},{2,26},{10... | collective-permute-start | bytes 49160 | tf_op jit(solution)/shard_map/ppermute | solution.py:56
  13.8 4.5 %collective-permute-start.3 = (bf16[16,512]{1,0:T(8,128)(2,1)S(1)}, bf16[16,512]{1,0:T(8,128)(2,1)S(1)}, u32[]{:S(2)}, u32[]{:S(2)}) collective-permute-start(bf16[16,512]{1,0:T(8,128)(2,1)S(1)} %get-tuple-element.40), channel_id=1, source_target_pairs={{0,8},{8,0},{16,24},{24,16},{1,9},{9,1},{17,25},{25,17},{2,10},{10... | collective-permute-start | bytes 49160 | tf_op jit(solution)/shard_map/ppermute | solution.py:75
  13.9 4.7 %collective-permute-start.4 = (bf16[16,512]{1,0:T(8,128)(2,1)S(1)}, bf16[16,512]{1,0:T(8,128)(2,1)S(1)}, u32[]{:S(2)}, u32[]{:S(2)}) collective-permute-start(bf16[16,512]{1,0:T(8,128)(2,1)S(1)} %get-tuple-element.41), channel_id=1, source_target_pairs={{0,16},{8,24},{16,0},{24,8},{1,17},{9,25},{17,1},{25,9},{2,18},{10... | collective-permute-start | bytes 49160 | tf_op jit(solution)/shard_map/ppermute | solution.py:75
  15.1 5.5 %collective-permute-start.5 = (bf16[16,512]{1,0:T(8,128)(2,1)S(1)}, bf16[16,512]{1,0:T(8,128)(2,1)S(1)}, u32[]{:S(2)}, u32[]{:S(2)}) collective-permute-start(bf16[16,512]{1,0:T(8,128)(2,1)S(1)} %get-tuple-element.42), channel_id=1, source_target_pairs={{0,24},{8,16},{16,8},{24,0},{1,25},{9,17},{17,9},{25,1},{2,26},{10... | collective-permute-start | bytes 49160 | tf_op jit(solution)/shard_map/ppermute | solution.py:75
  20.6 4.8 %collective-permute-start.6 = (bf16[16,512]{1,0:T(8,128)(2,1)S(1)}, bf16[16,512]{1,0:T(8,128)(2,1)S(1)}, u32[]{:S(2)}, u32[]{:S(2)}) collective-permute-start(bf16[16,512]{1,0:T(8,128)(2,1)S(1)} %add_convert_fusion.1), channel_id=1, source_target_pairs={{0,2},{2,0},{4,6},{6,4},{1,3},{3,1},{5,7},{7,5},{8,10},{10,8},{12,... | collective-permute-start | bytes 49160 | tf_op jit(solution)/shard_map/ppermute | solution.py:86
  22.2 3.7 %collective-permute-start.7 = (bf16[16,512]{1,0:T(8,128)(2,1)S(1)}, bf16[16,512]{1,0:T(8,128)(2,1)S(1)}, u32[]{:S(2)}, u32[]{:S(2)}) collective-permute-start(bf16[16,512]{1,0:T(8,128)(2,1)S(1)} %add_convert_fusion.1), channel_id=1, source_target_pairs={{0,4},{2,6},{4,0},{6,2},{1,5},{3,7},{5,1},{7,3},{8,12},{10,14},{12... | collective-permute-start | bytes 49160 | tf_op jit(solution)/shard_map/ppermute | solution.py:86
  23.7 4.6 %collective-permute-start.8 = (bf16[16,512]{1,0:T(8,128)(2,1)S(1)}, bf16[16,512]{1,0:T(8,128)(2,1)S(1)}, u32[]{:S(2)}, u32[]{:S(2)}) collective-permute-start(bf16[16,512]{1,0:T(8,128)(2,1)S(1)} %add_convert_fusion.1), channel_id=1, source_target_pairs={{0,6},{2,4},{4,2},{6,0},{1,7},{3,5},{5,3},{7,1},{8,14},{10,12},{12... | collective-permute-start | bytes 49160 | tf_op jit(solution)/shard_map/ppermute | solution.py:86

commit v3 on v2

--- a/solution.py
+++ b/solution.py
@@ -12,6 +12,9 @@
 HD = 128
 PER = QH // KVH
 RADIX = 4
+GATHER = (2, 3, 1)
+SCATTER = (3, 2, 1)
+SUM = (3, 2, 1)
 LOG2E = 1.4426950408889634
 NT = (((1,), (1,)), ((), ()))
 NN = (((1,), (0,)), ((), ()))
@@ -47,15 +50,26 @@
     return pairs
 
 
+def in_order(count, order):
+    return [step for step in order if step < count] + list(range(len(order) + 1, count))
+
+
+def exchange(blocks, axis, size, stride, steps, sign):
+    count = len(steps) + 1
+    return [
+        lax.ppermute(block, axis, moved(size, stride, count, step, sign))
+        for block, step in zip(blocks, steps)
+    ]
+
+
 def gather_parts(x, axis, size):
     parts = [x]
     for stride, count in digits(size):
-        block = parts[0] if len(parts) == 1 else jnp.stack(parts)
-        out = list(parts)
-        for step in range(1, count):
-            got = lax.ppermute(block, axis, moved(size, stride, count, step, 1))
-            out += [got] if len(parts) == 1 else [got[i] for i in range(len(parts))]
-        parts = out
+        low = len(parts)
+        block = x if low == 1 else jnp.stack(parts)
+        steps = in_order(count, GATHER)
+        for got in exchange([block] * (count - 1), axis, size, stride, steps, 1):
+            parts += [got] if low == 1 else [got[i] for i in range(low)]
     return parts
 
 
@@ -66,24 +80,24 @@
 
 
 def scatter_sum(parts, axis, size):
+    parts, dtype = list(parts), parts[0].dtype
     for stride, count in reversed(digits(size)):
         low = len(parts) // count
-        terms = [parts[0].astype(jnp.float32) if low == 1 else jnp.stack(parts[:low]).astype(jnp.float32)]
-        for step in range(1, count):
-            piece = parts[step * low : (step + 1) * low]
-            block = piece[0] if low == 1 else jnp.stack(piece)
-            got = lax.ppermute(block, axis, moved(size, stride, count, step, -1))
-            terms.append(got.astype(jnp.float32))
-        total = tree_sum(terms).astype(parts[0].dtype)
+        blocks = parts if low == 1 else [
+            jnp.stack(parts[i * low : (i + 1) * low]) for i in range(count)
+        ]
+        found = dict(zip(in_order(count, GATHER), blocks[1:]))
+        steps = in_order(count, SCATTER)
+        terms = blocks[:1] + exchange([found[s] for s in steps], axis, size, stride, steps, -1)
+        total = tree_sum([t.astype(jnp.float32) for t in terms]).astype(dtype)
         parts = [total] if low == 1 else [total[i] for i in range(low)]
     return parts[0]
 
 
 def all_sum(x, axis, size):
     for stride, count in digits(size):
-        terms = [x]
-        for step in range(1, count):
-            terms.append(lax.ppermute(x, axis, moved(size, stride, count, step, 1)))
+        steps = in_order(count, SUM)
+        terms = [x] + exchange([x] * (count - 1), axis, size, stride, steps, 1)
         x = tree_sum([t.astype(jnp.float32) for t in terms]).astype(x.dtype)
     return x
 

time: 29.3 us -> 26.7 us (0.911)
  waiting for transfers between devices: 8.42 us -> 5.85 us
    ppermute x9, waiting for transfers between devices: 8.42 us -> 5.85 us  [exchange(): lax.ppermute(block, axis, moved(size, stride, count, step, sign))]
  transfers between devices with their start and end apart: 9 -> 9, of which waited for: 5 -> 5; matrix products, arithmetic and copies ran while one was open for 0% -> 0% of each run, Pallas kernels for 12% -> 14%
where the time goes in v3:
time: 26.7 us; the launch traced here: 26.4 us
  starting transfers between devices  13.7 us (51%)
  waiting for transfers between devices  5.85 us (22%)
  Pallas kernels  4.81 us (18%)
  local copies, waits for them, and re-layouts  1.32 us (5%)
  between operations  0.68 us (3%)
    ppermute x9, starting transfers between devices, exchange(): lax.ppermute(block, axis, moved(size, stride, count, step, sign))  13.7 us
    ppermute x9, waiting for transfers between devices, exchange(): lax.ppermute(block, axis, moved(size, stride, count, step, sign))  5.85 us
    pallas_call x1, Pallas kernels, body(): pl.pallas_call(tree_kernel, out_shape=[like(queries), like(out_grad), lik...  2.29 us
    pallas_call x1, Pallas kernels, body(): pl.pallas_call(functools.partial(branch_kernel, parts=groups), out_shape=...  1.28 us
    pallas_call x1, Pallas kernels, body(): pl.pallas_call(functools.partial(prefix_kernel, parts=groups), out_shape=...  1.23 us
    unnamed x7, local copies, waits for them, and re-layouts  0.72 us
    slice x1, local copies, waits for them, and re-layouts, body(): total[:, half:]  0.61 us
  transfers between devices with their start and end apart: 9, of which 5 were waited for; matrix products, arithmetic and copies ran while one was open for 0% of the time, Pallas kernels for 14%

profile of v3, /device:TPU:0, one launch (start us, length us, event | category | flops | bytes accessed | tf_op | source)
XLA Modules:
  0.0 26.4 jit_solution(14457800926562120674)
XLA Ops:
  0.6 0.0 copy-start.2
  0.6 0.7 %constant_dynamic-update-slice_fusion.1 = bf16[16,512]{1,0:T(8,128)(2,1)S(1)} fusion(bf16[16,256]{1,0:T(8,128)(2,1)} %param.11), kind=kLoop, calls=%fused_computation.3 | loop fusion | bytes 16384
  1.3 0.0 copy-done.2
  1.3 0.0 copy-start
  1.4 0.0 copy-start.1
  1.4 4.1 %collective-permute-start = (bf16[16,512]{1,0:T(8,128)(2,1)S(1)}, bf16[16,512]{1,0:T(8,128)(2,1)S(1)}, u32[]{:S(2)}, u32[]{:S(2)}) collective-permute-start(bf16[16,512]{1,0:T(8,128)(2,1)S(1)} %constant_dynamic-update-slice_fusion.refs_6_.refs_8_), channel_id=1, source_target_pairs={{0,16},{8,24},{16,0},{24,8},{1,17},{9,25},{17,1},{25,9},{2,18},{10... | collective-permute-start | bytes 49160 | tf_op jit(solution)/shard_map/ppermute | solution.py:60
  5.5 1.3 %collective-permute-start.1 = (bf16[16,512]{1,0:T(8,128)(2,1)S(1)}, bf16[16,512]{1,0:T(8,128)(2,1)S(1)}, u32[]{:S(2)}, u32[]{:S(2)}) collective-permute-start(bf16[16,512]{1,0:T(8,128)(2,1)S(1)} %constant_dynamic-update-slice_fusion.refs_6_.refs_8_), channel_id=1, source_target_pairs={{0,24},{8,16},{16,8},{24,0},{1,25},{9,17},{17,9},{25,1},{2,26},{10... | collective-permute-start | bytes 49160 | tf_op jit(solution)/shard_map/ppermute | solution.py:60
  6.8 0.2 collective-permute-start.2
  7.0 0.0 copy-done
  7.0 0.0 copy-done.1
  7.0 2.3 %tree.1 = (bf16[2,64,2048]{2,1,0:T(8,128)(2,1)S(1)}, bf16[2,64,2048]{2,1,0:T(8,128)(2,1)S(1)}, bf16[2,64,256]{2,1,0:T(8,128)(2,1)S(1)}, f32[4,64,512]{2,1,0:T(8,...) custom-call(bf16[2,64,2048]{2,1,0:T(8,128)(2,1)} %q_hbm.1, ...), custom_call_target="tpu_custom_call" | custom-call | flops 67108864 | bytes 1048576 | tf_op jit(solution)/shard_map/tree/pallas_call | solution.py:243
  9.3 0.0 collective-permute-done.refs_7_.refs_9_
  9.4 1.6 %collective-permute-done.1.refs_8_.refs_10_ = bf16[16,512]{1,0:T(8,128)(2,1)S(1)} collective-permute-done((bf16[16,512]{1,0:T(8,128)(2,1)S(1)}, bf16[16,512]{1,0:T(8,128)(2,1)S(1)}, u32[]{:S(2)}, u32[]{:S(2)}) %collective-permute-start.1) | collective-permute-done | bytes 16416 | tf_op jit(solution)/shard_map/ppermute | solution.py:60
  11.0 0.0 collective-permute-done.2.refs_9_.refs_11_
  11.0 1.2 %prefix.1 = (bf16[4,64,512]{2,1,0:T(8,128)(2,1)S(1)}, f32[4,1,512]{2,1,0:T(1,128)S(1)}, f32[4,1,512]{2,1,0:T(1,128)S(1)}, bf16[16,512]{1,0:T(8,128)(2,1)S(1)}, b...) custom-call(bf16[2,64,2048]{2,1,0:T(8,128)(2,1)S(1)} %get-tuple-element.24.refs_0_, ...), custom_call_target="tpu_custom_call" | custom-call | flops 134217728 | tf_op jit(solution)/shard_map/prefix/pallas_call | solution.py:258
  12.2 2.1 %collective-permute-start.3 = (bf16[16,512]{1,0:T(8,128)(2,1)S(1)}, bf16[16,512]{1,0:T(8,128)(2,1)S(1)}, u32[]{:S(2)}, u32[]{:S(2)}) collective-permute-start(bf16[16,512]{1,0:T(8,128)(2,1)S(1)} %get-tuple-element.40), channel_id=1, source_target_pairs={{0,24},{8,16},{16,8},{24,0},{1,25},{9,17},{17,9},{25,1},{2,26},{10... | collective-permute-start | bytes 49160 | tf_op jit(solution)/shard_map/ppermute | solution.py:60
  14.3 0.0 collective-permute-start.4
  14.3 2.4 %collective-permute-start.5 = (bf16[16,512]{1,0:T(8,128)(2,1)S(1)}, bf16[16,512]{1,0:T(8,128)(2,1)S(1)}, u32[]{:S(2)}, u32[]{:S(2)}) collective-permute-start(bf16[16,512]{1,0:T(8,128)(2,1)S(1)} %get-tuple-element.42), channel_id=1, source_target_pairs={{0,8},{8,0},{16,24},{24,16},{1,9},{9,1},{17,25},{25,17},{2,10},{10... | collective-permute-start | bytes 49160 | tf_op jit(solution)/shard_map/ppermute | solution.py:60
  16.7 1.1 %collective-permute-done.3 = bf16[16,512]{1,0:T(8,128)(2,1)S(1)} collective-permute-done((bf16[16,512]{1,0:T(8,128)(2,1)S(1)}, bf16[16,512]{1,0:T(8,128)(2,1)S(1)}, u32[]{:S(2)}, u32[]{:S(2)}) %collective-permute-start.3) | collective-permute-done | bytes 16416 | tf_op jit(solution)/shard_map/ppermute | solution.py:60
  17.8 1.1 %collective-permute-done.4 = bf16[16,512]{1,0:T(8,128)(2,1)S(1)} collective-permute-done((bf16[16,512]{1,0:T(8,128)(2,1)S(1)}, bf16[16,512]{1,0:T(8,128)(2,1)S(1)}, u32[]{:S(2)}, u32[]{:S(2)}) %collective-permute-start.4) | collective-permute-done | bytes 16416 | tf_op jit(solution)/shard_map/ppermute | solution.py:60
  19.0 0.0 collective-permute-done.5
  19.0 2.5 %collective-permute-start.6 = (bf16[16,512]{1,0:T(8,128)(2,1)S(1)}, bf16[16,512]{1,0:T(8,128)(2,1)S(1)}, u32[]{:S(2)}, u32[]{:S(2)}) collective-permute-start(bf16[16,512]{1,0:T(8,128)(2,1)S(1)} %add_convert_fusion.1), channel_id=1, source_target_pairs={{0,6},{2,4},{4,2},{6,0},{1,7},{3,5},{5,3},{7,1},{8,14},{10,12},{12... | collective-permute-start | bytes 49160 | tf_op jit(solution)/shard_map/ppermute | solution.py:60
  21.5 0.5 %collective-permute-start.7 = (bf16[16,512]{1,0:T(8,128)(2,1)S(1)}, bf16[16,512]{1,0:T(8,128)(2,1)S(1)}, u32[]{:S(2)}, u32[]{:S(2)}) collective-permute-start(bf16[16,512]{1,0:T(8,128)(2,1)S(1)} %add_convert_fusion.1), channel_id=1, source_target_pairs={{0,4},{2,6},{4,0},{6,2},{1,5},{3,7},{5,1},{7,3},{8,12},{10,14},{12... | collective-permute-start | bytes 49160 | tf_op jit(solution)/shard_map/ppermute | solution.py:60
  22.0 0.5 %collective-permute-start.8 = (bf16[16,512]{1,0:T(8,128)(2,1)S(1)}, bf16[16,512]{1,0:T(8,128)(2,1)S(1)}, u32[]{:S(2)}, u32[]{:S(2)}) collective-permute-start(bf16[16,512]{1,0:T(8,128)(2,1)S(1)} %add_convert_fusion.1), channel_id=1, source_target_pairs={{0,2},{2,0},{4,6},{6,4},{1,3},{3,1},{5,7},{7,5},{8,10},{10,8},{12,... | collective-permute-start | bytes 49160 | tf_op jit(solution)/shard_map/ppermute | solution.py:60
  22.5 1.3 %branch.1 = (bf16[2,64,2048]{2,1,0:T(8,128)(2,1)}, bf16[2,64,256]{2,1,0:T(8,128)(2,1)}, bf16[2,64,256]{2,1,0:T(8,128)(2,1)}) custom-call(bf16[2,64,2048]{2,1,0:T(8,128)(2,1)S(1)} %get-tuple-element.24.refs_0_, bf16[2,64,2048]{2,1,0:T(8,128)(2,1)S(1)} %get-tuple-element.25.refs_1_, bf16[2,64,256]{2,1,0:T(8,128)(2,1)S(1)} %get-tuple-element.26.refs_2_, ...), custom_call_target="tpu_custom_call" | custom-call | flops 134217728 | bytes 524288 | tf_op jit(solution)/shard_map/branch/pallas_call | solution.py:272
  23.8 0.0 collective-permute-done.6
  23.8 1.4 %collective-permute-done.7 = bf16[16,512]{1,0:T(8,128)(2,1)S(1)} collective-permute-done((bf16[16,512]{1,0:T(8,128)(2,1)S(1)}, bf16[16,512]{1,0:T(8,128)(2,1)S(1)}, u32[]{:S(2)}, u32[]{:S(2)}) %collective-permute-start.7) | collective-permute-done | bytes 16416 | tf_op jit(solution)/shard_map/ppermute | solution.py:60
  25.2 0.5 %collective-permute-done.8 = bf16[16,512]{1,0:T(8,128)(2,1)S(1)} collective-permute-done((bf16[16,512]{1,0:T(8,128)(2,1)S(1)}, bf16[16,512]{1,0:T(8,128)(2,1)S(1)}, u32[]{:S(2)}, u32[]{:S(2)}) %collective-permute-start.8) | collective-permute-done | bytes 16416 | tf_op jit(solution)/shard_map/ppermute | solution.py:60
  25.8 0.6 %fusion = (bf16[16,256]{1,0:T(8,128)(2,1)}, bf16[16,256]{1,0:T(8,128)(2,1)}) fusion(bf16[16,512]{1,0:T(8,128)(2,1)S(1)} %add_convert_fusion), kind=kLoop, calls=%fused_computation.4 | loop fusion | bytes 32768 | tf_op jit(solution)/shard_map/slice | solution.py:286
  (3 shorter events, 0.0 us)
Async XLA Ops:
  0.6 0.7 %copy-start.2 = (bf16[16,256]{1,0:T(8,128)(2,1)S(1)}, bf16[16,256]{1,0:T(8,128)(2,1)}, u32[]{:S(2)}) copy-start(bf16[16,256]{1,0:T(8,128)(2,1)} %param.12) | copy-start | bytes 24580
  1.3 5.7 %copy-start = (s32[2,64]{1,0:T(2,128)S(1)}, s32[2,64]{1,0:T(2,128)}, u32[]{:S(2)}) copy-start(s32[2,64]{1,0:T(2,128)} %par_ref.1) | copy-start | bytes 1540
  1.4 5.7 %copy-start.1 = (s32[2]{0:T(128)S(1)}, s32[2]{0:T(128)}, u32[]{:S(2)}) copy-start(s32[2]{0:T(128)} %len_ref.1) | copy-start | bytes 28
  1.4 8.0 %collective-permute-start = (bf16[16,512]{1,0:T(8,128)(2,1)S(1)}, bf16[16,512]{1,0:T(8,128)(2,1)S(1)}, u32[]{:S(2)}, u32[]{:S(2)}) collective-permute-start(bf16[16,512]{1,0:T(8,128)(2,1)S(1)} %constant_dynamic-update-slice_fusion.refs_6_.refs_8_), channel_id=1, source_target_pairs={{0,16},{8,24},{16,0},{24,8},{1,17},{9,25},{17,1},{25,9},{2,18},{10... | collective-permute-start | bytes 49160 | tf_op jit(solution)/shard_map/ppermute | solution.py:60
  5.5 5.5 %collective-permute-start.1 = (bf16[16,512]{1,0:T(8,128)(2,1)S(1)}, bf16[16,512]{1,0:T(8,128)(2,1)S(1)}, u32[]{:S(2)}, u32[]{:S(2)}) collective-permute-start(bf16[16,512]{1,0:T(8,128)(2,1)S(1)} %constant_dynamic-update-slice_fusion.refs_6_.refs_8_), channel_id=1, source_target_pairs={{0,24},{8,16},{16,8},{24,0},{1,25},{9,17},{17,9},{25,1},{2,26},{10... | collective-permute-start | bytes 49160 | tf_op jit(solution)/shard_map/ppermute | solution.py:60
  6.8 4.2 %collective-permute-start.2 = (bf16[16,512]{1,0:T(8,128)(2,1)S(1)}, bf16[16,512]{1,0:T(8,128)(2,1)S(1)}, u32[]{:S(2)}, u32[]{:S(2)}) collective-permute-start(bf16[16,512]{1,0:T(8,128)(2,1)S(1)} %constant_dynamic-update-slice_fusion.refs_6_.refs_8_), channel_id=1, source_target_pairs={{0,8},{8,0},{16,24},{24,16},{1,9},{9,1},{17,25},{25,17},{2,10},{10... | collective-permute-start | bytes 49160 | tf_op jit(solution)/shard_map/ppermute | solution.py:60
  12.2 5.6 %collective-permute-start.3 = (bf16[16,512]{1,0:T(8,128)(2,1)S(1)}, bf16[16,512]{1,0:T(8,128)(2,1)S(1)}, u32[]{:S(2)}, u32[]{:S(2)}) collective-permute-start(bf16[16,512]{1,0:T(8,128)(2,1)S(1)} %get-tuple-element.40), channel_id=1, source_target_pairs={{0,24},{8,16},{16,8},{24,0},{1,25},{9,17},{17,9},{25,1},{2,26},{10... | collective-permute-start | bytes 49160 | tf_op jit(solution)/shard_map/ppermute | solution.py:60
  14.3 4.6 %collective-permute-start.4 = (bf16[16,512]{1,0:T(8,128)(2,1)S(1)}, bf16[16,512]{1,0:T(8,128)(2,1)S(1)}, u32[]{:S(2)}, u32[]{:S(2)}) collective-permute-start(bf16[16,512]{1,0:T(8,128)(2,1)S(1)} %get-tuple-element.41), channel_id=1, source_target_pairs={{0,16},{8,24},{16,0},{24,8},{1,17},{9,25},{17,1},{25,9},{2,18},{10... | collective-permute-start | bytes 49160 | tf_op jit(solution)/shard_map/ppermute | solution.py:60
  14.3 4.6 %collective-permute-start.5 = (bf16[16,512]{1,0:T(8,128)(2,1)S(1)}, bf16[16,512]{1,0:T(8,128)(2,1)S(1)}, u32[]{:S(2)}, u32[]{:S(2)}) collective-permute-start(bf16[16,512]{1,0:T(8,128)(2,1)S(1)} %get-tuple-element.42), channel_id=1, source_target_pairs={{0,8},{8,0},{16,24},{24,16},{1,9},{9,1},{17,25},{25,17},{2,10},{10... | collective-permute-start | bytes 49160 | tf_op jit(solution)/shard_map/ppermute | solution.py:60
  19.0 4.8 %collective-permute-start.6 = (bf16[16,512]{1,0:T(8,128)(2,1)S(1)}, bf16[16,512]{1,0:T(8,128)(2,1)S(1)}, u32[]{:S(2)}, u32[]{:S(2)}) collective-permute-start(bf16[16,512]{1,0:T(8,128)(2,1)S(1)} %add_convert_fusion.1), channel_id=1, source_target_pairs={{0,6},{2,4},{4,2},{6,0},{1,7},{3,5},{5,3},{7,1},{8,14},{10,12},{12... | collective-permute-start | bytes 49160 | tf_op jit(solution)/shard_map/ppermute | solution.py:60
  21.5 3.7 %collective-permute-start.7 = (bf16[16,512]{1,0:T(8,128)(2,1)S(1)}, bf16[16,512]{1,0:T(8,128)(2,1)S(1)}, u32[]{:S(2)}, u32[]{:S(2)}) collective-permute-start(bf16[16,512]{1,0:T(8,128)(2,1)S(1)} %add_convert_fusion.1), channel_id=1, source_target_pairs={{0,4},{2,6},{4,0},{6,2},{1,5},{3,7},{5,1},{7,3},{8,12},{10,14},{12... | collective-permute-start | bytes 49160 | tf_op jit(solution)/shard_map/ppermute | solution.py:60
  22.0 3.7 %collective-permute-start.8 = (bf16[16,512]{1,0:T(8,128)(2,1)S(1)}, bf16[16,512]{1,0:T(8,128)(2,1)S(1)}, u32[]{:S(2)}, u32[]{:S(2)}) collective-permute-start(bf16[16,512]{1,0:T(8,128)(2,1)S(1)} %add_convert_fusion.1), channel_id=1, source_target_pairs={{0,2},{2,0},{4,6},{6,4},{1,3},{3,1},{5,7},{7,5},{8,10},{10,8},{12,... | collective-permute-start | bytes 49160 | tf_op jit(solution)/shard_map/ppermute | solution.py:60

commit v4 on v3

--- a/solution.py
+++ b/solution.py
@@ -12,7 +12,7 @@
 HD = 128
 PER = QH // KVH
 RADIX = 4
-GATHER = (2, 3, 1)
+GATHER = (3, 2, 1)
 SCATTER = (3, 2, 1)
 SUM = (3, 2, 1)
 LOG2E = 1.4426950408889634
@@ -114,7 +114,10 @@
 ):
     count, length, _ = q_ref.shape
     heads = bk_ref.shape[2] // HD
-    pairs = ((q_hbm, q_ref), (g_hbm, g_ref), (bk_hbm, bk_ref), (bv_hbm, bv_ref))
+    pairs = [(q_hbm.at[0], q_ref.at[0]), (g_hbm.at[0], g_ref.at[0])]
+    pairs += [(bk_hbm, bk_ref), (bv_hbm, bv_ref)]
+    for b in range(1, count):
+        pairs += [(q_hbm.at[b], q_ref.at[b]), (g_hbm.at[b], g_ref.at[b])]
     copies = [pltpu.make_async_copy(s, d, sems.at[i]) for i, (s, d) in enumerate(pairs)]
     for copy in copies:
         copy.start()
@@ -128,21 +131,25 @@
         reaches = [jnp.minimum(dot(r, r, NN), 1.0).astype(jnp.bfloat16) for r in reaches]
     masks = [jnp.concatenate([r.astype(jnp.float32)] * PER, axis=1) > 0.5 for r in reaches]
     place = lax.broadcasted_iota(jnp.int32, (1, PER * length), 1) % length
-    lives = [(place < len_ref[b]).astype(jnp.float32) for b in range(count)]
-    for copy in copies:
-        copy.wait()
-    for h in range(heads):
-        low = h * HD
-        for b in range(count):
+    for b in range(count):
+        for copy in copies[2 * b + 2 if b else 0 : 2 * b + 4]:
+            copy.wait()
+        stage = []
+        for h in range(heads):
+            cols = slice(h * HD, (h + 1) * HD)
+            stage.append((
+                dot(bk_ref[b, :, cols], head_rows(q_ref, b, h), NT),
+                dot(bv_ref[b, :, cols], head_rows(g_ref, b, h), NT),
+            ))
+        live = (place < len_ref[:, b : b + 1]).astype(jnp.float32)
+        for h, (scores, dweights) in enumerate(stage):
             i = h * count + b
-            scores = dot(bk_ref[b, :, low : low + HD], head_rows(q_ref, b, h), NT)
-            dweights = dot(bv_ref[b, :, low : low + HD], head_rows(g_ref, b, h), NT)
             scores = jnp.where(masks[b], scores * (HD**-0.5 * LOG2E), -1e30)
             top = jnp.max(scores, axis=0, keepdims=True)
             powers = jnp.exp2(scores - top)
             power_ref[i] = powers
             dweight_ref[i] = dweights
-            live_ref[i] = lives[b]
+            live_ref[i] = live
             max_ref[i] = top
             sum_ref[i] = jnp.sum(powers, axis=0, keepdims=True)
             dot_ref[i] = jnp.sum(powers * dweights, axis=0, keepdims=True)
@@ -159,32 +166,37 @@
     heads = width // HD
     factor = HD**-0.5
     pre = jnp.concatenate([r[...] for r in pre_refs], axis=0)
+    stage = []
     for h in range(heads):
         low = h * HD
         keys = pre[:, low : low + HD]
         values = pre[:, width + low : width + low + HD]
+        for b in range(count):
+            q = head_rows(q_ref, b, h)
+            g = head_rows(g_ref, b, h)
+            stage.append((q, g, dot(keys, q, NT), dot(values, g, NT)))
+    ready = []
+    for i, (q, g, scores, dweights) in enumerate(stage):
+        scores = scores * (factor * LOG2E)
+        tree_max = max_ref[i]
+        top = jnp.maximum(jnp.max(scores, axis=0, keepdims=True), tree_max)
+        powers = jnp.exp2(scores - top)
+        tree = jnp.exp2(tree_max - top)
+        scale = live_ref[i] / (jnp.sum(powers, axis=0, keepdims=True) + tree * sum_ref[i])
+        delta = scale * (jnp.sum(powers * dweights, axis=0, keepdims=True) + tree * dot_ref[i])
+        weights = powers * scale
+        dscores = (weights * (dweights - delta)).astype(jnp.bfloat16)
+        dscore_ref[i] = dscores
+        scale_ref[i] = scale * tree
+        delta_ref[i] = delta
+        ready.append((weights.astype(jnp.bfloat16), dscores))
+    for h in range(heads):
+        low = h * HD
         key_sum = value_sum = None
         for b in range(count):
             i = h * count + b
-            q = head_rows(q_ref, b, h)
-            g = head_rows(g_ref, b, h)
-            scores = dot(keys, q, NT) * (factor * LOG2E)
-            dweights = dot(values, g, NT)
-            tree_max = max_ref[i]
-            top = jnp.maximum(jnp.max(scores, axis=0, keepdims=True), tree_max)
-            powers = jnp.exp2(scores - top)
-            tree = jnp.exp2(tree_max - top)
-            scale = live_ref[i] / (jnp.sum(powers, axis=0, keepdims=True) + tree * sum_ref[i])
-            delta = scale * (
-                jnp.sum(powers * dweights, axis=0, keepdims=True) + tree * dot_ref[i]
-            )
-            weights = powers * scale
-            dscores = (weights * (dweights - delta)).astype(jnp.bfloat16)
-            value_grad = dot(weights.astype(jnp.bfloat16), g, NN)
-            key_grad = dot(dscores, q, NN) * factor
-            dscore_ref[i] = dscores
-            scale_ref[i] = scale * tree
-            delta_ref[i] = delta
+            value_grad = dot(ready[i][0], stage[i][1], NN)
+            key_grad = dot(ready[i][1], stage[i][0], NN) * factor
             key_sum = key_grad if b == 0 else key_sum + key_grad
             value_sum = value_grad if b == 0 else value_sum + value_grad
         for i, ref in enumerate(out_refs):
@@ -231,7 +243,6 @@
     packed = jnp.concatenate([prefix_keys, prefix_values], axis=1)
     parts = gather_parts(packed, "group", groups)
     vmem = pl.BlockSpec(memory_space=pltpu.VMEM)
-    smem = pl.BlockSpec(memory_space=pltpu.SMEM)
     anywhere = pl.BlockSpec(memory_space=pltpu.HBM)
     hbm = lambda x: pltpu.with_memory_space_constraint(x, pltpu.HBM)
     params = pltpu.CompilerParams(vmem_limit_bytes=16 * 1024 * 1024)
@@ -243,18 +254,18 @@
     q, g, keys, powers, dweights, tops, sums, dots, live = pl.pallas_call(
         tree_kernel,
         out_shape=[like(queries), like(out_grad), like(branch_keys), block, block, row, row, row, row],
-        in_specs=[anywhere] * 4 + [vmem, smem],
+        in_specs=[anywhere] * 4 + [vmem] * 2,
         out_specs=[vmem] * 9,
         scratch_shapes=[
             pltpu.VMEM(branch_values.shape, branch_values.dtype),
-            pltpu.SemaphoreType.DMA((4,)),
+            pltpu.SemaphoreType.DMA((2 + 2 * count,)),
         ],
         compiler_params=params,
         cost_estimate=pl.CostEstimate(
             flops=2 * work * length, bytes_accessed=2 * queries.size * 2, transcendentals=wide * length * 4
         ),
         name="tree",
-    )(*(hbm(x) for x in (queries, out_grad, branch_keys, branch_values)), parents, lengths)
+    )(*(hbm(x) for x in (queries, out_grad, branch_keys, branch_values)), parents, lengths.reshape(1, count))
     outs = pl.pallas_call(
         functools.partial(prefix_kernel, parts=groups),
         out_shape=[

time: 26.7 us -> 25.9 us (0.970)
  Pallas kernels: 4.81 us -> 3.81 us
    pallas_call x1, Pallas kernels: 2.29 us -> 1.74 us  [body(): pl.pallas_call(tree_kernel, out_shape=[like(queries), like(out_grad), lik...]
    pallas_call x1, Pallas kernels: 1.23 us -> 0.79 us  [body(): pl.pallas_call(functools.partial(prefix_kernel, parts=groups), out_shape=...]
  transfers between devices with their start and end apart: 9 -> 9, of which waited for: 5 -> 5; matrix products, arithmetic and copies ran while one was open for 0% -> 0% of each run, Pallas kernels for 14% -> 12%
where the time goes in v4:
time: 25.9 us; the launch traced here: 25.7 us
  starting transfers between devices  13.8 us (53%)
  waiting for transfers between devices  6.05 us (23%)
  Pallas kernels  3.81 us (15%)
  local copies, waits for them, and re-layouts  1.32 us (5%)
  between operations  0.69 us (3%)
    ppermute x9, starting transfers between devices, exchange(): lax.ppermute(block, axis, moved(size, stride, count, step, sign))  13.8 us
    ppermute x9, waiting for transfers between devices, exchange(): lax.ppermute(block, axis, moved(size, stride, count, step, sign))  6.05 us
    pallas_call x1, Pallas kernels, body(): pl.pallas_call(tree_kernel, out_shape=[like(queries), like(out_grad), lik...  1.74 us
    pallas_call x1, Pallas kernels, body(): pl.pallas_call(functools.partial(branch_kernel, parts=groups), out_shape=...  1.28 us
    pallas_call x1, Pallas kernels, body(): pl.pallas_call(functools.partial(prefix_kernel, parts=groups), out_shape=...  0.79 us
    unnamed x7, local copies, waits for them, and re-layouts  0.72 us
    slice x1, local copies, waits for them, and re-layouts, body(): total[:, half:]  0.61 us
  transfers between devices with their start and end apart: 9, of which 5 were waited for; matrix products, arithmetic and copies ran while one was open for 0% of the time, Pallas kernels for 12%

profile of v4, /device:TPU:0, one launch (start us, length us, event | category | flops | bytes accessed | tf_op | source)
XLA Modules:
  0.0 25.7 jit_solution(18348688272721516019)
XLA Ops:
  0.6 0.0 copy-start.2
  0.6 0.7 %constant_dynamic-update-slice_fusion.1 = bf16[16,512]{1,0:T(8,128)(2,1)S(1)} fusion(bf16[16,256]{1,0:T(8,128)(2,1)} %param.11), kind=kLoop, calls=%fused_computation.3 | loop fusion | bytes 16384
  1.3 0.0 copy-done.2
  1.4 0.0 copy-start
  1.4 0.0 copy-start.1
  1.4 5.1 %collective-permute-start = (bf16[16,512]{1,0:T(8,128)(2,1)S(1)}, bf16[16,512]{1,0:T(8,128)(2,1)S(1)}, u32[]{:S(2)}, u32[]{:S(2)}) collective-permute-start(bf16[16,512]{1,0:T(8,128)(2,1)S(1)} %constant_dynamic-update-slice_fusion.refs_6_.refs_8_), channel_id=1, source_target_pairs={{0,24},{8,16},{16,8},{24,0},{1,25},{9,17},{17,9},{25,1},{2,26},{10... | collective-permute-start | bytes 49160 | tf_op jit(solution)/shard_map/ppermute | solution.py:60
  6.5 0.0 collective-permute-start.1
  6.5 0.6 %collective-permute-start.2 = (bf16[16,512]{1,0:T(8,128)(2,1)S(1)}, bf16[16,512]{1,0:T(8,128)(2,1)S(1)}, u32[]{:S(2)}, u32[]{:S(2)}) collective-permute-start(bf16[16,512]{1,0:T(8,128)(2,1)S(1)} %constant_dynamic-update-slice_fusion.refs_6_.refs_8_), channel_id=1, source_target_pairs={{0,8},{8,0},{16,24},{24,16},{1,9},{9,1},{17,25},{25,17},{2,10},{10... | collective-permute-start | bytes 49160 | tf_op jit(solution)/shard_map/ppermute | solution.py:60
  7.1 0.0 copy-done
  7.1 0.0 copy-done.1
  7.1 1.7 %tree.1 = (bf16[2,64,2048]{2,1,0:T(8,128)(2,1)S(1)}, bf16[2,64,2048]{2,1,0:T(8,128)(2,1)S(1)}, bf16[2,64,256]{2,1,0:T(8,128)(2,1)S(1)}, f32[4,64,512]{2,1,0:T(8,...) custom-call(bf16[2,64,2048]{2,1,0:T(8,128)(2,1)} %q_hbm.1, ...), custom_call_target="tpu_custom_call" | custom-call | flops 67108864 | bytes 1048576 | tf_op jit(solution)/shard_map/tree/pallas_call | solution.py:254
  8.9 0.0 collective-permute-done.refs_7_.refs_9_
  8.9 2.2 %collective-permute-done.1.refs_8_.refs_10_ = bf16[16,512]{1,0:T(8,128)(2,1)S(1)} collective-permute-done((bf16[16,512]{1,0:T(8,128)(2,1)S(1)}, bf16[16,512]{1,0:T(8,128)(2,1)S(1)}, u32[]{:S(2)}, u32[]{:S(2)}) %collective-permute-start.1) | collective-permute-done | bytes 16416 | tf_op jit(solution)/shard_map/ppermute | solution.py:60
  11.1 0.0 collective-permute-done.2.refs_9_.refs_11_
  11.1 0.8 %prefix.1 = (bf16[4,64,512]{2,1,0:T(8,128)(2,1)S(1)}, f32[4,1,512]{2,1,0:T(1,128)S(1)}, f32[4,1,512]{2,1,0:T(1,128)S(1)}, bf16[16,512]{1,0:T(8,128)(2,1)S(1)}, b...) custom-call(bf16[2,64,2048]{2,1,0:T(8,128)(2,1)S(1)} %get-tuple-element.24.refs_0_, ...), custom_call_target="tpu_custom_call" | custom-call | flops 134217728 | tf_op jit(solution)/shard_map/prefix/pallas_call | solution.py:269
  11.9 1.6 %collective-permute-start.3 = (bf16[16,512]{1,0:T(8,128)(2,1)S(1)}, bf16[16,512]{1,0:T(8,128)(2,1)S(1)}, u32[]{:S(2)}, u32[]{:S(2)}) collective-permute-start(bf16[16,512]{1,0:T(8,128)(2,1)S(1)} %get-tuple-element.40), channel_id=1, source_target_pairs={{0,24},{8,16},{16,8},{24,0},{1,25},{9,17},{17,9},{25,1},{2,26},{10... | collective-permute-start | bytes 49160 | tf_op jit(solution)/shard_map/ppermute | solution.py:60
  13.5 0.6 %collective-permute-start.4 = (bf16[16,512]{1,0:T(8,128)(2,1)S(1)}, bf16[16,512]{1,0:T(8,128)(2,1)S(1)}, u32[]{:S(2)}, u32[]{:S(2)}) collective-permute-start(bf16[16,512]{1,0:T(8,128)(2,1)S(1)} %get-tuple-element.41), channel_id=1, source_target_pairs={{0,16},{8,24},{16,0},{24,8},{1,17},{9,25},{17,1},{25,9},{2,18},{10... | collective-permute-start | bytes 49160 | tf_op jit(solution)/shard_map/ppermute | solution.py:60
  14.1 2.3 %collective-permute-start.5 = (bf16[16,512]{1,0:T(8,128)(2,1)S(1)}, bf16[16,512]{1,0:T(8,128)(2,1)S(1)}, u32[]{:S(2)}, u32[]{:S(2)}) collective-permute-start(bf16[16,512]{1,0:T(8,128)(2,1)S(1)} %get-tuple-element.42), channel_id=1, source_target_pairs={{0,8},{8,0},{16,24},{24,16},{1,9},{9,1},{17,25},{25,17},{2,10},{10... | collective-permute-start | bytes 49160 | tf_op jit(solution)/shard_map/ppermute | solution.py:60
  16.4 1.1 %collective-permute-done.3 = bf16[16,512]{1,0:T(8,128)(2,1)S(1)} collective-permute-done((bf16[16,512]{1,0:T(8,128)(2,1)S(1)}, bf16[16,512]{1,0:T(8,128)(2,1)S(1)}, u32[]{:S(2)}, u32[]{:S(2)}) %collective-permute-start.3) | collective-permute-done | bytes 16416 | tf_op jit(solution)/shard_map/ppermute | solution.py:60
  17.5 0.7 %collective-permute-done.4 = bf16[16,512]{1,0:T(8,128)(2,1)S(1)} collective-permute-done((bf16[16,512]{1,0:T(8,128)(2,1)S(1)}, bf16[16,512]{1,0:T(8,128)(2,1)S(1)}, u32[]{:S(2)}, u32[]{:S(2)}) %collective-permute-start.4) | collective-permute-done | bytes 16416 | tf_op jit(solution)/shard_map/ppermute | solution.py:60
  18.3 0.0 collective-permute-done.5
  18.3 2.5 %collective-permute-start.6 = (bf16[16,512]{1,0:T(8,128)(2,1)S(1)}, bf16[16,512]{1,0:T(8,128)(2,1)S(1)}, u32[]{:S(2)}, u32[]{:S(2)}) collective-permute-start(bf16[16,512]{1,0:T(8,128)(2,1)S(1)} %add_convert_fusion.1), channel_id=1, source_target_pairs={{0,6},{2,4},{4,2},{6,0},{1,7},{3,5},{5,3},{7,1},{8,14},{10,12},{12... | collective-permute-start | bytes 49160 | tf_op jit(solution)/shard_map/ppermute | solution.py:60
  20.8 0.5 %collective-permute-start.7 = (bf16[16,512]{1,0:T(8,128)(2,1)S(1)}, bf16[16,512]{1,0:T(8,128)(2,1)S(1)}, u32[]{:S(2)}, u32[]{:S(2)}) collective-permute-start(bf16[16,512]{1,0:T(8,128)(2,1)S(1)} %add_convert_fusion.1), channel_id=1, source_target_pairs={{0,4},{2,6},{4,0},{6,2},{1,5},{3,7},{5,1},{7,3},{8,12},{10,14},{12... | collective-permute-start | bytes 49160 | tf_op jit(solution)/shard_map/ppermute | solution.py:60
  21.3 0.5 %collective-permute-start.8 = (bf16[16,512]{1,0:T(8,128)(2,1)S(1)}, bf16[16,512]{1,0:T(8,128)(2,1)S(1)}, u32[]{:S(2)}, u32[]{:S(2)}) collective-permute-start(bf16[16,512]{1,0:T(8,128)(2,1)S(1)} %add_convert_fusion.1), channel_id=1, source_target_pairs={{0,2},{2,0},{4,6},{6,4},{1,3},{3,1},{5,7},{7,5},{8,10},{10,8},{12,... | collective-permute-start | bytes 49160 | tf_op jit(solution)/shard_map/ppermute | solution.py:60
  21.8 1.3 %branch.1 = (bf16[2,64,2048]{2,1,0:T(8,128)(2,1)}, bf16[2,64,256]{2,1,0:T(8,128)(2,1)}, bf16[2,64,256]{2,1,0:T(8,128)(2,1)}) custom-call(bf16[2,64,2048]{2,1,0:T(8,128)(2,1)S(1)} %get-tuple-element.24.refs_0_, bf16[2,64,2048]{2,1,0:T(8,128)(2,1)S(1)} %get-tuple-element.25.refs_1_, bf16[2,64,256]{2,1,0:T(8,128)(2,1)S(1)} %get-tuple-element.26.refs_2_, ...), custom_call_target="tpu_custom_call" | custom-call | flops 134217728 | bytes 524288 | tf_op jit(solution)/shard_map/branch/pallas_call | solution.py:283
  23.1 0.0 collective-permute-done.6
  23.1 1.4 %collective-permute-done.7 = bf16[16,512]{1,0:T(8,128)(2,1)S(1)} collective-permute-done((bf16[16,512]{1,0:T(8,128)(2,1)S(1)}, bf16[16,512]{1,0:T(8,128)(2,1)S(1)}, u32[]{:S(2)}, u32[]{:S(2)}) %collective-permute-start.7) | collective-permute-done | bytes 16416 | tf_op jit(solution)/shard_map/ppermute | solution.py:60
  24.5 0.5 %collective-permute-done.8 = bf16[16,512]{1,0:T(8,128)(2,1)S(1)} collective-permute-done((bf16[16,512]{1,0:T(8,128)(2,1)S(1)}, bf16[16,512]{1,0:T(8,128)(2,1)S(1)}, u32[]{:S(2)}, u32[]{:S(2)}) %collective-permute-start.8) | collective-permute-done | bytes 16416 | tf_op jit(solution)/shard_map/ppermute | solution.py:60
  25.1 0.6 %fusion = (bf16[16,256]{1,0:T(8,128)(2,1)}, bf16[16,256]{1,0:T(8,128)(2,1)}) fusion(bf16[16,512]{1,0:T(8,128)(2,1)S(1)} %add_convert_fusion), kind=kLoop, calls=%fused_computation.4 | loop fusion | bytes 32768 | tf_op jit(solution)/shard_map/slice | solution.py:297
  (3 shorter events, 0.0 us)
Async XLA Ops:
  0.6 0.7 %copy-start.2 = (bf16[16,256]{1,0:T(8,128)(2,1)S(1)}, bf16[16,256]{1,0:T(8,128)(2,1)}, u32[]{:S(2)}) copy-start(bf16[16,256]{1,0:T(8,128)(2,1)} %param.12) | copy-start | bytes 24580
  1.4 5.8 %copy-start = (s32[2,64]{1,0:T(2,128)S(1)}, s32[2,64]{1,0:T(2,128)}, u32[]{:S(2)}) copy-start(s32[2,64]{1,0:T(2,128)} %par_ref.1) | copy-start | bytes 1540
  1.4 5.8 %copy-start.1 = (s32[2]{0:T(128)S(1)}, s32[2]{0:T(128)}, u32[]{:S(2)}) copy-start(s32[2]{0:T(128)} %param.15) | copy-start | bytes 28
  1.4 7.5 %collective-permute-start = (bf16[16,512]{1,0:T(8,128)(2,1)S(1)}, bf16[16,512]{1,0:T(8,128)(2,1)S(1)}, u32[]{:S(2)}, u32[]{:S(2)}) collective-permute-start(bf16[16,512]{1,0:T(8,128)(2,1)S(1)} %constant_dynamic-update-slice_fusion.refs_6_.refs_8_), channel_id=1, source_target_pairs={{0,24},{8,16},{16,8},{24,0},{1,25},{9,17},{17,9},{25,1},{2,26},{10... | collective-permute-start | bytes 49160 | tf_op jit(solution)/shard_map/ppermute | solution.py:60
  6.5 4.6 %collective-permute-start.1 = (bf16[16,512]{1,0:T(8,128)(2,1)S(1)}, bf16[16,512]{1,0:T(8,128)(2,1)S(1)}, u32[]{:S(2)}, u32[]{:S(2)}) collective-permute-start(bf16[16,512]{1,0:T(8,128)(2,1)S(1)} %constant_dynamic-update-slice_fusion.refs_6_.refs_8_), channel_id=1, source_target_pairs={{0,16},{8,24},{16,0},{24,8},{1,17},{9,25},{17,1},{25,9},{2,18},{10... | collective-permute-start | bytes 49160 | tf_op jit(solution)/shard_map/ppermute | solution.py:60
  6.5 4.6 %collective-permute-start.2 = (bf16[16,512]{1,0:T(8,128)(2,1)S(1)}, bf16[16,512]{1,0:T(8,128)(2,1)S(1)}, u32[]{:S(2)}, u32[]{:S(2)}) collective-permute-start(bf16[16,512]{1,0:T(8,128)(2,1)S(1)} %constant_dynamic-update-slice_fusion.refs_6_.refs_8_), channel_id=1, source_target_pairs={{0,8},{8,0},{16,24},{24,16},{1,9},{9,1},{17,25},{25,17},{2,10},{10... | collective-permute-start | bytes 49160 | tf_op jit(solution)/shard_map/ppermute | solution.py:60
  11.9 5.6 %collective-permute-start.3 = (bf16[16,512]{1,0:T(8,128)(2,1)S(1)}, bf16[16,512]{1,0:T(8,128)(2,1)S(1)}, u32[]{:S(2)}, u32[]{:S(2)}) collective-permute-start(bf16[16,512]{1,0:T(8,128)(2,1)S(1)} %get-tuple-element.40), channel_id=1, source_target_pairs={{0,24},{8,16},{16,8},{24,0},{1,25},{9,17},{17,9},{25,1},{2,26},{10... | collective-permute-start | bytes 49160 | tf_op jit(solution)/shard_map/ppermute | solution.py:60
  13.5 4.7 %collective-permute-start.4 = (bf16[16,512]{1,0:T(8,128)(2,1)S(1)}, bf16[16,512]{1,0:T(8,128)(2,1)S(1)}, u32[]{:S(2)}, u32[]{:S(2)}) collective-permute-start(bf16[16,512]{1,0:T(8,128)(2,1)S(1)} %get-tuple-element.41), channel_id=1, source_target_pairs={{0,16},{8,24},{16,0},{24,8},{1,17},{9,25},{17,1},{25,9},{2,18},{10... | collective-permute-start | bytes 49160 | tf_op jit(solution)/shard_map/ppermute | solution.py:60
  14.1 4.2 %collective-permute-start.5 = (bf16[16,512]{1,0:T(8,128)(2,1)S(1)}, bf16[16,512]{1,0:T(8,128)(2,1)S(1)}, u32[]{:S(2)}, u32[]{:S(2)}) collective-permute-start(bf16[16,512]{1,0:T(8,128)(2,1)S(1)} %get-tuple-element.42), channel_id=1, source_target_pairs={{0,8},{8,0},{16,24},{24,16},{1,9},{9,1},{17,25},{25,17},{2,10},{10... | collective-permute-start | bytes 49160 | tf_op jit(solution)/shard_map/ppermute | solution.py:60
  18.3 4.8 %collective-permute-start.6 = (bf16[16,512]{1,0:T(8,128)(2,1)S(1)}, bf16[16,512]{1,0:T(8,128)(2,1)S(1)}, u32[]{:S(2)}, u32[]{:S(2)}) collective-permute-start(bf16[16,512]{1,0:T(8,128)(2,1)S(1)} %add_convert_fusion.1), channel_id=1, source_target_pairs={{0,6},{2,4},{4,2},{6,0},{1,7},{3,5},{5,3},{7,1},{8,14},{10,12},{12... | collective-permute-start | bytes 49160 | tf_op jit(solution)/shard_map/ppermute | solution.py:60
  20.8 3.7 %collective-permute-start.7 = (bf16[16,512]{1,0:T(8,128)(2,1)S(1)}, bf16[16,512]{1,0:T(8,128)(2,1)S(1)}, u32[]{:S(2)}, u32[]{:S(2)}) collective-permute-start(bf16[16,512]{1,0:T(8,128)(2,1)S(1)} %add_convert_fusion.1), channel_id=1, source_target_pairs={{0,4},{2,6},{4,0},{6,2},{1,5},{3,7},{5,1},{7,3},{8,12},{10,14},{12... | collective-permute-start | bytes 49160 | tf_op jit(solution)/shard_map/ppermute | solution.py:60
  21.3 3.7 %collective-permute-start.8 = (bf16[16,512]{1,0:T(8,128)(2,1)S(1)}, bf16[16,512]{1,0:T(8,128)(2,1)S(1)}, u32[]{:S(2)}, u32[]{:S(2)}) collective-permute-start(bf16[16,512]{1,0:T(8,128)(2,1)S(1)} %add_convert_fusion.1), channel_id=1, source_target_pairs={{0,2},{2,0},{4,6},{6,4},{1,3},{3,1},{5,7},{7,5},{8,10},{10,8},{12,... | collective-permute-start | bytes 49160 | tf_op jit(solution)/shard_map/ppermute | solution.py:60

commit v5 on v4

--- a/solution.py
+++ b/solution.py
@@ -80,7 +80,7 @@
 
 
 def scatter_sum(parts, axis, size):
-    parts, dtype = list(parts), parts[0].dtype
+    parts, dtype = list(parts), parts[-1].dtype
     for stride, count in reversed(digits(size)):
         low = len(parts) // count
         blocks = parts if low == 1 else [
@@ -89,7 +89,8 @@
         found = dict(zip(in_order(count, GATHER), blocks[1:]))
         steps = in_order(count, SCATTER)
         terms = blocks[:1] + exchange([found[s] for s in steps], axis, size, stride, steps, -1)
-        total = tree_sum([t.astype(jnp.float32) for t in terms]).astype(dtype)
+        total = tree_sum([t.astype(jnp.float32) for t in terms])
+        total = total if low == 1 else total.astype(dtype)
         parts = [total] if low == 1 else [total[i] for i in range(low)]
     return parts[0]
 
@@ -271,7 +272,8 @@
         out_shape=[
             jax.ShapeDtypeStruct((heads * count, prefix, wide), jnp.bfloat16), row, row
         ]
-        + [like(packed)] * groups,
+        + [jax.ShapeDtypeStruct(packed.shape, jnp.float32)]
+        + [like(packed)] * (groups - 1),
         in_specs=[vmem] * (6 + groups),
         out_specs=[vmem] * (3 + groups),
         compiler_params=params,
@@ -293,6 +295,7 @@
     )(q, g, keys, powers, dweights, *outs[:3], *parts)
     owned = scatter_sum(outs[3:], "group", groups)
     total = all_sum(owned, "branch", branches)
+    total = total.astype(jnp.bfloat16)
     half = prefix_keys.shape[1]
     return query_grad, branch_key_grad, branch_value_grad, total[:, :half], total[:, half:]
 

time: 25.9 us -> 26.1 us (level)
  no operation moved by 1% of the time
where the time goes in v5:
time: 26.1 us; the launch traced here: 25.8 us
  starting transfers between devices  13.8 us (53%)
  waiting for transfers between devices  6.23 us (24%)
  Pallas kernels  3.81 us (15%)
  local copies, waits for them, and re-layouts  1.32 us (5%)
  between operations  0.69 us (3%)
    ppermute x9, starting transfers between devices, exchange(): lax.ppermute(block, axis, moved(size, stride, count, step, sign))  13.8 us
    ppermute x9, waiting for transfers between devices, exchange(): lax.ppermute(block, axis, moved(size, stride, count, step, sign))  6.23 us
    pallas_call x1, Pallas kernels, body(): pl.pallas_call(tree_kernel, out_shape=[like(queries), like(out_grad), lik...  1.74 us
    pallas_call x1, Pallas kernels, body(): pl.pallas_call(functools.partial(branch_kernel, parts=groups), out_shape=...  1.28 us
    pallas_call x1, Pallas kernels, body(): pl.pallas_call(functools.partial(prefix_kernel, parts=groups), out_shape=...  0.79 us
    unnamed x7, local copies, waits for them, and re-layouts  0.72 us
    slice x1, local copies, waits for them, and re-layouts, body(): total[:, half:]  0.61 us
  transfers between devices with their start and end apart: 9, of which 5 were waited for; matrix products, arithmetic and copies ran while one was open for 0% of the time, Pallas kernels for 12%

profile of v5, /device:TPU:0, one launch (start us, length us, event | category | flops | bytes accessed | tf_op | source)
XLA Modules:
  0.0 25.8 jit_solution(6582285694956517951)
XLA Ops:
  0.6 0.0 copy-start.2
  0.6 0.7 %constant_dynamic-update-slice_fusion.1 = bf16[16,512]{1,0:T(8,128)(2,1)S(1)} fusion(bf16[16,256]{1,0:T(8,128)(2,1)} %param.11), kind=kLoop, calls=%fused_computation.3 | loop fusion | bytes 16384
  1.3 0.0 copy-done.2
  1.4 0.0 copy-start
  1.4 0.0 copy-start.1
  1.4 5.1 %collective-permute-start = (bf16[16,512]{1,0:T(8,128)(2,1)S(1)}, bf16[16,512]{1,0:T(8,128)(2,1)S(1)}, u32[]{:S(2)}, u32[]{:S(2)}) collective-permute-start(bf16[16,512]{1,0:T(8,128)(2,1)S(1)} %constant_dynamic-update-slice_fusion.refs_6_.refs_8_), channel_id=1, source_target_pairs={{0,24},{8,16},{16,8},{24,0},{1,25},{9,17},{17,9},{25,1},{2,26},{10... | collective-permute-start | bytes 49160 | tf_op jit(solution)/shard_map/ppermute | solution.py:60
  6.5 0.0 collective-permute-start.1
  6.5 0.6 %collective-permute-start.2 = (bf16[16,512]{1,0:T(8,128)(2,1)S(1)}, bf16[16,512]{1,0:T(8,128)(2,1)S(1)}, u32[]{:S(2)}, u32[]{:S(2)}) collective-permute-start(bf16[16,512]{1,0:T(8,128)(2,1)S(1)} %constant_dynamic-update-slice_fusion.refs_6_.refs_8_), channel_id=1, source_target_pairs={{0,8},{8,0},{16,24},{24,16},{1,9},{9,1},{17,25},{25,17},{2,10},{10... | collective-permute-start | bytes 49160 | tf_op jit(solution)/shard_map/ppermute | solution.py:60
  7.1 0.0 copy-done
  7.1 0.0 copy-done.1
  7.1 1.7 %tree.1 = (bf16[2,64,2048]{2,1,0:T(8,128)(2,1)S(1)}, bf16[2,64,2048]{2,1,0:T(8,128)(2,1)S(1)}, bf16[2,64,256]{2,1,0:T(8,128)(2,1)S(1)}, f32[4,64,512]{2,1,0:T(8,...) custom-call(bf16[2,64,2048]{2,1,0:T(8,128)(2,1)} %q_hbm.1, ...), custom_call_target="tpu_custom_call" | custom-call | flops 67108864 | bytes 1048576 | tf_op jit(solution)/shard_map/tree/pallas_call | solution.py:255
  8.9 0.0 collective-permute-done.refs_7_.refs_9_
  8.9 2.2 %collective-permute-done.1.refs_8_.refs_10_ = bf16[16,512]{1,0:T(8,128)(2,1)S(1)} collective-permute-done((bf16[16,512]{1,0:T(8,128)(2,1)S(1)}, bf16[16,512]{1,0:T(8,128)(2,1)S(1)}, u32[]{:S(2)}, u32[]{:S(2)}) %collective-permute-start.1) | collective-permute-done | bytes 16416 | tf_op jit(solution)/shard_map/ppermute | solution.py:60
  11.1 0.0 collective-permute-done.2.refs_9_.refs_11_
  11.1 0.8 %prefix.1 = (bf16[4,64,512]{2,1,0:T(8,128)(2,1)S(1)}, f32[4,1,512]{2,1,0:T(1,128)S(1)}, f32[4,1,512]{2,1,0:T(1,128)S(1)}, f32[16,512]{1,0:T(8,128)S(1)}, bf16[16...) custom-call(bf16[2,64,2048]{2,1,0:T(8,128)(2,1)S(1)} %get-tuple-element.24.refs_0_, ...), custom_call_target="tpu_custom_call" | custom-call | flops 134217728 | tf_op jit(solution)/shard_map/prefix/pallas_call | solution.py:270
  11.9 1.6 %collective-permute-start.3 = (bf16[16,512]{1,0:T(8,128)(2,1)S(1)}, bf16[16,512]{1,0:T(8,128)(2,1)S(1)}, u32[]{:S(2)}, u32[]{:S(2)}) collective-permute-start(bf16[16,512]{1,0:T(8,128)(2,1)S(1)} %get-tuple-element.40), channel_id=1, source_target_pairs={{0,24},{8,16},{16,8},{24,0},{1,25},{9,17},{17,9},{25,1},{2,26},{10... | collective-permute-start | bytes 49160 | tf_op jit(solution)/shard_map/ppermute | solution.py:60
  13.5 0.6 %collective-permute-start.4 = (bf16[16,512]{1,0:T(8,128)(2,1)S(1)}, bf16[16,512]{1,0:T(8,128)(2,1)S(1)}, u32[]{:S(2)}, u32[]{:S(2)}) collective-permute-start(bf16[16,512]{1,0:T(8,128)(2,1)S(1)} %get-tuple-element.41), channel_id=1, source_target_pairs={{0,16},{8,24},{16,0},{24,8},{1,17},{9,25},{17,1},{25,9},{2,18},{10... | collective-permute-start | bytes 49160 | tf_op jit(solution)/shard_map/ppermute | solution.py:60
  14.1 2.3 %collective-permute-start.5 = (bf16[16,512]{1,0:T(8,128)(2,1)S(1)}, bf16[16,512]{1,0:T(8,128)(2,1)S(1)}, u32[]{:S(2)}, u32[]{:S(2)}) collective-permute-start(bf16[16,512]{1,0:T(8,128)(2,1)S(1)} %get-tuple-element.42), channel_id=1, source_target_pairs={{0,8},{8,0},{16,24},{24,16},{1,9},{9,1},{17,25},{25,17},{2,10},{10... | collective-permute-start | bytes 49160 | tf_op jit(solution)/shard_map/ppermute | solution.py:60
  16.4 1.1 %collective-permute-done.3 = bf16[16,512]{1,0:T(8,128)(2,1)S(1)} collective-permute-done((bf16[16,512]{1,0:T(8,128)(2,1)S(1)}, bf16[16,512]{1,0:T(8,128)(2,1)S(1)}, u32[]{:S(2)}, u32[]{:S(2)}) %collective-permute-start.3) | collective-permute-done | bytes 16416 | tf_op jit(solution)/shard_map/ppermute | solution.py:60
  17.5 0.7 %collective-permute-done.4 = bf16[16,512]{1,0:T(8,128)(2,1)S(1)} collective-permute-done((bf16[16,512]{1,0:T(8,128)(2,1)S(1)}, bf16[16,512]{1,0:T(8,128)(2,1)S(1)}, u32[]{:S(2)}, u32[]{:S(2)}) %collective-permute-start.4) | collective-permute-done | bytes 16416 | tf_op jit(solution)/shard_map/ppermute | solution.py:60
  18.3 0.0 collective-permute-done.5
  18.3 2.5 %collective-permute-start.6 = (f32[16,512]{1,0:T(8,128)S(1)}, f32[16,512]{1,0:T(8,128)S(1)}, u32[]{:S(2)}, u32[]{:S(2)}) collective-permute-start(f32[16,512]{1,0:T(8,128)S(1)} %add_add_fusion), channel_id=1, source_target_pairs={{0,6},{2,4},{4,2},{6,0},{1,7},{3,5},{5,3},{7,1},{8,14},{10,12},{12... | collective-permute-start | bytes 98312 | tf_op jit(solution)/shard_map/ppermute | solution.py:60
  20.8 0.5 %collective-permute-start.7 = (f32[16,512]{1,0:T(8,128)S(1)}, f32[16,512]{1,0:T(8,128)S(1)}, u32[]{:S(2)}, u32[]{:S(2)}) collective-permute-start(f32[16,512]{1,0:T(8,128)S(1)} %add_add_fusion), channel_id=1, source_target_pairs={{0,4},{2,6},{4,0},{6,2},{1,5},{3,7},{5,1},{7,3},{8,12},{10,14},{12... | collective-permute-start | bytes 98312 | tf_op jit(solution)/shard_map/ppermute | solution.py:60
  21.3 0.5 %collective-permute-start.8 = (f32[16,512]{1,0:T(8,128)S(1)}, f32[16,512]{1,0:T(8,128)S(1)}, u32[]{:S(2)}, u32[]{:S(2)}) collective-permute-start(f32[16,512]{1,0:T(8,128)S(1)} %add_add_fusion), channel_id=1, source_target_pairs={{0,2},{2,0},{4,6},{6,4},{1,3},{3,1},{5,7},{7,5},{8,10},{10,8},{12,... | collective-permute-start | bytes 98312 | tf_op jit(solution)/shard_map/ppermute | solution.py:60
  21.8 1.3 %branch.1 = (bf16[2,64,2048]{2,1,0:T(8,128)(2,1)}, bf16[2,64,256]{2,1,0:T(8,128)(2,1)}, bf16[2,64,256]{2,1,0:T(8,128)(2,1)}) custom-call(bf16[2,64,2048]{2,1,0:T(8,128)(2,1)S(1)} %get-tuple-element.24.refs_0_, bf16[2,64,2048]{2,1,0:T(8,128)(2,1)S(1)} %get-tuple-element.25.refs_1_, bf16[2,64,256]{2,1,0:T(8,128)(2,1)S(1)} %get-tuple-element.26.refs_2_, ...), custom_call_target="tpu_custom_call" | custom-call | flops 134217728 | bytes 524288 | tf_op jit(solution)/shard_map/branch/pallas_call | solution.py:285
  23.1 0.0 collective-permute-done.6
  23.2 1.5 %collective-permute-done.7 = f32[16,512]{1,0:T(8,128)S(1)} collective-permute-done((f32[16,512]{1,0:T(8,128)S(1)}, f32[16,512]{1,0:T(8,128)S(1)}, u32[]{:S(2)}, u32[]{:S(2)}) %collective-permute-start.7) | collective-permute-done | bytes 32800 | tf_op jit(solution)/shard_map/ppermute | solution.py:60
  24.7 0.5 %collective-permute-done.8 = f32[16,512]{1,0:T(8,128)S(1)} collective-permute-done((f32[16,512]{1,0:T(8,128)S(1)}, f32[16,512]{1,0:T(8,128)S(1)}, u32[]{:S(2)}, u32[]{:S(2)}) %collective-permute-start.8) | collective-permute-done | bytes 32800 | tf_op jit(solution)/shard_map/ppermute | solution.py:60
  25.2 0.6 %fusion = (bf16[16,256]{1,0:T(8,128)(2,1)}, bf16[16,256]{1,0:T(8,128)(2,1)}) fusion(bf16[16,512]{1,0:T(8,128)(2,1)S(1)} %add_convert_fusion), kind=kLoop, calls=%fused_computation.4 | loop fusion | bytes 32768 | tf_op jit(solution)/shard_map/slice | solution.py:300
  (3 shorter events, 0.0 us)
Async XLA Ops:
  0.6 0.7 %copy-start.2 = (bf16[16,256]{1,0:T(8,128)(2,1)S(1)}, bf16[16,256]{1,0:T(8,128)(2,1)}, u32[]{:S(2)}) copy-start(bf16[16,256]{1,0:T(8,128)(2,1)} %param.12) | copy-start | bytes 24580
  1.4 5.8 %copy-start = (s32[2,64]{1,0:T(2,128)S(1)}, s32[2,64]{1,0:T(2,128)}, u32[]{:S(2)}) copy-start(s32[2,64]{1,0:T(2,128)} %par_ref.1) | copy-start | bytes 1540
  1.4 5.8 %copy-start.1 = (s32[2]{0:T(128)S(1)}, s32[2]{0:T(128)}, u32[]{:S(2)}) copy-start(s32[2]{0:T(128)} %param.15) | copy-start | bytes 28
  1.4 7.5 %collective-permute-start = (bf16[16,512]{1,0:T(8,128)(2,1)S(1)}, bf16[16,512]{1,0:T(8,128)(2,1)S(1)}, u32[]{:S(2)}, u32[]{:S(2)}) collective-permute-start(bf16[16,512]{1,0:T(8,128)(2,1)S(1)} %constant_dynamic-update-slice_fusion.refs_6_.refs_8_), channel_id=1, source_target_pairs={{0,24},{8,16},{16,8},{24,0},{1,25},{9,17},{17,9},{25,1},{2,26},{10... | collective-permute-start | bytes 49160 | tf_op jit(solution)/shard_map/ppermute | solution.py:60
  6.5 4.6 %collective-permute-start.1 = (bf16[16,512]{1,0:T(8,128)(2,1)S(1)}, bf16[16,512]{1,0:T(8,128)(2,1)S(1)}, u32[]{:S(2)}, u32[]{:S(2)}) collective-permute-start(bf16[16,512]{1,0:T(8,128)(2,1)S(1)} %constant_dynamic-update-slice_fusion.refs_6_.refs_8_), channel_id=1, source_target_pairs={{0,16},{8,24},{16,0},{24,8},{1,17},{9,25},{17,1},{25,9},{2,18},{10... | collective-permute-start | bytes 49160 | tf_op jit(solution)/shard_map/ppermute | solution.py:60
  6.5 4.6 %collective-permute-start.2 = (bf16[16,512]{1,0:T(8,128)(2,1)S(1)}, bf16[16,512]{1,0:T(8,128)(2,1)S(1)}, u32[]{:S(2)}, u32[]{:S(2)}) collective-permute-start(bf16[16,512]{1,0:T(8,128)(2,1)S(1)} %constant_dynamic-update-slice_fusion.refs_6_.refs_8_), channel_id=1, source_target_pairs={{0,8},{8,0},{16,24},{24,16},{1,9},{9,1},{17,25},{25,17},{2,10},{10... | collective-permute-start | bytes 49160 | tf_op jit(solution)/shard_map/ppermute | solution.py:60
  11.9 5.6 %collective-permute-start.3 = (bf16[16,512]{1,0:T(8,128)(2,1)S(1)}, bf16[16,512]{1,0:T(8,128)(2,1)S(1)}, u32[]{:S(2)}, u32[]{:S(2)}) collective-permute-start(bf16[16,512]{1,0:T(8,128)(2,1)S(1)} %get-tuple-element.40), channel_id=1, source_target_pairs={{0,24},{8,16},{16,8},{24,0},{1,25},{9,17},{17,9},{25,1},{2,26},{10... | collective-permute-start | bytes 49160 | tf_op jit(solution)/shard_map/ppermute | solution.py:60
  13.5 4.7 %collective-permute-start.4 = (bf16[16,512]{1,0:T(8,128)(2,1)S(1)}, bf16[16,512]{1,0:T(8,128)(2,1)S(1)}, u32[]{:S(2)}, u32[]{:S(2)}) collective-permute-start(bf16[16,512]{1,0:T(8,128)(2,1)S(1)} %get-tuple-element.41), channel_id=1, source_target_pairs={{0,16},{8,24},{16,0},{24,8},{1,17},{9,25},{17,1},{25,9},{2,18},{10... | collective-permute-start | bytes 49160 | tf_op jit(solution)/shard_map/ppermute | solution.py:60
  14.1 4.2 %collective-permute-start.5 = (bf16[16,512]{1,0:T(8,128)(2,1)S(1)}, bf16[16,512]{1,0:T(8,128)(2,1)S(1)}, u32[]{:S(2)}, u32[]{:S(2)}) collective-permute-start(bf16[16,512]{1,0:T(8,128)(2,1)S(1)} %get-tuple-element.42), channel_id=1, source_target_pairs={{0,8},{8,0},{16,24},{24,16},{1,9},{9,1},{17,25},{25,17},{2,10},{10... | collective-permute-start | bytes 49160 | tf_op jit(solution)/shard_map/ppermute | solution.py:60
  18.3 4.9 %collective-permute-start.6 = (f32[16,512]{1,0:T(8,128)S(1)}, f32[16,512]{1,0:T(8,128)S(1)}, u32[]{:S(2)}, u32[]{:S(2)}) collective-permute-start(f32[16,512]{1,0:T(8,128)S(1)} %add_add_fusion), channel_id=1, source_target_pairs={{0,6},{2,4},{4,2},{6,0},{1,7},{3,5},{5,3},{7,1},{8,14},{10,12},{12... | collective-permute-start | bytes 98312 | tf_op jit(solution)/shard_map/ppermute | solution.py:60
  20.8 3.9 %collective-permute-start.7 = (f32[16,512]{1,0:T(8,128)S(1)}, f32[16,512]{1,0:T(8,128)S(1)}, u32[]{:S(2)}, u32[]{:S(2)}) collective-permute-start(f32[16,512]{1,0:T(8,128)S(1)} %add_add_fusion), channel_id=1, source_target_pairs={{0,4},{2,6},{4,0},{6,2},{1,5},{3,7},{5,1},{7,3},{8,12},{10,14},{12... | collective-permute-start | bytes 98312 | tf_op jit(solution)/shard_map/ppermute | solution.py:60
  21.3 3.9 %collective-permute-start.8 = (f32[16,512]{1,0:T(8,128)S(1)}, f32[16,512]{1,0:T(8,128)S(1)}, u32[]{:S(2)}, u32[]{:S(2)}) collective-permute-start(f32[16,512]{1,0:T(8,128)S(1)} %add_add_fusion), channel_id=1, source_target_pairs={{0,2},{2,0},{4,6},{6,4},{1,3},{3,1},{5,7},{7,5},{8,10},{10,8},{12,... | collective-permute-start | bytes 98312 | tf_op jit(solution)/shard_map/ppermute | solution.py:60

commit v6 on v5

--- a/solution.py
+++ b/solution.py
@@ -80,7 +80,7 @@
 
 
 def scatter_sum(parts, axis, size):
-    parts, dtype = list(parts), parts[-1].dtype
+    parts = list(parts)
     for stride, count in reversed(digits(size)):
         low = len(parts) // count
         blocks = parts if low == 1 else [
@@ -90,7 +90,6 @@
         steps = in_order(count, SCATTER)
         terms = blocks[:1] + exchange([found[s] for s in steps], axis, size, stride, steps, -1)
         total = tree_sum([t.astype(jnp.float32) for t in terms])
-        total = total if low == 1 else total.astype(dtype)
         parts = [total] if low == 1 else [total[i] for i in range(low)]
     return parts[0]
 
@@ -98,8 +97,7 @@
 def all_sum(x, axis, size):
     for stride, count in digits(size):
         steps = in_order(count, SUM)
-        terms = [x] + exchange([x] * (count - 1), axis, size, stride, steps, 1)
-        x = tree_sum([t.astype(jnp.float32) for t in terms]).astype(x.dtype)
+        x = tree_sum([x] + exchange([x] * (count - 1), axis, size, stride, steps, 1))
     return x
 
 
@@ -272,8 +270,8 @@
         out_shape=[
             jax.ShapeDtypeStruct((heads * count, prefix, wide), jnp.bfloat16), row, row
         ]
-        + [jax.ShapeDtypeStruct(packed.shape, jnp.float32)]
-        + [like(packed)] * (groups - 1),
+        + [jax.ShapeDtypeStruct(packed.shape, jnp.float32)] * (groups - 1)
+        + [like(packed)],
         in_specs=[vmem] * (6 + groups),
         out_specs=[vmem] * (3 + groups),
         compiler_params=params,

time: 26.1 us -> 26.3 us (level)
  transfers between devices with their start and end apart: 9 -> 9, of which waited for: 5 -> 4; matrix products, arithmetic and copies ran while one was open for 0% -> 0% of each run, Pallas kernels for 12% -> 12%
where the time goes in v6:
time: 26.3 us; the launch traced here: 26 us
  starting transfers between devices  13.8 us (52%)
  waiting for transfers between devices  6.41 us (24%)
  Pallas kernels  3.81 us (14%)
  local copies, waits for them, and re-layouts  1.32 us (5%)
  between operations  0.69 us (3%)
    ppermute x9, starting transfers between devices, exchange(): lax.ppermute(block, axis, moved(size, stride, count, step, sign))  13.8 us
    ppermute x9, waiting for transfers between devices, exchange(): lax.ppermute(block, axis, moved(size, stride, count, step, sign))  6.41 us
    pallas_call x1, Pallas kernels, body(): pl.pallas_call(tree_kernel, out_shape=[like(queries), like(out_grad), lik...  1.74 us
    pallas_call x1, Pallas kernels, body(): pl.pallas_call(functools.partial(branch_kernel, parts=groups), out_shape=...  1.28 us
    pallas_call x1, Pallas kernels, body(): pl.pallas_call(functools.partial(prefix_kernel, parts=groups), out_shape=...  0.79 us
    unnamed x7, local copies, waits for them, and re-layouts  0.72 us
    slice x1, local copies, waits for them, and re-layouts, body(): total[:, half:]  0.61 us
  transfers between devices with their start and end apart: 9, of which 4 were waited for; matrix products, arithmetic and copies ran while one was open for 0% of the time, Pallas kernels for 12%

profile of v6, /device:TPU:0, one launch (start us, length us, event | category | flops | bytes accessed | tf_op | source)
XLA Modules:
  0.0 26.0 jit_solution(266879662446133721)
XLA Ops:
  0.6 0.0 copy-start.2
  0.6 0.7 %constant_dynamic-update-slice_fusion.1 = bf16[16,512]{1,0:T(8,128)(2,1)S(1)} fusion(bf16[16,256]{1,0:T(8,128)(2,1)} %param.11), kind=kLoop, calls=%fused_computation.3 | loop fusion | bytes 16384
  1.3 0.0 copy-done.2
  1.4 0.0 copy-start
  1.4 0.0 copy-start.1
  1.4 5.1 %collective-permute-start = (bf16[16,512]{1,0:T(8,128)(2,1)S(1)}, bf16[16,512]{1,0:T(8,128)(2,1)S(1)}, u32[]{:S(2)}, u32[]{:S(2)}) collective-permute-start(bf16[16,512]{1,0:T(8,128)(2,1)S(1)} %constant_dynamic-update-slice_fusion.refs_6_.refs_8_), channel_id=1, source_target_pairs={{0,24},{8,16},{16,8},{24,0},{1,25},{9,17},{17,9},{25,1},{2,26},{10... | collective-permute-start | bytes 49160 | tf_op jit(solution)/shard_map/ppermute | solution.py:60
  6.5 0.0 collective-permute-start.1
  6.5 0.6 %collective-permute-start.2 = (bf16[16,512]{1,0:T(8,128)(2,1)S(1)}, bf16[16,512]{1,0:T(8,128)(2,1)S(1)}, u32[]{:S(2)}, u32[]{:S(2)}) collective-permute-start(bf16[16,512]{1,0:T(8,128)(2,1)S(1)} %constant_dynamic-update-slice_fusion.refs_6_.refs_8_), channel_id=1, source_target_pairs={{0,8},{8,0},{16,24},{24,16},{1,9},{9,1},{17,25},{25,17},{2,10},{10... | collective-permute-start | bytes 49160 | tf_op jit(solution)/shard_map/ppermute | solution.py:60
  7.1 0.0 copy-done
  7.1 0.0 copy-done.1
  7.1 1.7 %tree.1 = (bf16[2,64,2048]{2,1,0:T(8,128)(2,1)S(1)}, bf16[2,64,2048]{2,1,0:T(8,128)(2,1)S(1)}, bf16[2,64,256]{2,1,0:T(8,128)(2,1)S(1)}, f32[4,64,512]{2,1,0:T(8,...) custom-call(bf16[2,64,2048]{2,1,0:T(8,128)(2,1)} %q_hbm.1, ...), custom_call_target="tpu_custom_call" | custom-call | flops 67108864 | bytes 1048576 | tf_op jit(solution)/shard_map/tree/pallas_call | solution.py:253
  8.9 0.0 collective-permute-done.refs_7_.refs_9_
  8.9 2.2 %collective-permute-done.1.refs_8_.refs_10_ = bf16[16,512]{1,0:T(8,128)(2,1)S(1)} collective-permute-done((bf16[16,512]{1,0:T(8,128)(2,1)S(1)}, bf16[16,512]{1,0:T(8,128)(2,1)S(1)}, u32[]{:S(2)}, u32[]{:S(2)}) %collective-permute-start.1) | collective-permute-done | bytes 16416 | tf_op jit(solution)/shard_map/ppermute | solution.py:60
  11.1 0.0 collective-permute-done.2.refs_9_.refs_11_
  11.1 0.8 %prefix.1 = (bf16[4,64,512]{2,1,0:T(8,128)(2,1)S(1)}, f32[4,1,512]{2,1,0:T(1,128)S(1)}, f32[4,1,512]{2,1,0:T(1,128)S(1)}, f32[16,512]{1,0:T(8,128)S(1)}, f32[16,...) custom-call(bf16[2,64,2048]{2,1,0:T(8,128)(2,1)S(1)} %get-tuple-element.24.refs_0_, ...), custom_call_target="tpu_custom_call" | custom-call | flops 134217728 | tf_op jit(solution)/shard_map/prefix/pallas_call | solution.py:268
  11.9 1.6 %collective-permute-start.3 = (f32[16,512]{1,0:T(8,128)S(1)}, f32[16,512]{1,0:T(8,128)S(1)}, u32[]{:S(2)}, u32[]{:S(2)}) collective-permute-start(f32[16,512]{1,0:T(8,128)S(1)} %get-tuple-element.40), channel_id=1, source_target_pairs={{0,24},{8,16},{16,8},{24,0},{1,25},{9,17},{17,9},{25,1},{2,26},{10... | collective-permute-start | bytes 98312 | tf_op jit(solution)/shard_map/ppermute | solution.py:60
  13.5 0.6 %collective-permute-start.4 = (f32[16,512]{1,0:T(8,128)S(1)}, f32[16,512]{1,0:T(8,128)S(1)}, u32[]{:S(2)}, u32[]{:S(2)}) collective-permute-start(f32[16,512]{1,0:T(8,128)S(1)} %get-tuple-element.41), channel_id=1, source_target_pairs={{0,16},{8,24},{16,0},{24,8},{1,17},{9,25},{17,1},{25,9},{2,18},{10... | collective-permute-start | bytes 98312 | tf_op jit(solution)/shard_map/ppermute | solution.py:60
  14.1 2.3 %collective-permute-start.5 = (bf16[16,512]{1,0:T(8,128)(2,1)S(1)}, bf16[16,512]{1,0:T(8,128)(2,1)S(1)}, u32[]{:S(2)}, u32[]{:S(2)}) collective-permute-start(bf16[16,512]{1,0:T(8,128)(2,1)S(1)} %get-tuple-element.42), channel_id=1, source_target_pairs={{0,8},{8,0},{16,24},{24,16},{1,9},{9,1},{17,25},{25,17},{2,10},{10... | collective-permute-start | bytes 49160 | tf_op jit(solution)/shard_map/ppermute | solution.py:60
  16.4 2.1 %collective-permute-done.5 = bf16[16,512]{1,0:T(8,128)(2,1)S(1)} collective-permute-done((bf16[16,512]{1,0:T(8,128)(2,1)S(1)}, bf16[16,512]{1,0:T(8,128)(2,1)S(1)}, u32[]{:S(2)}, u32[]{:S(2)}) %collective-permute-start.5) | collective-permute-done | bytes 16416 | tf_op jit(solution)/shard_map/ppermute | solution.py:60
  18.4 0.0 collective-permute-done.3
  18.4 0.0 collective-permute-done.4
  18.5 2.5 %collective-permute-start.6 = (f32[16,512]{1,0:T(8,128)S(1)}, f32[16,512]{1,0:T(8,128)S(1)}, u32[]{:S(2)}, u32[]{:S(2)}) collective-permute-start(f32[16,512]{1,0:T(8,128)S(1)} %add_add_fusion), channel_id=1, source_target_pairs={{0,6},{2,4},{4,2},{6,0},{1,7},{3,5},{5,3},{7,1},{8,14},{10,12},{12... | collective-permute-start | bytes 98312 | tf_op jit(solution)/shard_map/ppermute | solution.py:60
  21.0 0.5 %collective-permute-start.7 = (f32[16,512]{1,0:T(8,128)S(1)}, f32[16,512]{1,0:T(8,128)S(1)}, u32[]{:S(2)}, u32[]{:S(2)}) collective-permute-start(f32[16,512]{1,0:T(8,128)S(1)} %add_add_fusion), channel_id=1, source_target_pairs={{0,4},{2,6},{4,0},{6,2},{1,5},{3,7},{5,1},{7,3},{8,12},{10,14},{12... | collective-permute-start | bytes 98312 | tf_op jit(solution)/shard_map/ppermute | solution.py:60
  21.5 0.5 %collective-permute-start.8 = (f32[16,512]{1,0:T(8,128)S(1)}, f32[16,512]{1,0:T(8,128)S(1)}, u32[]{:S(2)}, u32[]{:S(2)}) collective-permute-start(f32[16,512]{1,0:T(8,128)S(1)} %add_add_fusion), channel_id=1, source_target_pairs={{0,2},{2,0},{4,6},{6,4},{1,3},{3,1},{5,7},{7,5},{8,10},{10,8},{12,... | collective-permute-start | bytes 98312 | tf_op jit(solution)/shard_map/ppermute | solution.py:60
  22.0 1.3 %branch.1 = (bf16[2,64,2048]{2,1,0:T(8,128)(2,1)}, bf16[2,64,256]{2,1,0:T(8,128)(2,1)}, bf16[2,64,256]{2,1,0:T(8,128)(2,1)}) custom-call(bf16[2,64,2048]{2,1,0:T(8,128)(2,1)S(1)} %get-tuple-element.24.refs_0_, bf16[2,64,2048]{2,1,0:T(8,128)(2,1)S(1)} %get-tuple-element.25.refs_1_, bf16[2,64,256]{2,1,0:T(8,128)(2,1)S(1)} %get-tuple-element.26.refs_2_, ...), custom_call_target="tpu_custom_call" | custom-call | flops 134217728 | bytes 524288 | tf_op jit(solution)/shard_map/branch/pallas_call | solution.py:283
  23.3 0.0 collective-permute-done.6
  23.3 1.6 %collective-permute-done.7 = f32[16,512]{1,0:T(8,128)S(1)} collective-permute-done((f32[16,512]{1,0:T(8,128)S(1)}, f32[16,512]{1,0:T(8,128)S(1)}, u32[]{:S(2)}, u32[]{:S(2)}) %collective-permute-start.7) | collective-permute-done | bytes 32800 | tf_op jit(solution)/shard_map/ppermute | solution.py:60
  24.9 0.5 %collective-permute-done.8 = f32[16,512]{1,0:T(8,128)S(1)} collective-permute-done((f32[16,512]{1,0:T(8,128)S(1)}, f32[16,512]{1,0:T(8,128)S(1)}, u32[]{:S(2)}, u32[]{:S(2)}) %collective-permute-start.8) | collective-permute-done | bytes 32800 | tf_op jit(solution)/shard_map/ppermute | solution.py:60
  25.4 0.6 %fusion = (bf16[16,256]{1,0:T(8,128)(2,1)}, bf16[16,256]{1,0:T(8,128)(2,1)}) fusion(bf16[16,512]{1,0:T(8,128)(2,1)S(1)} %add_convert_fusion), kind=kLoop, calls=%fused_computation.4 | loop fusion | bytes 32768 | tf_op jit(solution)/shard_map/slice | solution.py:298
  (3 shorter events, 0.0 us)
Async XLA Ops:
  0.6 0.7 %copy-start.2 = (bf16[16,256]{1,0:T(8,128)(2,1)S(1)}, bf16[16,256]{1,0:T(8,128)(2,1)}, u32[]{:S(2)}) copy-start(bf16[16,256]{1,0:T(8,128)(2,1)} %param.12) | copy-start | bytes 24580
  1.4 5.8 %copy-start = (s32[2,64]{1,0:T(2,128)S(1)}, s32[2,64]{1,0:T(2,128)}, u32[]{:S(2)}) copy-start(s32[2,64]{1,0:T(2,128)} %par_ref.1) | copy-start | bytes 1540
  1.4 5.8 %copy-start.1 = (s32[2]{0:T(128)S(1)}, s32[2]{0:T(128)}, u32[]{:S(2)}) copy-start(s32[2]{0:T(128)} %param.15) | copy-start | bytes 28
  1.4 7.5 %collective-permute-start = (bf16[16,512]{1,0:T(8,128)(2,1)S(1)}, bf16[16,512]{1,0:T(8,128)(2,1)S(1)}, u32[]{:S(2)}, u32[]{:S(2)}) collective-permute-start(bf16[16,512]{1,0:T(8,128)(2,1)S(1)} %constant_dynamic-update-slice_fusion.refs_6_.refs_8_), channel_id=1, source_target_pairs={{0,24},{8,16},{16,8},{24,0},{1,25},{9,17},{17,9},{25,1},{2,26},{10... | collective-permute-start | bytes 49160 | tf_op jit(solution)/shard_map/ppermute | solution.py:60
  6.5 4.6 %collective-permute-start.1 = (bf16[16,512]{1,0:T(8,128)(2,1)S(1)}, bf16[16,512]{1,0:T(8,128)(2,1)S(1)}, u32[]{:S(2)}, u32[]{:S(2)}) collective-permute-start(bf16[16,512]{1,0:T(8,128)(2,1)S(1)} %constant_dynamic-update-slice_fusion.refs_6_.refs_8_), channel_id=1, source_target_pairs={{0,16},{8,24},{16,0},{24,8},{1,17},{9,25},{17,1},{25,9},{2,18},{10... | collective-permute-start | bytes 49160 | tf_op jit(solution)/shard_map/ppermute | solution.py:60
  6.5 4.6 %collective-permute-start.2 = (bf16[16,512]{1,0:T(8,128)(2,1)S(1)}, bf16[16,512]{1,0:T(8,128)(2,1)S(1)}, u32[]{:S(2)}, u32[]{:S(2)}) collective-permute-start(bf16[16,512]{1,0:T(8,128)(2,1)S(1)} %constant_dynamic-update-slice_fusion.refs_6_.refs_8_), channel_id=1, source_target_pairs={{0,8},{8,0},{16,24},{24,16},{1,9},{9,1},{17,25},{25,17},{2,10},{10... | collective-permute-start | bytes 49160 | tf_op jit(solution)/shard_map/ppermute | solution.py:60
  11.9 6.5 %collective-permute-start.3 = (f32[16,512]{1,0:T(8,128)S(1)}, f32[16,512]{1,0:T(8,128)S(1)}, u32[]{:S(2)}, u32[]{:S(2)}) collective-permute-start(f32[16,512]{1,0:T(8,128)S(1)} %get-tuple-element.40), channel_id=1, source_target_pairs={{0,24},{8,16},{16,8},{24,0},{1,25},{9,17},{17,9},{25,1},{2,26},{10... | collective-permute-start | bytes 98312 | tf_op jit(solution)/shard_map/ppermute | solution.py:60
  13.5 4.9 %collective-permute-start.4 = (f32[16,512]{1,0:T(8,128)S(1)}, f32[16,512]{1,0:T(8,128)S(1)}, u32[]{:S(2)}, u32[]{:S(2)}) collective-permute-start(f32[16,512]{1,0:T(8,128)S(1)} %get-tuple-element.41), channel_id=1, source_target_pairs={{0,16},{8,24},{16,0},{24,8},{1,17},{9,25},{17,1},{25,9},{2,18},{10... | collective-permute-start | bytes 98312 | tf_op jit(solution)/shard_map/ppermute | solution.py:60
  14.1 4.3 %collective-permute-start.5 = (bf16[16,512]{1,0:T(8,128)(2,1)S(1)}, bf16[16,512]{1,0:T(8,128)(2,1)S(1)}, u32[]{:S(2)}, u32[]{:S(2)}) collective-permute-start(bf16[16,512]{1,0:T(8,128)(2,1)S(1)} %get-tuple-element.42), channel_id=1, source_target_pairs={{0,8},{8,0},{16,24},{24,16},{1,9},{9,1},{17,25},{25,17},{2,10},{10... | collective-permute-start | bytes 49160 | tf_op jit(solution)/shard_map/ppermute | solution.py:60
  18.5 4.9 %collective-permute-start.6 = (f32[16,512]{1,0:T(8,128)S(1)}, f32[16,512]{1,0:T(8,128)S(1)}, u32[]{:S(2)}, u32[]{:S(2)}) collective-permute-start(f32[16,512]{1,0:T(8,128)S(1)} %add_add_fusion), channel_id=1, source_target_pairs={{0,6},{2,4},{4,2},{6,0},{1,7},{3,5},{5,3},{7,1},{8,14},{10,12},{12... | collective-permute-start | bytes 98312 | tf_op jit(solution)/shard_map/ppermute | solution.py:60
  21.0 3.9 %collective-permute-start.7 = (f32[16,512]{1,0:T(8,128)S(1)}, f32[16,512]{1,0:T(8,128)S(1)}, u32[]{:S(2)}, u32[]{:S(2)}) collective-permute-start(f32[16,512]{1,0:T(8,128)S(1)} %add_add_fusion), channel_id=1, source_target_pairs={{0,4},{2,6},{4,0},{6,2},{1,5},{3,7},{5,1},{7,3},{8,12},{10,14},{12... | collective-permute-start | bytes 98312 | tf_op jit(solution)/shard_map/ppermute | solution.py:60
  21.5 3.9 %collective-permute-start.8 = (f32[16,512]{1,0:T(8,128)S(1)}, f32[16,512]{1,0:T(8,128)S(1)}, u32[]{:S(2)}, u32[]{:S(2)}) collective-permute-start(f32[16,512]{1,0:T(8,128)S(1)} %add_add_fusion), channel_id=1, source_target_pairs={{0,2},{2,0},{4,6},{6,4},{1,3},{3,1},{5,7},{7,5},{8,10},{10,8},{12,... | collective-permute-start | bytes 98312 | tf_op jit(solution)/shard_map/ppermute | solution.py:60

commit v7 on v6

--- a/solution.py
+++ b/solution.py
@@ -97,7 +97,9 @@
 def all_sum(x, axis, size):
     for stride, count in digits(size):
         steps = in_order(count, SUM)
-        x = tree_sum([x] + exchange([x] * (count - 1), axis, size, stride, steps, 1))
+        sent = x.astype(jnp.bfloat16)
+        terms = [sent] + exchange([sent] * (count - 1), axis, size, stride, steps, 1)
+        x = tree_sum([t.astype(jnp.float32) for t in terms])
     return x
 
 
@@ -270,8 +272,8 @@
         out_shape=[
             jax.ShapeDtypeStruct((heads * count, prefix, wide), jnp.bfloat16), row, row
         ]
-        + [jax.ShapeDtypeStruct(packed.shape, jnp.float32)] * (groups - 1)
-        + [like(packed)],
+        + [jax.ShapeDtypeStruct(packed.shape, jnp.float32)]
+        + [like(packed)] * (groups - 1),
         in_specs=[vmem] * (6 + groups),
         out_specs=[vmem] * (3 + groups),
         compiler_params=params,

time: 26.3 us -> 25.9 us (0.985)
  waiting for transfers between devices: 6.41 us -> 6.05 us
    ppermute x9, waiting for transfers between devices: 6.41 us -> 6.05 us  [exchange(): lax.ppermute(block, axis, moved(size, stride, count, step, sign))]
  transfers between devices with their start and end apart: 9 -> 9, of which waited for: 4 -> 5; matrix products, arithmetic and copies ran while one was open for 0% -> 0% of each run, Pallas kernels for 12% -> 12%
where the time goes in v7:
time: 25.9 us; the launch traced here: 25.7 us
  starting transfers between devices  13.8 us (53%)
  waiting for transfers between devices  6.05 us (23%)
  Pallas kernels  3.81 us (15%)
  local copies, waits for them, and re-layouts  1.32 us (5%)
  between operations  0.69 us (3%)
    ppermute x9, starting transfers between devices, exchange(): lax.ppermute(block, axis, moved(size, stride, count, step, sign))  13.8 us
    ppermute x9, waiting for transfers between devices, exchange(): lax.ppermute(block, axis, moved(size, stride, count, step, sign))  6.05 us
    pallas_call x1, Pallas kernels, body(): pl.pallas_call(tree_kernel, out_shape=[like(queries), like(out_grad), lik...  1.74 us
    pallas_call x1, Pallas kernels, body(): pl.pallas_call(functools.partial(branch_kernel, parts=groups), out_shape=...  1.28 us
    pallas_call x1, Pallas kernels, body(): pl.pallas_call(functools.partial(prefix_kernel, parts=groups), out_shape=...  0.79 us
    unnamed x7, local copies, waits for them, and re-layouts  0.72 us
    slice x1, local copies, waits for them, and re-layouts, body(): total[:, half:]  0.61 us
  transfers between devices with their start and end apart: 9, of which 5 were waited for; matrix products, arithmetic and copies ran while one was open for 0% of the time, Pallas kernels for 12%

profile of v7, /device:TPU:0, one launch (start us, length us, event | category | flops | bytes accessed | tf_op | source)
XLA Modules:
  0.0 25.7 jit_solution(3781796876141260977)
XLA Ops:
  0.6 0.0 copy-start.2
  0.6 0.7 %constant_dynamic-update-slice_fusion.1 = bf16[16,512]{1,0:T(8,128)(2,1)S(1)} fusion(bf16[16,256]{1,0:T(8,128)(2,1)} %param.11), kind=kLoop, calls=%fused_computation.3 | loop fusion | bytes 16384
  1.3 0.0 copy-done.2
  1.4 0.0 copy-start
  1.4 0.0 copy-start.1
  1.4 5.1 %collective-permute-start = (bf16[16,512]{1,0:T(8,128)(2,1)S(1)}, bf16[16,512]{1,0:T(8,128)(2,1)S(1)}, u32[]{:S(2)}, u32[]{:S(2)}) collective-permute-start(bf16[16,512]{1,0:T(8,128)(2,1)S(1)} %constant_dynamic-update-slice_fusion.refs_6_.refs_8_), channel_id=1, source_target_pairs={{0,24},{8,16},{16,8},{24,0},{1,25},{9,17},{17,9},{25,1},{2,26},{10... | collective-permute-start | bytes 49160 | tf_op jit(solution)/shard_map/ppermute | solution.py:60
  6.5 0.0 collective-permute-start.1
  6.5 0.6 %collective-permute-start.2 = (bf16[16,512]{1,0:T(8,128)(2,1)S(1)}, bf16[16,512]{1,0:T(8,128)(2,1)S(1)}, u32[]{:S(2)}, u32[]{:S(2)}) collective-permute-start(bf16[16,512]{1,0:T(8,128)(2,1)S(1)} %constant_dynamic-update-slice_fusion.refs_6_.refs_8_), channel_id=1, source_target_pairs={{0,8},{8,0},{16,24},{24,16},{1,9},{9,1},{17,25},{25,17},{2,10},{10... | collective-permute-start | bytes 49160 | tf_op jit(solution)/shard_map/ppermute | solution.py:60
  7.1 0.0 copy-done
  7.1 0.0 copy-done.1
  7.1 1.7 %tree.1 = (bf16[2,64,2048]{2,1,0:T(8,128)(2,1)S(1)}, bf16[2,64,2048]{2,1,0:T(8,128)(2,1)S(1)}, bf16[2,64,256]{2,1,0:T(8,128)(2,1)S(1)}, f32[4,64,512]{2,1,0:T(8,...) custom-call(bf16[2,64,2048]{2,1,0:T(8,128)(2,1)} %q_hbm.1, ...), custom_call_target="tpu_custom_call" | custom-call | flops 67108864 | bytes 1048576 | tf_op jit(solution)/shard_map/tree/pallas_call | solution.py:255
  8.9 0.0 collective-permute-done.refs_7_.refs_9_
  8.9 2.2 %collective-permute-done.1.refs_8_.refs_10_ = bf16[16,512]{1,0:T(8,128)(2,1)S(1)} collective-permute-done((bf16[16,512]{1,0:T(8,128)(2,1)S(1)}, bf16[16,512]{1,0:T(8,128)(2,1)S(1)}, u32[]{:S(2)}, u32[]{:S(2)}) %collective-permute-start.1) | collective-permute-done | bytes 16416 | tf_op jit(solution)/shard_map/ppermute | solution.py:60
  11.1 0.0 collective-permute-done.2.refs_9_.refs_11_
  11.1 0.8 %prefix.1 = (bf16[4,64,512]{2,1,0:T(8,128)(2,1)S(1)}, f32[4,1,512]{2,1,0:T(1,128)S(1)}, f32[4,1,512]{2,1,0:T(1,128)S(1)}, f32[16,512]{1,0:T(8,128)S(1)}, bf16[16...) custom-call(bf16[2,64,2048]{2,1,0:T(8,128)(2,1)S(1)} %get-tuple-element.24.refs_0_, ...), custom_call_target="tpu_custom_call" | custom-call | flops 134217728 | tf_op jit(solution)/shard_map/prefix/pallas_call | solution.py:270
  11.9 1.6 %collective-permute-start.3 = (bf16[16,512]{1,0:T(8,128)(2,1)S(1)}, bf16[16,512]{1,0:T(8,128)(2,1)S(1)}, u32[]{:S(2)}, u32[]{:S(2)}) collective-permute-start(bf16[16,512]{1,0:T(8,128)(2,1)S(1)} %get-tuple-element.40), channel_id=1, source_target_pairs={{0,24},{8,16},{16,8},{24,0},{1,25},{9,17},{17,9},{25,1},{2,26},{10... | collective-permute-start | bytes 49160 | tf_op jit(solution)/shard_map/ppermute | solution.py:60
  13.5 0.6 %collective-permute-start.4 = (bf16[16,512]{1,0:T(8,128)(2,1)S(1)}, bf16[16,512]{1,0:T(8,128)(2,1)S(1)}, u32[]{:S(2)}, u32[]{:S(2)}) collective-permute-start(bf16[16,512]{1,0:T(8,128)(2,1)S(1)} %get-tuple-element.41), channel_id=1, source_target_pairs={{0,16},{8,24},{16,0},{24,8},{1,17},{9,25},{17,1},{25,9},{2,18},{10... | collective-permute-start | bytes 49160 | tf_op jit(solution)/shard_map/ppermute | solution.py:60
  14.1 2.3 %collective-permute-start.5 = (bf16[16,512]{1,0:T(8,128)(2,1)S(1)}, bf16[16,512]{1,0:T(8,128)(2,1)S(1)}, u32[]{:S(2)}, u32[]{:S(2)}) collective-permute-start(bf16[16,512]{1,0:T(8,128)(2,1)S(1)} %get-tuple-element.42), channel_id=1, source_target_pairs={{0,8},{8,0},{16,24},{24,16},{1,9},{9,1},{17,25},{25,17},{2,10},{10... | collective-permute-start | bytes 49160 | tf_op jit(solution)/shard_map/ppermute | solution.py:60
  16.4 1.1 %collective-permute-done.3 = bf16[16,512]{1,0:T(8,128)(2,1)S(1)} collective-permute-done((bf16[16,512]{1,0:T(8,128)(2,1)S(1)}, bf16[16,512]{1,0:T(8,128)(2,1)S(1)}, u32[]{:S(2)}, u32[]{:S(2)}) %collective-permute-start.3) | collective-permute-done | bytes 16416 | tf_op jit(solution)/shard_map/ppermute | solution.py:60
  17.5 0.7 %collective-permute-done.4 = bf16[16,512]{1,0:T(8,128)(2,1)S(1)} collective-permute-done((bf16[16,512]{1,0:T(8,128)(2,1)S(1)}, bf16[16,512]{1,0:T(8,128)(2,1)S(1)}, u32[]{:S(2)}, u32[]{:S(2)}) %collective-permute-start.4) | collective-permute-done | bytes 16416 | tf_op jit(solution)/shard_map/ppermute | solution.py:60
  18.3 0.0 collective-permute-done.5
  18.3 2.5 %collective-permute-start.6 = (bf16[16,512]{1,0:T(8,128)(2,1)S(1)}, bf16[16,512]{1,0:T(8,128)(2,1)S(1)}, u32[]{:S(2)}, u32[]{:S(2)}) collective-permute-start(bf16[16,512]{1,0:T(8,128)(2,1)S(1)} %add_convert_fusion.1), channel_id=1, source_target_pairs={{0,6},{2,4},{4,2},{6,0},{1,7},{3,5},{5,3},{7,1},{8,14},{10,12},{12... | collective-permute-start | bytes 49160 | tf_op jit(solution)/shard_map/ppermute | solution.py:60
  20.8 0.5 %collective-permute-start.7 = (bf16[16,512]{1,0:T(8,128)(2,1)S(1)}, bf16[16,512]{1,0:T(8,128)(2,1)S(1)}, u32[]{:S(2)}, u32[]{:S(2)}) collective-permute-start(bf16[16,512]{1,0:T(8,128)(2,1)S(1)} %add_convert_fusion.1), channel_id=1, source_target_pairs={{0,4},{2,6},{4,0},{6,2},{1,5},{3,7},{5,1},{7,3},{8,12},{10,14},{12... | collective-permute-start | bytes 49160 | tf_op jit(solution)/shard_map/ppermute | solution.py:60
  21.3 0.5 %collective-permute-start.8 = (bf16[16,512]{1,0:T(8,128)(2,1)S(1)}, bf16[16,512]{1,0:T(8,128)(2,1)S(1)}, u32[]{:S(2)}, u32[]{:S(2)}) collective-permute-start(bf16[16,512]{1,0:T(8,128)(2,1)S(1)} %add_convert_fusion.1), channel_id=1, source_target_pairs={{0,2},{2,0},{4,6},{6,4},{1,3},{3,1},{5,7},{7,5},{8,10},{10,8},{12,... | collective-permute-start | bytes 49160 | tf_op jit(solution)/shard_map/ppermute | solution.py:60
  21.8 1.3 %branch.1 = (bf16[2,64,2048]{2,1,0:T(8,128)(2,1)}, bf16[2,64,256]{2,1,0:T(8,128)(2,1)}, bf16[2,64,256]{2,1,0:T(8,128)(2,1)}) custom-call(bf16[2,64,2048]{2,1,0:T(8,128)(2,1)S(1)} %get-tuple-element.24.refs_0_, bf16[2,64,2048]{2,1,0:T(8,128)(2,1)S(1)} %get-tuple-element.25.refs_1_, bf16[2,64,256]{2,1,0:T(8,128)(2,1)S(1)} %get-tuple-element.26.refs_2_, ...), custom_call_target="tpu_custom_call" | custom-call | flops 134217728 | bytes 524288 | tf_op jit(solution)/shard_map/branch/pallas_call | solution.py:285
  23.1 0.0 collective-permute-done.6
  23.1 1.4 %collective-permute-done.7 = bf16[16,512]{1,0:T(8,128)(2,1)S(1)} collective-permute-done((bf16[16,512]{1,0:T(8,128)(2,1)S(1)}, bf16[16,512]{1,0:T(8,128)(2,1)S(1)}, u32[]{:S(2)}, u32[]{:S(2)}) %collective-permute-start.7) | collective-permute-done | bytes 16416 | tf_op jit(solution)/shard_map/ppermute | solution.py:60
  24.5 0.5 %collective-permute-done.8 = bf16[16,512]{1,0:T(8,128)(2,1)S(1)} collective-permute-done((bf16[16,512]{1,0:T(8,128)(2,1)S(1)}, bf16[16,512]{1,0:T(8,128)(2,1)S(1)}, u32[]{:S(2)}, u32[]{:S(2)}) %collective-permute-start.8) | collective-permute-done | bytes 16416 | tf_op jit(solution)/shard_map/ppermute | solution.py:60
  25.1 0.6 %fusion = (bf16[16,256]{1,0:T(8,128)(2,1)}, bf16[16,256]{1,0:T(8,128)(2,1)}) fusion(bf16[16,512]{1,0:T(8,128)(2,1)S(1)} %add_convert_fusion), kind=kLoop, calls=%fused_computation.4 | loop fusion | bytes 32768 | tf_op jit(solution)/shard_map/slice | solution.py:300
  (3 shorter events, 0.0 us)
Async XLA Ops:
  0.6 0.7 %copy-start.2 = (bf16[16,256]{1,0:T(8,128)(2,1)S(1)}, bf16[16,256]{1,0:T(8,128)(2,1)}, u32[]{:S(2)}) copy-start(bf16[16,256]{1,0:T(8,128)(2,1)} %param.12) | copy-start | bytes 24580
  1.4 5.8 %copy-start = (s32[2,64]{1,0:T(2,128)S(1)}, s32[2,64]{1,0:T(2,128)}, u32[]{:S(2)}) copy-start(s32[2,64]{1,0:T(2,128)} %par_ref.1) | copy-start | bytes 1540
  1.4 5.8 %copy-start.1 = (s32[2]{0:T(128)S(1)}, s32[2]{0:T(128)}, u32[]{:S(2)}) copy-start(s32[2]{0:T(128)} %param.15) | copy-start | bytes 28
  1.4 7.5 %collective-permute-start = (bf16[16,512]{1,0:T(8,128)(2,1)S(1)}, bf16[16,512]{1,0:T(8,128)(2,1)S(1)}, u32[]{:S(2)}, u32[]{:S(2)}) collective-permute-start(bf16[16,512]{1,0:T(8,128)(2,1)S(1)} %constant_dynamic-update-slice_fusion.refs_6_.refs_8_), channel_id=1, source_target_pairs={{0,24},{8,16},{16,8},{24,0},{1,25},{9,17},{17,9},{25,1},{2,26},{10... | collective-permute-start | bytes 49160 | tf_op jit(solution)/shard_map/ppermute | solution.py:60
  6.5 4.6 %collective-permute-start.1 = (bf16[16,512]{1,0:T(8,128)(2,1)S(1)}, bf16[16,512]{1,0:T(8,128)(2,1)S(1)}, u32[]{:S(2)}, u32[]{:S(2)}) collective-permute-start(bf16[16,512]{1,0:T(8,128)(2,1)S(1)} %constant_dynamic-update-slice_fusion.refs_6_.refs_8_), channel_id=1, source_target_pairs={{0,16},{8,24},{16,0},{24,8},{1,17},{9,25},{17,1},{25,9},{2,18},{10... | collective-permute-start | bytes 49160 | tf_op jit(solution)/shard_map/ppermute | solution.py:60
  6.5 4.6 %collective-permute-start.2 = (bf16[16,512]{1,0:T(8,128)(2,1)S(1)}, bf16[16,512]{1,0:T(8,128)(2,1)S(1)}, u32[]{:S(2)}, u32[]{:S(2)}) collective-permute-start(bf16[16,512]{1,0:T(8,128)(2,1)S(1)} %constant_dynamic-update-slice_fusion.refs_6_.refs_8_), channel_id=1, source_target_pairs={{0,8},{8,0},{16,24},{24,16},{1,9},{9,1},{17,25},{25,17},{2,10},{10... | collective-permute-start | bytes 49160 | tf_op jit(solution)/shard_map/ppermute | solution.py:60
  11.9 5.6 %collective-permute-start.3 = (bf16[16,512]{1,0:T(8,128)(2,1)S(1)}, bf16[16,512]{1,0:T(8,128)(2,1)S(1)}, u32[]{:S(2)}, u32[]{:S(2)}) collective-permute-start(bf16[16,512]{1,0:T(8,128)(2,1)S(1)} %get-tuple-element.40), channel_id=1, source_target_pairs={{0,24},{8,16},{16,8},{24,0},{1,25},{9,17},{17,9},{25,1},{2,26},{10... | collective-permute-start | bytes 49160 | tf_op jit(solution)/shard_map/ppermute | solution.py:60
  13.5 4.7 %collective-permute-start.4 = (bf16[16,512]{1,0:T(8,128)(2,1)S(1)}, bf16[16,512]{1,0:T(8,128)(2,1)S(1)}, u32[]{:S(2)}, u32[]{:S(2)}) collective-permute-start(bf16[16,512]{1,0:T(8,128)(2,1)S(1)} %get-tuple-element.41), channel_id=1, source_target_pairs={{0,16},{8,24},{16,0},{24,8},{1,17},{9,25},{17,1},{25,9},{2,18},{10... | collective-permute-start | bytes 49160 | tf_op jit(solution)/shard_map/ppermute | solution.py:60
  14.1 4.2 %collective-permute-start.5 = (bf16[16,512]{1,0:T(8,128)(2,1)S(1)}, bf16[16,512]{1,0:T(8,128)(2,1)S(1)}, u32[]{:S(2)}, u32[]{:S(2)}) collective-permute-start(bf16[16,512]{1,0:T(8,128)(2,1)S(1)} %get-tuple-element.42), channel_id=1, source_target_pairs={{0,8},{8,0},{16,24},{24,16},{1,9},{9,1},{17,25},{25,17},{2,10},{10... | collective-permute-start | bytes 49160 | tf_op jit(solution)/shard_map/ppermute | solution.py:60
  18.3 4.8 %collective-permute-start.6 = (bf16[16,512]{1,0:T(8,128)(2,1)S(1)}, bf16[16,512]{1,0:T(8,128)(2,1)S(1)}, u32[]{:S(2)}, u32[]{:S(2)}) collective-permute-start(bf16[16,512]{1,0:T(8,128)(2,1)S(1)} %add_convert_fusion.1), channel_id=1, source_target_pairs={{0,6},{2,4},{4,2},{6,0},{1,7},{3,5},{5,3},{7,1},{8,14},{10,12},{12... | collective-permute-start | bytes 49160 | tf_op jit(solution)/shard_map/ppermute | solution.py:60
  20.8 3.7 %collective-permute-start.7 = (bf16[16,512]{1,0:T(8,128)(2,1)S(1)}, bf16[16,512]{1,0:T(8,128)(2,1)S(1)}, u32[]{:S(2)}, u32[]{:S(2)}) collective-permute-start(bf16[16,512]{1,0:T(8,128)(2,1)S(1)} %add_convert_fusion.1), channel_id=1, source_target_pairs={{0,4},{2,6},{4,0},{6,2},{1,5},{3,7},{5,1},{7,3},{8,12},{10,14},{12... | collective-permute-start | bytes 49160 | tf_op jit(solution)/shard_map/ppermute | solution.py:60
  21.3 3.7 %collective-permute-start.8 = (bf16[16,512]{1,0:T(8,128)(2,1)S(1)}, bf16[16,512]{1,0:T(8,128)(2,1)S(1)}, u32[]{:S(2)}, u32[]{:S(2)}) collective-permute-start(bf16[16,512]{1,0:T(8,128)(2,1)S(1)} %add_convert_fusion.1), channel_id=1, source_target_pairs={{0,2},{2,0},{4,6},{6,4},{1,3},{3,1},{5,7},{7,5},{8,10},{10,8},{12,... | collective-permute-start | bytes 49160 | tf_op jit(solution)/shard_map/ppermute | solution.py:60

commit v8 on v7

--- a/solution.py
+++ b/solution.py
@@ -167,39 +167,42 @@
     heads = width // HD
     factor = HD**-0.5
     pre = jnp.concatenate([r[...] for r in pre_refs], axis=0)
+    lanes = lambda ref, h: jnp.concatenate([ref[h * count + b] for b in range(count)], axis=1)
     stage = []
     for h in range(heads):
         low = h * HD
         keys = pre[:, low : low + HD]
         values = pre[:, width + low : width + low + HD]
-        for b in range(count):
-            q = head_rows(q_ref, b, h)
-            g = head_rows(g_ref, b, h)
-            stage.append((q, g, dot(keys, q, NT), dot(values, g, NT)))
+        q = jnp.concatenate([head_rows(q_ref, b, h) for b in range(count)], axis=0)
+        g = jnp.concatenate([head_rows(g_ref, b, h) for b in range(count)], axis=0)
+        stage.append((q, g, dot(keys, q, NT), dot(values, g, NT)))
     ready = []
-    for i, (q, g, scores, dweights) in enumerate(stage):
+    for h, (q, g, scores, dweights) in enumerate(stage):
         scores = scores * (factor * LOG2E)
-        tree_max = max_ref[i]
+        tree_max = lanes(max_ref, h)
         top = jnp.maximum(jnp.max(scores, axis=0, keepdims=True), tree_max)
         powers = jnp.exp2(scores - top)
         tree = jnp.exp2(tree_max - top)
-        scale = live_ref[i] / (jnp.sum(powers, axis=0, keepdims=True) + tree * sum_ref[i])
-        delta = scale * (jnp.sum(powers * dweights, axis=0, keepdims=True) + tree * dot_ref[i])
+        scale = lanes(live_ref, h) / (
+            jnp.sum(powers, axis=0, keepdims=True) + tree * lanes(sum_ref, h)
+        )
+        delta = scale * (
+            jnp.sum(powers * dweights, axis=0, keepdims=True) + tree * lanes(dot_ref, h)
+        )
         weights = powers * scale
         dscores = (weights * (dweights - delta)).astype(jnp.bfloat16)
-        dscore_ref[i] = dscores
-        scale_ref[i] = scale * tree
-        delta_ref[i] = delta
+        tree_scale = scale * tree
+        wide = scores.shape[1] // count
+        for b in range(count):
+            i, cols = h * count + b, slice(b * wide, (b + 1) * wide)
+            dscore_ref[i] = dscores[:, cols]
+            scale_ref[i] = tree_scale[:, cols]
+            delta_ref[i] = delta[:, cols]
         ready.append((weights.astype(jnp.bfloat16), dscores))
     for h in range(heads):
         low = h * HD
-        key_sum = value_sum = None
-        for b in range(count):
-            i = h * count + b
-            value_grad = dot(ready[i][0], stage[i][1], NN)
-            key_grad = dot(ready[i][1], stage[i][0], NN) * factor
-            key_sum = key_grad if b == 0 else key_sum + key_grad
-            value_sum = value_grad if b == 0 else value_sum + value_grad
+        value_sum = dot(ready[h][0], stage[h][1], NN)
+        key_sum = dot(ready[h][1], stage[h][0], NN) * factor
         for i, ref in enumerate(out_refs):
             ref[:, low : low + HD] = key_sum[i * rows : (i + 1) * rows].astype(ref.dtype)
             ref[:, width + low : width + low + HD] = value_sum[i * rows : (i + 1) * rows].astype(
@@ -215,23 +218,25 @@
     heads = bk_ref.shape[2] // HD
     factor = HD**-0.5
     pre = jnp.concatenate([r[:, : heads * HD] for r in pre_refs], axis=0)
+    ready = []
+    for i in range(heads * count):
+        weights = power_ref[i] * scale_ref[i]
+        dscores = (weights * (dweight_ref[i] - delta_ref[i])).astype(jnp.bfloat16)
+        ready.append((dscores, weights.astype(jnp.bfloat16)))
     for h in range(heads):
         low = h * HD
         for b in range(count):
-            i = h * count + b
-            weights = power_ref[i] * scale_ref[i]
-            dscores = (weights * (dweight_ref[i] - delta_ref[i])).astype(jnp.bfloat16)
-            tree_keys = bk_ref[b, :, low : low + HD]
-            value_grad = dot(weights.astype(jnp.bfloat16), head_rows(g_ref, b, h), NN)
-            key_grad = dot(dscores, head_rows(q_ref, b, h), NN) * factor
-            dbk_ref[b, :, low : low + HD] = key_grad.astype(jnp.bfloat16)
-            dbv_ref[b, :, low : low + HD] = value_grad.astype(jnp.bfloat16)
-            both = jnp.concatenate([dscore_ref[i], dscores], axis=0)
-            keys = jnp.concatenate([pre[:, low : low + HD], tree_keys], axis=0)
+            dscores, weights = ready[h * count + b]
+            both = jnp.concatenate([dscore_ref[h * count + b], dscores], axis=0)
+            keys = jnp.concatenate([pre[:, low : low + HD], bk_ref[b, :, low : low + HD]], axis=0)
             query_grad = (dot(both, keys, TN) * factor).astype(jnp.bfloat16)
             for m in range(PER):
                 col = (h * PER + m) * HD
                 dq_ref[b, :, col : col + HD] = query_grad[m * length : (m + 1) * length]
+            value_grad = dot(weights, head_rows(g_ref, b, h), NN)
+            key_grad = dot(dscores, head_rows(q_ref, b, h), NN) * factor
+            dbk_ref[b, :, low : low + HD] = key_grad.astype(jnp.bfloat16)
+            dbv_ref[b, :, low : low + HD] = value_grad.astype(jnp.bfloat16)
 
 
 def body(

time: 25.9 us -> 25.9 us (level)
  no operation moved by 1% of the time
where the time goes in v8:
time: 25.9 us; the launch traced here: 25.6 us
  starting transfers between devices  13.8 us (53%)
  waiting for transfers between devices  6.05 us (23%)
  Pallas kernels  3.77 us (15%)
  local copies, waits for them, and re-layouts  1.32 us (5%)
  between operations  0.68 us (3%)
    ppermute x9, starting transfers between devices, exchange(): lax.ppermute(block, axis, moved(size, stride, count, step, sign))  13.8 us
    ppermute x9, waiting for transfers between devices, exchange(): lax.ppermute(block, axis, moved(size, stride, count, step, sign))  6.05 us
    pallas_call x1, Pallas kernels, body(): pl.pallas_call(tree_kernel, out_shape=[like(queries), like(out_grad), lik...  1.74 us
    pallas_call x1, Pallas kernels, body(): pl.pallas_call(functools.partial(branch_kernel, parts=groups), out_shape=...  1.28 us
    pallas_call x1, Pallas kernels, body(): pl.pallas_call(functools.partial(prefix_kernel, parts=groups), out_shape=...  0.75 us
    unnamed x7, local copies, waits for them, and re-layouts  0.72 us
    slice x1, local copies, waits for them, and re-layouts, body(): total[:, half:]  0.61 us
  transfers between devices with their start and end apart: 9, of which 5 were waited for; matrix products, arithmetic and copies ran while one was open for 0% of the time, Pallas kernels for 12%

profile of v8, /device:TPU:0, one launch (start us, length us, event | category | flops | bytes accessed | tf_op | source)
XLA Modules:
  0.0 25.6 jit_solution(3821149254741599372)
XLA Ops:
  0.6 0.0 copy-start.2
  0.6 0.7 %constant_dynamic-update-slice_fusion.1 = bf16[16,512]{1,0:T(8,128)(2,1)S(1)} fusion(bf16[16,256]{1,0:T(8,128)(2,1)} %param.11), kind=kLoop, calls=%fused_computation.3 | loop fusion | bytes 16384
  1.3 0.0 copy-done.2
  1.4 0.0 copy-start
  1.4 0.0 copy-start.1
  1.4 5.1 %collective-permute-start = (bf16[16,512]{1,0:T(8,128)(2,1)S(1)}, bf16[16,512]{1,0:T(8,128)(2,1)S(1)}, u32[]{:S(2)}, u32[]{:S(2)}) collective-permute-start(bf16[16,512]{1,0:T(8,128)(2,1)S(1)} %constant_dynamic-update-slice_fusion.refs_6_.refs_8_), channel_id=1, source_target_pairs={{0,24},{8,16},{16,8},{24,0},{1,25},{9,17},{17,9},{25,1},{2,26},{10... | collective-permute-start | bytes 49160 | tf_op jit(solution)/shard_map/ppermute | solution.py:60
  6.5 0.0 collective-permute-start.1
  6.5 0.6 %collective-permute-start.2 = (bf16[16,512]{1,0:T(8,128)(2,1)S(1)}, bf16[16,512]{1,0:T(8,128)(2,1)S(1)}, u32[]{:S(2)}, u32[]{:S(2)}) collective-permute-start(bf16[16,512]{1,0:T(8,128)(2,1)S(1)} %constant_dynamic-update-slice_fusion.refs_6_.refs_8_), channel_id=1, source_target_pairs={{0,8},{8,0},{16,24},{24,16},{1,9},{9,1},{17,25},{25,17},{2,10},{10... | collective-permute-start | bytes 49160 | tf_op jit(solution)/shard_map/ppermute | solution.py:60
  7.1 0.0 copy-done
  7.1 0.0 copy-done.1
  7.1 1.7 %tree.1 = (bf16[2,64,2048]{2,1,0:T(8,128)(2,1)S(1)}, bf16[2,64,2048]{2,1,0:T(8,128)(2,1)S(1)}, bf16[2,64,256]{2,1,0:T(8,128)(2,1)S(1)}, f32[4,64,512]{2,1,0:T(8,...) custom-call(bf16[2,64,2048]{2,1,0:T(8,128)(2,1)} %q_hbm.1, ...), custom_call_target="tpu_custom_call" | custom-call | flops 67108864 | bytes 1048576 | tf_op jit(solution)/shard_map/tree/pallas_call | solution.py:260
  8.9 0.0 collective-permute-done.refs_7_.refs_9_
  8.9 2.2 %collective-permute-done.1.refs_8_.refs_10_ = bf16[16,512]{1,0:T(8,128)(2,1)S(1)} collective-permute-done((bf16[16,512]{1,0:T(8,128)(2,1)S(1)}, bf16[16,512]{1,0:T(8,128)(2,1)S(1)}, u32[]{:S(2)}, u32[]{:S(2)}) %collective-permute-start.1) | collective-permute-done | bytes 16416 | tf_op jit(solution)/shard_map/ppermute | solution.py:60
  11.1 0.0 collective-permute-done.2.refs_9_.refs_11_
  11.1 0.8 %prefix.1 = (bf16[4,64,512]{2,1,0:T(8,128)(2,1)S(1)}, f32[4,1,512]{2,1,0:T(1,128)S(1)}, f32[4,1,512]{2,1,0:T(1,128)S(1)}, f32[16,512]{1,0:T(8,128)S(1)}, bf16[16...) custom-call(bf16[2,64,2048]{2,1,0:T(8,128)(2,1)S(1)} %get-tuple-element.24.refs_0_, ...), custom_call_target="tpu_custom_call" | custom-call | flops 134217728 | tf_op jit(solution)/shard_map/prefix/pallas_call | solution.py:275
  11.9 1.6 %collective-permute-start.3 = (bf16[16,512]{1,0:T(8,128)(2,1)S(1)}, bf16[16,512]{1,0:T(8,128)(2,1)S(1)}, u32[]{:S(2)}, u32[]{:S(2)}) collective-permute-start(bf16[16,512]{1,0:T(8,128)(2,1)S(1)} %get-tuple-element.40), channel_id=1, source_target_pairs={{0,24},{8,16},{16,8},{24,0},{1,25},{9,17},{17,9},{25,1},{2,26},{10... | collective-permute-start | bytes 49160 | tf_op jit(solution)/shard_map/ppermute | solution.py:60
  13.5 0.6 %collective-permute-start.4 = (bf16[16,512]{1,0:T(8,128)(2,1)S(1)}, bf16[16,512]{1,0:T(8,128)(2,1)S(1)}, u32[]{:S(2)}, u32[]{:S(2)}) collective-permute-start(bf16[16,512]{1,0:T(8,128)(2,1)S(1)} %get-tuple-element.41), channel_id=1, source_target_pairs={{0,16},{8,24},{16,0},{24,8},{1,17},{9,25},{17,1},{25,9},{2,18},{10... | collective-permute-start | bytes 49160 | tf_op jit(solution)/shard_map/ppermute | solution.py:60
  14.0 2.3 %collective-permute-start.5 = (bf16[16,512]{1,0:T(8,128)(2,1)S(1)}, bf16[16,512]{1,0:T(8,128)(2,1)S(1)}, u32[]{:S(2)}, u32[]{:S(2)}) collective-permute-start(bf16[16,512]{1,0:T(8,128)(2,1)S(1)} %get-tuple-element.42), channel_id=1, source_target_pairs={{0,8},{8,0},{16,24},{24,16},{1,9},{9,1},{17,25},{25,17},{2,10},{10... | collective-permute-start | bytes 49160 | tf_op jit(solution)/shard_map/ppermute | solution.py:60
  16.3 1.1 %collective-permute-done.3 = bf16[16,512]{1,0:T(8,128)(2,1)S(1)} collective-permute-done((bf16[16,512]{1,0:T(8,128)(2,1)S(1)}, bf16[16,512]{1,0:T(8,128)(2,1)S(1)}, u32[]{:S(2)}, u32[]{:S(2)}) %collective-permute-start.3) | collective-permute-done | bytes 16416 | tf_op jit(solution)/shard_map/ppermute | solution.py:60
  17.5 0.7 %collective-permute-done.4 = bf16[16,512]{1,0:T(8,128)(2,1)S(1)} collective-permute-done((bf16[16,512]{1,0:T(8,128)(2,1)S(1)}, bf16[16,512]{1,0:T(8,128)(2,1)S(1)}, u32[]{:S(2)}, u32[]{:S(2)}) %collective-permute-start.4) | collective-permute-done | bytes 16416 | tf_op jit(solution)/shard_map/ppermute | solution.py:60
  18.2 0.0 collective-permute-done.5
  18.2 2.5 %collective-permute-start.6 = (bf16[16,512]{1,0:T(8,128)(2,1)S(1)}, bf16[16,512]{1,0:T(8,128)(2,1)S(1)}, u32[]{:S(2)}, u32[]{:S(2)}) collective-permute-start(bf16[16,512]{1,0:T(8,128)(2,1)S(1)} %add_convert_fusion.1), channel_id=1, source_target_pairs={{0,6},{2,4},{4,2},{6,0},{1,7},{3,5},{5,3},{7,1},{8,14},{10,12},{12... | collective-permute-start | bytes 49160 | tf_op jit(solution)/shard_map/ppermute | solution.py:60
  20.7 0.5 %collective-permute-start.7 = (bf16[16,512]{1,0:T(8,128)(2,1)S(1)}, bf16[16,512]{1,0:T(8,128)(2,1)S(1)}, u32[]{:S(2)}, u32[]{:S(2)}) collective-permute-start(bf16[16,512]{1,0:T(8,128)(2,1)S(1)} %add_convert_fusion.1), channel_id=1, source_target_pairs={{0,4},{2,6},{4,0},{6,2},{1,5},{3,7},{5,1},{7,3},{8,12},{10,14},{12... | collective-permute-start | bytes 49160 | tf_op jit(solution)/shard_map/ppermute | solution.py:60
  21.3 0.5 %collective-permute-start.8 = (bf16[16,512]{1,0:T(8,128)(2,1)S(1)}, bf16[16,512]{1,0:T(8,128)(2,1)S(1)}, u32[]{:S(2)}, u32[]{:S(2)}) collective-permute-start(bf16[16,512]{1,0:T(8,128)(2,1)S(1)} %add_convert_fusion.1), channel_id=1, source_target_pairs={{0,2},{2,0},{4,6},{6,4},{1,3},{3,1},{5,7},{7,5},{8,10},{10,8},{12,... | collective-permute-start | bytes 49160 | tf_op jit(solution)/shard_map/ppermute | solution.py:60
  21.8 1.3 %branch.1 = (bf16[2,64,2048]{2,1,0:T(8,128)(2,1)}, bf16[2,64,256]{2,1,0:T(8,128)(2,1)}, bf16[2,64,256]{2,1,0:T(8,128)(2,1)}) custom-call(bf16[2,64,2048]{2,1,0:T(8,128)(2,1)S(1)} %get-tuple-element.24.refs_0_, bf16[2,64,2048]{2,1,0:T(8,128)(2,1)S(1)} %get-tuple-element.25.refs_1_, bf16[2,64,256]{2,1,0:T(8,128)(2,1)S(1)} %get-tuple-element.26.refs_2_, ...), custom_call_target="tpu_custom_call" | custom-call | flops 134217728 | bytes 524288 | tf_op jit(solution)/shard_map/branch/pallas_call | solution.py:290
  23.1 0.0 collective-permute-done.6
  23.1 1.4 %collective-permute-done.7 = bf16[16,512]{1,0:T(8,128)(2,1)S(1)} collective-permute-done((bf16[16,512]{1,0:T(8,128)(2,1)S(1)}, bf16[16,512]{1,0:T(8,128)(2,1)S(1)}, u32[]{:S(2)}, u32[]{:S(2)}) %collective-permute-start.7) | collective-permute-done | bytes 16416 | tf_op jit(solution)/shard_map/ppermute | solution.py:60
  24.5 0.5 %collective-permute-done.8 = bf16[16,512]{1,0:T(8,128)(2,1)S(1)} collective-permute-done((bf16[16,512]{1,0:T(8,128)(2,1)S(1)}, bf16[16,512]{1,0:T(8,128)(2,1)S(1)}, u32[]{:S(2)}, u32[]{:S(2)}) %collective-permute-start.8) | collective-permute-done | bytes 16416 | tf_op jit(solution)/shard_map/ppermute | solution.py:60
  25.0 0.6 %fusion = (bf16[16,256]{1,0:T(8,128)(2,1)}, bf16[16,256]{1,0:T(8,128)(2,1)}) fusion(bf16[16,512]{1,0:T(8,128)(2,1)S(1)} %add_convert_fusion), kind=kLoop, calls=%fused_computation.4 | loop fusion | bytes 32768 | tf_op jit(solution)/shard_map/slice | solution.py:305
  (3 shorter events, 0.0 us)
Async XLA Ops:
  0.6 0.7 %copy-start.2 = (bf16[16,256]{1,0:T(8,128)(2,1)S(1)}, bf16[16,256]{1,0:T(8,128)(2,1)}, u32[]{:S(2)}) copy-start(bf16[16,256]{1,0:T(8,128)(2,1)} %param.12) | copy-start | bytes 24580
  1.4 5.8 %copy-start = (s32[2,64]{1,0:T(2,128)S(1)}, s32[2,64]{1,0:T(2,128)}, u32[]{:S(2)}) copy-start(s32[2,64]{1,0:T(2,128)} %par_ref.1) | copy-start | bytes 1540
  1.4 5.8 %copy-start.1 = (s32[2]{0:T(128)S(1)}, s32[2]{0:T(128)}, u32[]{:S(2)}) copy-start(s32[2]{0:T(128)} %param.15) | copy-start | bytes 28
  1.4 7.5 %collective-permute-start = (bf16[16,512]{1,0:T(8,128)(2,1)S(1)}, bf16[16,512]{1,0:T(8,128)(2,1)S(1)}, u32[]{:S(2)}, u32[]{:S(2)}) collective-permute-start(bf16[16,512]{1,0:T(8,128)(2,1)S(1)} %constant_dynamic-update-slice_fusion.refs_6_.refs_8_), channel_id=1, source_target_pairs={{0,24},{8,16},{16,8},{24,0},{1,25},{9,17},{17,9},{25,1},{2,26},{10... | collective-permute-start | bytes 49160 | tf_op jit(solution)/shard_map/ppermute | solution.py:60
  6.5 4.6 %collective-permute-start.1 = (bf16[16,512]{1,0:T(8,128)(2,1)S(1)}, bf16[16,512]{1,0:T(8,128)(2,1)S(1)}, u32[]{:S(2)}, u32[]{:S(2)}) collective-permute-start(bf16[16,512]{1,0:T(8,128)(2,1)S(1)} %constant_dynamic-update-slice_fusion.refs_6_.refs_8_), channel_id=1, source_target_pairs={{0,16},{8,24},{16,0},{24,8},{1,17},{9,25},{17,1},{25,9},{2,18},{10... | collective-permute-start | bytes 49160 | tf_op jit(solution)/shard_map/ppermute | solution.py:60
  6.5 4.6 %collective-permute-start.2 = (bf16[16,512]{1,0:T(8,128)(2,1)S(1)}, bf16[16,512]{1,0:T(8,128)(2,1)S(1)}, u32[]{:S(2)}, u32[]{:S(2)}) collective-permute-start(bf16[16,512]{1,0:T(8,128)(2,1)S(1)} %constant_dynamic-update-slice_fusion.refs_6_.refs_8_), channel_id=1, source_target_pairs={{0,8},{8,0},{16,24},{24,16},{1,9},{9,1},{17,25},{25,17},{2,10},{10... | collective-permute-start | bytes 49160 | tf_op jit(solution)/shard_map/ppermute | solution.py:60
  11.9 5.6 %collective-permute-start.3 = (bf16[16,512]{1,0:T(8,128)(2,1)S(1)}, bf16[16,512]{1,0:T(8,128)(2,1)S(1)}, u32[]{:S(2)}, u32[]{:S(2)}) collective-permute-start(bf16[16,512]{1,0:T(8,128)(2,1)S(1)} %get-tuple-element.40), channel_id=1, source_target_pairs={{0,24},{8,16},{16,8},{24,0},{1,25},{9,17},{17,9},{25,1},{2,26},{10... | collective-permute-start | bytes 49160 | tf_op jit(solution)/shard_map/ppermute | solution.py:60
  13.5 4.7 %collective-permute-start.4 = (bf16[16,512]{1,0:T(8,128)(2,1)S(1)}, bf16[16,512]{1,0:T(8,128)(2,1)S(1)}, u32[]{:S(2)}, u32[]{:S(2)}) collective-permute-start(bf16[16,512]{1,0:T(8,128)(2,1)S(1)} %get-tuple-element.41), channel_id=1, source_target_pairs={{0,16},{8,24},{16,0},{24,8},{1,17},{9,25},{17,1},{25,9},{2,18},{10... | collective-permute-start | bytes 49160 | tf_op jit(solution)/shard_map/ppermute | solution.py:60
  14.0 4.2 %collective-permute-start.5 = (bf16[16,512]{1,0:T(8,128)(2,1)S(1)}, bf16[16,512]{1,0:T(8,128)(2,1)S(1)}, u32[]{:S(2)}, u32[]{:S(2)}) collective-permute-start(bf16[16,512]{1,0:T(8,128)(2,1)S(1)} %get-tuple-element.42), channel_id=1, source_target_pairs={{0,8},{8,0},{16,24},{24,16},{1,9},{9,1},{17,25},{25,17},{2,10},{10... | collective-permute-start | bytes 49160 | tf_op jit(solution)/shard_map/ppermute | solution.py:60
  18.2 4.8 %collective-permute-start.6 = (bf16[16,512]{1,0:T(8,128)(2,1)S(1)}, bf16[16,512]{1,0:T(8,128)(2,1)S(1)}, u32[]{:S(2)}, u32[]{:S(2)}) collective-permute-start(bf16[16,512]{1,0:T(8,128)(2,1)S(1)} %add_convert_fusion.1), channel_id=1, source_target_pairs={{0,6},{2,4},{4,2},{6,0},{1,7},{3,5},{5,3},{7,1},{8,14},{10,12},{12... | collective-permute-start | bytes 49160 | tf_op jit(solution)/shard_map/ppermute | solution.py:60
  20.7 3.7 %collective-permute-start.7 = (bf16[16,512]{1,0:T(8,128)(2,1)S(1)}, bf16[16,512]{1,0:T(8,128)(2,1)S(1)}, u32[]{:S(2)}, u32[]{:S(2)}) collective-permute-start(bf16[16,512]{1,0:T(8,128)(2,1)S(1)} %add_convert_fusion.1), channel_id=1, source_target_pairs={{0,4},{2,6},{4,0},{6,2},{1,5},{3,7},{5,1},{7,3},{8,12},{10,14},{12... | collective-permute-start | bytes 49160 | tf_op jit(solution)/shard_map/ppermute | solution.py:60
  21.3 3.7 %collective-permute-start.8 = (bf16[16,512]{1,0:T(8,128)(2,1)S(1)}, bf16[16,512]{1,0:T(8,128)(2,1)S(1)}, u32[]{:S(2)}, u32[]{:S(2)}) collective-permute-start(bf16[16,512]{1,0:T(8,128)(2,1)S(1)} %add_convert_fusion.1), channel_id=1, source_target_pairs={{0,2},{2,0},{4,6},{6,4},{1,3},{3,1},{5,7},{7,5},{8,10},{10,8},{12,... | collective-permute-start | bytes 49160 | tf_op jit(solution)/shard_map/ppermute | solution.py:60

commit v9 on v7

--- a/solution.py
+++ b/solution.py
@@ -12,7 +12,8 @@
 HD = 128
 PER = QH // KVH
 RADIX = 4
-GATHER = (3, 2, 1)
+CYCLES = {1: (1, 3, 0, 2), 2: (3, 2, 1, 0), 3: (2, 0, 3, 1)}
+GATHER = (1, 2, 3)
 SCATTER = (3, 2, 1)
 SUM = (3, 2, 1)
 LOG2E = 1.4426950408889634
@@ -42,10 +43,13 @@
     pairs = []
     for i in range(size):
         digit = (i // stride) % count
-        if count & (count - 1) == 0:
+        if count == 4 and sign:
+            cycle = CYCLES[step]
+            other = cycle[digit] if sign > 0 else cycle.index(digit)
+        elif count & (count - 1) == 0:
             other = digit ^ step
         else:
-            other = (digit + sign * step) % count
+            other = (digit + (sign or 1) * step) % count
         pairs.append((i, i + (other - digit) * stride))
     return pairs
 
@@ -68,7 +72,13 @@
         low = len(parts)
         block = x if low == 1 else jnp.stack(parts)
         steps = in_order(count, GATHER)
-        for got in exchange([block] * (count - 1), axis, size, stride, steps, 1):
+        gots = exchange([block] * (count - 1), axis, size, stride, steps, 1)
+        if count == 4:
+            one, two, three = lax.optimization_barrier(tuple(gots))
+            digit = lax.axis_index(axis) // stride % count
+            outer = (digit == 0) | (digit == 3)
+            gots = [two, jnp.where(outer, one, three), jnp.where(outer, three, one)]
+        for got in gots:
             parts += [got] if low == 1 else [got[i] for i in range(low)]
     return parts
 
@@ -86,9 +96,9 @@
         blocks = parts if low == 1 else [
             jnp.stack(parts[i * low : (i + 1) * low]) for i in range(count)
         ]
-        found = dict(zip(in_order(count, GATHER), blocks[1:]))
+        found = dict(zip(in_order(count, SCATTER if count == 4 else GATHER), blocks[1:]))
         steps = in_order(count, SCATTER)
-        terms = blocks[:1] + exchange([found[s] for s in steps], axis, size, stride, steps, -1)
+        terms = blocks[:1] + exchange([found[s] for s in steps], axis, size, stride, steps, 0 if count == 4 else -1)
         total = tree_sum([t.astype(jnp.float32) for t in terms])
         parts = [total] if low == 1 else [total[i] for i in range(low)]
     return parts[0]
@@ -98,7 +108,7 @@
     for stride, count in digits(size):
         steps = in_order(count, SUM)
         sent = x.astype(jnp.bfloat16)
-        terms = [sent] + exchange([sent] * (count - 1), axis, size, stride, steps, 1)
+        terms = [sent] + exchange([sent] * (count - 1), axis, size, stride, steps, 0)
         x = tree_sum([t.astype(jnp.float32) for t in terms])
     return x
 

time: 25.9 us -> 25.8 us (level)
  waiting for transfers between devices: 6.05 us -> 3.82 us
  starting transfers between devices: 13.8 us -> 15.1 us
  local copies, waits for them, and re-layouts: 1.32 us -> 2 us
    ppermute x9, waiting for transfers between devices: 6.05 us -> 3.82 us  [exchange(): lax.ppermute(block, axis, moved(size, stride, count, step, sign))]
    ppermute x9, starting transfers between devices: 13.8 us -> 15.1 us  [exchange(): lax.ppermute(block, axis, moved(size, stride, count, step, sign))]
    unnamed x7, local copies, waits for them, and re-layouts: 0.72 us -> 1.39 us
  transfers between devices with their start and end apart: 9 -> 9, of which waited for: 5 -> 4; matrix products, arithmetic and copies ran while one was open for 0% -> 0% of each run, Pallas kernels for 12% -> 12%
where the time goes in v9:
time: 25.8 us; the launch traced here: 25.5 us
  starting transfers between devices  15.1 us (59%)
  Pallas kernels  3.82 us (15%)
  waiting for transfers between devices  3.82 us (15%)
  local copies, waits for them, and re-layouts  2 us (8%)
  between operations  0.7 us (3%)
    ppermute x9, starting transfers between devices, exchange(): lax.ppermute(block, axis, moved(size, stride, count, step, sign))  15.1 us
    ppermute x9, waiting for transfers between devices, exchange(): lax.ppermute(block, axis, moved(size, stride, count, step, sign))  3.82 us
    pallas_call x1, Pallas kernels, body(): pl.pallas_call(tree_kernel, out_shape=[like(queries), like(out_grad), lik...  1.74 us
    unnamed x7, local copies, waits for them, and re-layouts  1.39 us
    pallas_call x1, Pallas kernels, body(): pl.pallas_call(functools.partial(branch_kernel, parts=groups), out_shape=...  1.28 us
    pallas_call x1, Pallas kernels, body(): pl.pallas_call(functools.partial(prefix_kernel, parts=groups), out_shape=...  0.8 us
    slice x1, local copies, waits for them, and re-layouts, body(): total[:, half:]  0.61 us
  transfers between devices with their start and end apart: 9, of which 4 were waited for; matrix products, arithmetic and copies ran while one was open for 0% of the time, Pallas kernels for 12%

profile of v9, /device:TPU:0, one launch (start us, length us, event | category | flops | bytes accessed | tf_op | source)
XLA Modules:
  0.0 25.5 jit_solution(8709533846849105295)
XLA Ops:
  0.6 0.0 copy-start.2
  0.6 0.7 %constant_dynamic-update-slice_fusion.1 = bf16[16,512]{1,0:T(8,128)(2,1)S(1)} fusion(bf16[16,256]{1,0:T(8,128)(2,1)} %param.11), kind=kLoop, calls=%fused_computation.5 | loop fusion | bytes 16384
  1.3 0.0 copy-done.2
  1.4 3.0 %collective-permute-start = (bf16[16,512]{1,0:T(8,128)(2,1)S(1)}, bf16[16,512]{1,0:T(8,128)(2,1)S(1)}, u32[]{:S(2)}, u32[]{:S(2)}) collective-permute-start(bf16[16,512]{1,0:T(8,128)(2,1)S(1)} %constant_dynamic-update-slice_fusion.refs_6_.refs_8_), channel_id=1, source_target_pairs={{0,8},{8,24},{16,0},{24,16},{1,9},{9,25},{17,1},{25,17},{2,10},{10... | collective-permute-start | bytes 49160 | tf_op jit(solution)/shard_map/ppermute | solution.py:64
  4.4 2.5 %collective-permute-start.1 = (bf16[16,512]{1,0:T(8,128)(2,1)S(1)}, bf16[16,512]{1,0:T(8,128)(2,1)S(1)}, u32[]{:S(2)}, u32[]{:S(2)}) collective-permute-start(bf16[16,512]{1,0:T(8,128)(2,1)S(1)} %constant_dynamic-update-slice_fusion.refs_6_.refs_8_), channel_id=1, source_target_pairs={{0,24},{8,16},{16,8},{24,0},{1,25},{9,17},{17,9},{25,1},{2,26},{10... | collective-permute-start | bytes 49160 | tf_op jit(solution)/shard_map/ppermute | solution.py:64
  6.8 1.6 %collective-permute-start.2 = (bf16[16,512]{1,0:T(8,128)(2,1)S(1)}, bf16[16,512]{1,0:T(8,128)(2,1)S(1)}, u32[]{:S(2)}, u32[]{:S(2)}) collective-permute-start(bf16[16,512]{1,0:T(8,128)(2,1)S(1)} %constant_dynamic-update-slice_fusion.refs_6_.refs_8_), channel_id=1, source_target_pairs={{0,16},{8,0},{16,24},{24,8},{1,17},{9,1},{17,25},{25,9},{2,18},{10... | collective-permute-start | bytes 49160 | tf_op jit(solution)/shard_map/ppermute | solution.py:64
  8.4 0.0 copy-start
  8.4 0.0 copy-start.1
  8.4 0.7 %copy-done = s32[2,64]{1,0:T(2,128)S(1)} copy-done((s32[2,64]{1,0:T(2,128)S(1)}, s32[2,64]{1,0:T(2,128)}, u32[]{:S(2)}) %copy-start) | copy-done | bytes 536
  9.1 0.0 copy-done.1
  9.1 1.7 %tree.1 = (bf16[2,64,2048]{2,1,0:T(8,128)(2,1)S(1)}, bf16[2,64,2048]{2,1,0:T(8,128)(2,1)S(1)}, bf16[2,64,256]{2,1,0:T(8,128)(2,1)S(1)}, f32[4,64,512]{2,1,0:T(8,...) custom-call(bf16[2,64,2048]{2,1,0:T(8,128)(2,1)} %q_hbm.1, ...), custom_call_target="tpu_custom_call" | custom-call | flops 67108864 | bytes 1048576 | tf_op jit(solution)/shard_map/tree/pallas_call | solution.py:265
  10.9 0.0 collective-permute-done
  10.9 0.0 collective-permute-done.1.refs_7_.refs_9_
  10.9 0.0 collective-permute-done.2
  10.9 0.8 %prefix.1 = (bf16[4,64,512]{2,1,0:T(8,128)(2,1)S(1)}, f32[4,1,512]{2,1,0:T(1,128)S(1)}, f32[4,1,512]{2,1,0:T(1,128)S(1)}, f32[16,512]{1,0:T(8,128)S(1)}, bf16[16...) custom-call(bf16[2,64,2048]{2,1,0:T(8,128)(2,1)S(1)} %get-tuple-element.27.refs_0_, ...), custom_call_target="tpu_custom_call" | custom-call | flops 134217728 | tf_op jit(solution)/shard_map/prefix/pallas_call | solution.py:280
  11.7 1.6 %collective-permute-start.3 = (bf16[16,512]{1,0:T(8,128)(2,1)S(1)}, bf16[16,512]{1,0:T(8,128)(2,1)S(1)}, u32[]{:S(2)}, u32[]{:S(2)}) collective-permute-start(bf16[16,512]{1,0:T(8,128)(2,1)S(1)} %get-tuple-element.46), channel_id=1, source_target_pairs={{0,24},{8,16},{16,8},{24,0},{1,25},{9,17},{17,9},{25,1},{2,26},{10... | collective-permute-start | bytes 49160 | tf_op jit(solution)/shard_map/ppermute | solution.py:64
  13.3 0.7 %collective-permute-start.4 = (bf16[16,512]{1,0:T(8,128)(2,1)S(1)}, bf16[16,512]{1,0:T(8,128)(2,1)S(1)}, u32[]{:S(2)}, u32[]{:S(2)}) collective-permute-start(bf16[16,512]{1,0:T(8,128)(2,1)S(1)} %get-tuple-element.47), channel_id=1, source_target_pairs={{0,16},{8,24},{16,0},{24,8},{1,17},{9,25},{17,1},{25,9},{2,18},{10... | collective-permute-start | bytes 49160 | tf_op jit(solution)/shard_map/ppermute | solution.py:64
  14.0 2.1 %collective-permute-start.5 = (bf16[16,512]{1,0:T(8,128)(2,1)S(1)}, bf16[16,512]{1,0:T(8,128)(2,1)S(1)}, u32[]{:S(2)}, u32[]{:S(2)}) collective-permute-start(bf16[16,512]{1,0:T(8,128)(2,1)S(1)} %get-tuple-element.48), channel_id=1, source_target_pairs={{0,8},{8,0},{16,24},{24,16},{1,9},{9,1},{17,25},{25,17},{2,10},{10... | collective-permute-start | bytes 49160 | tf_op jit(solution)/shard_map/ppermute | solution.py:64
  16.2 1.1 %collective-permute-done.3 = bf16[16,512]{1,0:T(8,128)(2,1)S(1)} collective-permute-done((bf16[16,512]{1,0:T(8,128)(2,1)S(1)}, bf16[16,512]{1,0:T(8,128)(2,1)S(1)}, u32[]{:S(2)}, u32[]{:S(2)}) %collective-permute-start.3) | collective-permute-done | bytes 16416 | tf_op jit(solution)/shard_map/ppermute | solution.py:64
  17.3 0.7 %collective-permute-done.4 = bf16[16,512]{1,0:T(8,128)(2,1)S(1)} collective-permute-done((bf16[16,512]{1,0:T(8,128)(2,1)S(1)}, bf16[16,512]{1,0:T(8,128)(2,1)S(1)}, u32[]{:S(2)}, u32[]{:S(2)}) %collective-permute-start.4) | collective-permute-done | bytes 16416 | tf_op jit(solution)/shard_map/ppermute | solution.py:64
  18.1 0.0 collective-permute-done.5
  18.1 2.5 %collective-permute-start.6 = (bf16[16,512]{1,0:T(8,128)(2,1)S(1)}, bf16[16,512]{1,0:T(8,128)(2,1)S(1)}, u32[]{:S(2)}, u32[]{:S(2)}) collective-permute-start(bf16[16,512]{1,0:T(8,128)(2,1)S(1)} %add_convert_fusion.1), channel_id=1, source_target_pairs={{0,6},{2,4},{4,2},{6,0},{1,7},{3,5},{5,3},{7,1},{8,14},{10,12},{12... | collective-permute-start | bytes 49160 | tf_op jit(solution)/shard_map/ppermute | solution.py:64
  20.6 0.5 %collective-permute-start.7 = (bf16[16,512]{1,0:T(8,128)(2,1)S(1)}, bf16[16,512]{1,0:T(8,128)(2,1)S(1)}, u32[]{:S(2)}, u32[]{:S(2)}) collective-permute-start(bf16[16,512]{1,0:T(8,128)(2,1)S(1)} %add_convert_fusion.1), channel_id=1, source_target_pairs={{0,4},{2,6},{4,0},{6,2},{1,5},{3,7},{5,1},{7,3},{8,12},{10,14},{12... | collective-permute-start | bytes 49160 | tf_op jit(solution)/shard_map/ppermute | solution.py:64
  21.1 0.5 %collective-permute-start.8 = (bf16[16,512]{1,0:T(8,128)(2,1)S(1)}, bf16[16,512]{1,0:T(8,128)(2,1)S(1)}, u32[]{:S(2)}, u32[]{:S(2)}) collective-permute-start(bf16[16,512]{1,0:T(8,128)(2,1)S(1)} %add_convert_fusion.1), channel_id=1, source_target_pairs={{0,2},{2,0},{4,6},{6,4},{1,3},{3,1},{5,7},{7,5},{8,10},{10,8},{12,... | collective-permute-start | bytes 49160 | tf_op jit(solution)/shard_map/ppermute | solution.py:64
  21.6 1.3 %branch.1 = (bf16[2,64,2048]{2,1,0:T(8,128)(2,1)}, bf16[2,64,256]{2,1,0:T(8,128)(2,1)}, bf16[2,64,256]{2,1,0:T(8,128)(2,1)}) custom-call(bf16[2,64,2048]{2,1,0:T(8,128)(2,1)S(1)} %get-tuple-element.27.refs_0_, bf16[2,64,2048]{2,1,0:T(8,128)(2,1)S(1)} %get-tuple-element.28.refs_1_, bf16[2,64,256]{2,1,0:T(8,128)(2,1)S(1)} %get-tuple-element.29.refs_2_, ...), custom_call_target="tpu_custom_call" | custom-call | flops 134217728 | bytes 524288 | tf_op jit(solution)/shard_map/branch/pallas_call | solution.py:295
  22.9 0.0 collective-permute-done.6
  22.9 1.4 %collective-permute-done.7 = bf16[16,512]{1,0:T(8,128)(2,1)S(1)} collective-permute-done((bf16[16,512]{1,0:T(8,128)(2,1)S(1)}, bf16[16,512]{1,0:T(8,128)(2,1)S(1)}, u32[]{:S(2)}, u32[]{:S(2)}) %collective-permute-start.7) | collective-permute-done | bytes 16416 | tf_op jit(solution)/shard_map/ppermute | solution.py:64
  24.3 0.5 %collective-permute-done.8 = bf16[16,512]{1,0:T(8,128)(2,1)S(1)} collective-permute-done((bf16[16,512]{1,0:T(8,128)(2,1)S(1)}, bf16[16,512]{1,0:T(8,128)(2,1)S(1)}, u32[]{:S(2)}, u32[]{:S(2)}) %collective-permute-start.8) | collective-permute-done | bytes 16416 | tf_op jit(solution)/shard_map/ppermute | solution.py:64
  24.8 0.6 %fusion = (bf16[16,256]{1,0:T(8,128)(2,1)}, bf16[16,256]{1,0:T(8,128)(2,1)}) fusion(bf16[16,512]{1,0:T(8,128)(2,1)S(1)} %add_convert_fusion), kind=kLoop, calls=%fused_computation.6 | loop fusion | bytes 32768 | tf_op jit(solution)/shard_map/slice | solution.py:310
  (4 shorter events, 0.0 us)
Async XLA Ops:
  0.6 0.7 %copy-start.2 = (bf16[16,256]{1,0:T(8,128)(2,1)S(1)}, bf16[16,256]{1,0:T(8,128)(2,1)}, u32[]{:S(2)}) copy-start(bf16[16,256]{1,0:T(8,128)(2,1)} %param.12) | copy-start | bytes 24580
  1.4 9.5 %collective-permute-start = (bf16[16,512]{1,0:T(8,128)(2,1)S(1)}, bf16[16,512]{1,0:T(8,128)(2,1)S(1)}, u32[]{:S(2)}, u32[]{:S(2)}) collective-permute-start(bf16[16,512]{1,0:T(8,128)(2,1)S(1)} %constant_dynamic-update-slice_fusion.refs_6_.refs_8_), channel_id=1, source_target_pairs={{0,8},{8,24},{16,0},{24,16},{1,9},{9,25},{17,1},{25,17},{2,10},{10... | collective-permute-start | bytes 49160 | tf_op jit(solution)/shard_map/ppermute | solution.py:64
  4.4 6.5 %collective-permute-start.1 = (bf16[16,512]{1,0:T(8,128)(2,1)S(1)}, bf16[16,512]{1,0:T(8,128)(2,1)S(1)}, u32[]{:S(2)}, u32[]{:S(2)}) collective-permute-start(bf16[16,512]{1,0:T(8,128)(2,1)S(1)} %constant_dynamic-update-slice_fusion.refs_6_.refs_8_), channel_id=1, source_target_pairs={{0,24},{8,16},{16,8},{24,0},{1,25},{9,17},{17,9},{25,1},{2,26},{10... | collective-permute-start | bytes 49160 | tf_op jit(solution)/shard_map/ppermute | solution.py:64
  6.8 4.0 %collective-permute-start.2 = (bf16[16,512]{1,0:T(8,128)(2,1)S(1)}, bf16[16,512]{1,0:T(8,128)(2,1)S(1)}, u32[]{:S(2)}, u32[]{:S(2)}) collective-permute-start(bf16[16,512]{1,0:T(8,128)(2,1)S(1)} %constant_dynamic-update-slice_fusion.refs_6_.refs_8_), channel_id=1, source_target_pairs={{0,16},{8,0},{16,24},{24,8},{1,17},{9,1},{17,25},{25,9},{2,18},{10... | collective-permute-start | bytes 49160 | tf_op jit(solution)/shard_map/ppermute | solution.py:64
  8.4 0.7 %copy-start = (s32[2,64]{1,0:T(2,128)S(1)}, s32[2,64]{1,0:T(2,128)}, u32[]{:S(2)}) copy-start(s32[2,64]{1,0:T(2,128)} %par_ref.1) | copy-start | bytes 1540
  8.4 0.7 %copy-start.1 = (s32[2]{0:T(128)S(1)}, s32[2]{0:T(128)}, u32[]{:S(2)}) copy-start(s32[2]{0:T(128)} %param.15) | copy-start | bytes 28
  11.7 5.6 %collective-permute-start.3 = (bf16[16,512]{1,0:T(8,128)(2,1)S(1)}, bf16[16,512]{1,0:T(8,128)(2,1)S(1)}, u32[]{:S(2)}, u32[]{:S(2)}) collective-permute-start(bf16[16,512]{1,0:T(8,128)(2,1)S(1)} %get-tuple-element.46), channel_id=1, source_target_pairs={{0,24},{8,16},{16,8},{24,0},{1,25},{9,17},{17,9},{25,1},{2,26},{10... | collective-permute-start | bytes 49160 | tf_op jit(solution)/shard_map/ppermute | solution.py:64
  13.3 4.7 %collective-permute-start.4 = (bf16[16,512]{1,0:T(8,128)(2,1)S(1)}, bf16[16,512]{1,0:T(8,128)(2,1)S(1)}, u32[]{:S(2)}, u32[]{:S(2)}) collective-permute-start(bf16[16,512]{1,0:T(8,128)(2,1)S(1)} %get-tuple-element.47), channel_id=1, source_target_pairs={{0,16},{8,24},{16,0},{24,8},{1,17},{9,25},{17,1},{25,9},{2,18},{10... | collective-permute-start | bytes 49160 | tf_op jit(solution)/shard_map/ppermute | solution.py:64
  14.0 4.0 %collective-permute-start.5 = (bf16[16,512]{1,0:T(8,128)(2,1)S(1)}, bf16[16,512]{1,0:T(8,128)(2,1)S(1)}, u32[]{:S(2)}, u32[]{:S(2)}) collective-permute-start(bf16[16,512]{1,0:T(8,128)(2,1)S(1)} %get-tuple-element.48), channel_id=1, source_target_pairs={{0,8},{8,0},{16,24},{24,16},{1,9},{9,1},{17,25},{25,17},{2,10},{10... | collective-permute-start | bytes 49160 | tf_op jit(solution)/shard_map/ppermute | solution.py:64
  18.1 4.8 %collective-permute-start.6 = (bf16[16,512]{1,0:T(8,128)(2,1)S(1)}, bf16[16,512]{1,0:T(8,128)(2,1)S(1)}, u32[]{:S(2)}, u32[]{:S(2)}) collective-permute-start(bf16[16,512]{1,0:T(8,128)(2,1)S(1)} %add_convert_fusion.1), channel_id=1, source_target_pairs={{0,6},{2,4},{4,2},{6,0},{1,7},{3,5},{5,3},{7,1},{8,14},{10,12},{12... | collective-permute-start | bytes 49160 | tf_op jit(solution)/shard_map/ppermute | solution.py:64
  20.6 3.7 %collective-permute-start.7 = (bf16[16,512]{1,0:T(8,128)(2,1)S(1)}, bf16[16,512]{1,0:T(8,128)(2,1)S(1)}, u32[]{:S(2)}, u32[]{:S(2)}) collective-permute-start(bf16[16,512]{1,0:T(8,128)(2,1)S(1)} %add_convert_fusion.1), channel_id=1, source_target_pairs={{0,4},{2,6},{4,0},{6,2},{1,5},{3,7},{5,1},{7,3},{8,12},{10,14},{12... | collective-permute-start | bytes 49160 | tf_op jit(solution)/shard_map/ppermute | solution.py:64
  21.1 3.7 %collective-permute-start.8 = (bf16[16,512]{1,0:T(8,128)(2,1)S(1)}, bf16[16,512]{1,0:T(8,128)(2,1)S(1)}, u32[]{:S(2)}, u32[]{:S(2)}) collective-permute-start(bf16[16,512]{1,0:T(8,128)(2,1)S(1)} %add_convert_fusion.1), channel_id=1, source_target_pairs={{0,2},{2,0},{4,6},{6,4},{1,3},{3,1},{5,7},{7,5},{8,10},{10,8},{12,... | collective-permute-start | bytes 49160 | tf_op jit(solution)/shard_map/ppermute | solution.py:64
